TPU v7x, 32 devices: a whole 2x2x4 slice. The times are simulated.
32 devices in a mesh: lon: 16 (over z, y, x), lat: 2 (over core).
Axes of the slice: x: 2, y: 2, z: 4, core: 2. Of those that a mesh axis runs over, the one named last changes fastest.
Arguments:
- latent_field: bfloat16 [2, 12, 192, 384], P(None, 'lat', 'lon'), may hold values from -6 to 6
- cotangent: bfloat16 [2, 12, 192, 384], P(None, 'lat', 'lon'), may hold values from -6 to 6
- norm_gain: float32 [384], replicated, may hold values from 0.1 to 1.9
- input_weight: bfloat16 [384, 1152], replicated, may hold values from -0.3125 to 0.3125
- output_weight: bfloat16 [384, 384], replicated, may hold values from -0.3125 to 0.3125
- bias_table: bfloat16 [2, 12, 3312], P('lat'), may hold values from -6 to 256
- regions: int32 [2, 12, 192], P(None, 'lat', 'lon'), may hold values from 0 to 3
Outputs:
- grad_field: bfloat16 [2, 12, 192, 384], P(None, 'lat', 'lon')
- grad_input_weight: bfloat16 [384, 1152], P('lon')
- grad_output_weight: bfloat16 [384, 384], P('lon')
- grad_gain: float32 [384], replicated
- grad_table: float32 [2, 12, 3312], P('lat')
Inputs may be any that keep to these rules, and one draw needn't show every extreme that they name: `regions`: two cells of a window attend to each other only where their region ids agree.
All inputs are finite; a program needn't handle non-finite values.
Results may differ from a plain program's by a relative error of at most 0.02.
Values may be sent and summed in bfloat16 or wider, within the bound.
No kernel may reach another device: no remote copies, remote signals or barrier semaphores. Data moves between devices by JAX's collectives and lax.ppermute only.
A program may use at most 128 MiB of HBM per device.

v0:
```python
import math

import jax
import jax.numpy as jnp
from jax import lax
from jax.sharding import PartitionSpec as P

HEADS = 12
LEV = 2
WIN_LAT = 6
WIN_LON = 12


norm_eps = 1e-05
masked_score = -1000000000.0
highest = lax.Precision.HIGHEST


def from_behind(value, axis, steps):
    count = lax.axis_size(axis)
    pairs = [(source, (source + steps) % count) for source in range(count)]
    return lax.ppermute(value, axis, pairs)


def longitude_onehot(span_cells):
    first_index = jnp.arange(span_cells)[:, None, None]
    second_index = jnp.arange(span_cells)[None, :, None]
    offset_index = jnp.arange(2 * span_cells - 1)[None, None, :]
    return (first_index - second_index + span_cells - 1 == offset_index).astype(jnp.float32)


def expand_bias(bias_rows):
    num_bands, num_heads = (bias_rows.shape[0], bias_rows.shape[1])
    shaped = bias_rows.astype(jnp.float32).reshape(
        num_bands, num_heads, LEV, LEV, WIN_LAT, WIN_LAT, 2 * WIN_LON - 1
    )
    spread = jnp.einsum(
        "bhxyuvr,cdr->bhxucyvd", shaped, longitude_onehot(WIN_LON), precision=highest
    )
    window_cells = LEV * WIN_LAT * WIN_LON
    return spread.reshape(num_bands, num_heads, window_cells, window_cells)


def fold_bias(grad_full):
    num_bands, num_heads = (grad_full.shape[0], grad_full.shape[1])
    shaped = grad_full.reshape(num_bands, num_heads, LEV, WIN_LAT, WIN_LON, LEV, WIN_LAT, WIN_LON)
    folded = jnp.einsum(
        "bhxucyvd,cdr->bhxyuvr", shaped, longitude_onehot(WIN_LON), precision=highest
    )
    return folded.reshape(num_bands, num_heads, -1)


def to_windows(cells_grid):
    levels, row_count, col_count = (cells_grid.shape[0], cells_grid.shape[1], cells_grid.shape[2])
    trailing = cells_grid.shape[3:]
    shaped = cells_grid.reshape(
        (levels, row_count // WIN_LAT, WIN_LAT, col_count // WIN_LON, WIN_LON) + trailing
    )
    axes_order = (1, 3, 0, 2, 4) + tuple(range(5, 5 + len(trailing)))
    return jnp.transpose(shaped, axes_order).reshape(
        (row_count // WIN_LAT, col_count // WIN_LON, levels * WIN_LAT * WIN_LON) + trailing
    )


def from_windows(blocks):
    num_bands, num_windows, features = (blocks.shape[0], blocks.shape[1], blocks.shape[3])
    shaped = blocks.reshape(num_bands, num_windows, LEV, WIN_LAT, WIN_LON, features)
    return jnp.transpose(shaped, (2, 0, 3, 1, 4, 5)).reshape(
        LEV, num_bands * WIN_LAT, num_windows * WIN_LON, features
    )


def window_grads(normed_win, grad_win, region_win, bias_rows, input_weight, output_weight):
    num_bands, num_windows, window_cells, features = normed_win.shape
    head_dim = features // HEADS
    score_scale = head_dim ** (-0.5)
    flat_normed = normed_win.reshape(-1, features)
    projected = jnp.dot(flat_normed, input_weight, preferred_element_type=jnp.float32).astype(
        jnp.bfloat16
    )
    projected = projected.reshape(num_bands, num_windows, window_cells, 3, HEADS, head_dim)
    queries, key_rows, values = (
        projected[:, :, :, 0],
        projected[:, :, :, 1],
        projected[:, :, :, 2],
    )
    scores = (
        jnp.einsum("bwihe,bwjhe->bwhij", queries, key_rows, preferred_element_type=jnp.float32)
        * score_scale
    )
    scores = scores + expand_bias(bias_rows)[:, None]
    same_region = region_win[:, :, :, None] == region_win[:, :, None, :]
    scores = jnp.where(same_region[:, :, None], scores, masked_score)
    softmax_out = jax.nn.softmax(scores, axis=-1)
    probs_low = softmax_out.astype(jnp.bfloat16)
    attended = jnp.einsum(
        "bwhij,bwjhe->bwihe", probs_low, values, preferred_element_type=jnp.float32
    ).astype(jnp.bfloat16)
    flat_attended = attended.reshape(-1, features)
    flat_grad = grad_win.reshape(-1, features)
    grad_attended = jnp.dot(flat_grad, output_weight.T, preferred_element_type=jnp.float32).astype(
        jnp.bfloat16
    )
    grad_attended = grad_attended.reshape(num_bands, num_windows, window_cells, HEADS, head_dim)
    grad_probs = jnp.einsum(
        "bwihe,bwjhe->bwhij", grad_attended, values, preferred_element_type=jnp.float32
    )
    grad_values = jnp.einsum(
        "bwhij,bwihe->bwjhe", probs_low, grad_attended, preferred_element_type=jnp.float32
    )
    grad_scores = softmax_out * (
        grad_probs - jnp.sum(softmax_out * grad_probs, axis=-1, keepdims=True)
    )
    grad_table = fold_bias(jnp.sum(grad_scores, axis=1))
    scores_low = (grad_scores * score_scale).astype(jnp.bfloat16)
    grad_queries = jnp.einsum(
        "bwhij,bwjhe->bwihe", scores_low, key_rows, preferred_element_type=jnp.float32
    )
    grad_keys = jnp.einsum(
        "bwhij,bwihe->bwjhe", scores_low, queries, preferred_element_type=jnp.float32
    )
    grad_projected = jnp.stack([grad_queries, grad_keys, grad_values], axis=3).astype(jnp.bfloat16)
    grad_projected = grad_projected.reshape(-1, 3 * features)
    grad_normed = jnp.dot(
        grad_projected, input_weight.T, preferred_element_type=jnp.float32
    ).astype(jnp.bfloat16)
    return (
        grad_normed.reshape(normed_win.shape),
        flat_normed,
        grad_projected,
        flat_attended,
        flat_grad,
        grad_table,
    )


def advance_longitude(stacked):
    half_cols = WIN_LON // 2
    edge_cells = from_behind(stacked[:, :, :, :half_cols], "lon", -1)
    return jnp.concatenate([stacked[:, :, :, half_cols:], edge_cells], axis=3)


def advance_latitude(stacked):
    half_rows = WIN_LAT // 2
    edge_cells = from_behind(stacked[:, :, :half_rows], "lat", -1)
    return jnp.concatenate([stacked[:, :, half_rows:], edge_cells], axis=2)


def retreat_longitude(cells_grid):
    half_cols = WIN_LON // 2
    edge_cells = from_behind(cells_grid[:, :, -half_cols:], "lon", 1)
    return jnp.concatenate([edge_cells, cells_grid[:, :, :-half_cols]], axis=2)


def retreat_latitude(cells_grid):
    half_rows = WIN_LAT // 2
    edge_cells = from_behind(cells_grid[:, -half_rows:], "lat", 1)
    return jnp.concatenate([edge_cells, cells_grid[:, :-half_rows]], axis=1)


def on_device(latent_field, cotangent, norm_gain, input_weight, output_weight, bias_table, regions):
    field_f32 = latent_field.astype(jnp.float32)
    centred = field_f32 - jnp.mean(field_f32, axis=-1, keepdims=True)
    inv_std = lax.rsqrt(jnp.mean(centred * centred, axis=-1, keepdims=True) + norm_eps)
    normalized = centred * inv_std
    normed = (normalized * norm_gain).astype(jnp.bfloat16)
    stacked = jnp.roll(jnp.stack([normed, cotangent]), -(LEV // 2), axis=1)
    stacked = advance_latitude(advance_longitude(stacked))
    features = latent_field.shape[3]

    def one_band(band_item):
        normed_band, grad_band, region_band, table_band = band_item
        return window_grads(
            normed_band[None],
            grad_band[None],
            region_band[None],
            table_band[None],
            input_weight,
            output_weight,
        )

    results = lax.map(
        one_band, (to_windows(stacked[0]), to_windows(stacked[1]), to_windows(regions), bias_table)
    )
    grad_windows, flat_normed, grad_projected, flat_attended, flat_grad, grad_table = results
    grad_windows = grad_windows[:, 0]
    grad_table = grad_table[:, 0]
    flat_normed = flat_normed.reshape(-1, features)
    grad_projected = grad_projected.reshape(-1, 3 * features)
    flat_attended = flat_attended.reshape(-1, features)
    flat_grad = flat_grad.reshape(-1, features)
    grad_shifted = from_windows(grad_windows)
    grad_back = retreat_latitude(retreat_longitude(grad_shifted))
    grad_normed = jnp.roll(grad_back, LEV // 2, axis=0)
    grad_f32 = grad_normed.astype(jnp.float32)
    scaled = grad_f32 * norm_gain
    grad_field = cotangent.astype(jnp.float32) + inv_std * (
        scaled
        - jnp.mean(scaled, axis=-1, keepdims=True)
        - normalized * jnp.mean(scaled * normalized, axis=-1, keepdims=True)
    )
    grad_gain = jnp.sum(grad_f32 * normalized, axis=(0, 1, 2))
    grad_gain, grad_table = lax.psum((grad_gain, grad_table), "lon")
    joined = jnp.concatenate(
        [
            jnp.dot(flat_normed.T, grad_projected, preferred_element_type=jnp.float32),
            jnp.dot(flat_attended.T, flat_grad, preferred_element_type=jnp.float32),
        ],
        axis=1,
    )
    joined, grad_gain = (
        lax.psum(joined.astype(jnp.bfloat16), "lat").astype(jnp.float32),
        lax.psum(grad_gain.astype(jnp.bfloat16), "lat").astype(jnp.float32),
    )
    shares = lax.psum_scatter(joined, "lon", scatter_dimension=0, tiled=True)
    total_cells = (
        latent_field.shape[0]
        * latent_field.shape[1]
        * latent_field.shape[2]
        * lax.axis_size("lon")
        * lax.axis_size("lat")
    )
    factor = 1.0 / math.sqrt(total_cells)
    grad_input_weight = (shares[:, : 3 * features] * factor).astype(jnp.bfloat16)
    grad_output_weight = (shares[:, 3 * features :] * factor).astype(jnp.bfloat16)
    return (
        grad_field.astype(jnp.bfloat16),
        grad_input_weight,
        grad_output_weight,
        grad_gain * factor,
        grad_table,
    )


def solution(mesh):
    in_specs = (
        P(None, "lat", "lon", None),
        P(None, "lat", "lon", None),
        P(),
        P(),
        P(),
        P("lat", None, None),
        P(None, "lat", "lon"),
    )
    out_specs = (
        P(None, "lat", "lon", None),
        P("lon", None),
        P("lon", None),
        P(),
        P("lat", None, None),
    )
    return jax.shard_map(
        on_device, mesh=mesh, in_specs=in_specs, out_specs=out_specs, check_vma=False
    )
```

profile of v0, /device:TPU:0, one launch (start us, length us, event | category | flops | bytes accessed | tf_op | source)
XLA Modules:
  0.0 360.7 jit_solution(10091719786542506025)
XLA Ops:
  7.2 0.0 copy-start
  7.2 0.0 all-reduce.3.cloned.1.call-start
  7.2 1.1 convert_reduce_fusion
  8.3 1.1 fusion.21
  9.4 0.9 copy.71
  10.4 1.0 fusion.29
  11.4 0.1 fusion.24
  11.5 0.1 fusion.52
  11.6 7.0 %collective-permute-start = (bf16[2,2,6,6,384]{4,3,2,1,0:T(8,128)(2,1)S(1)}, bf16[2,2,6,6,384]{4,3,2,1,0:T(8,128)(2,1)S(1)}, u32[]{:S(2)}, u32[]{:S(2)}) collective-permute-start(bf16[2,2,6,6,384]{4,3,2,1,0:T(8,128)(2,1)S(1)} %get-tuple-element.57), channel_id=1, source_target_pairs={{0,30},{2,0},{4,2},{6,4},{8,6},{10,8},{12,10},{14,12},{16,14},{18,... | collective-permute-start | bytes 331784 | tf_op jit(solution)/shard_map/ppermute | solution.py:22
  18.6 0.8 reshape.286
  19.4 0.1 eq.61
  19.5 0.1 broadcast_compare_fusion
  19.6 2.1 collective-permute-done
  21.7 0.1 fusion.27
  21.8 0.1 collective-permute-start.1
  21.8 7.2 %convolution_bitcast_fusion = f32[1,12,2,6,12,2,6,12]{1,7,6,3,5,2,4,0:T(8,128)} fusion(bf16[12,2,2,6,6,23]{5,4,3,2,1,0:T(8,128)(2,1)S(1)} %reshape.286, s32[12,12]{1,0:T(8,128)S(1)} %subtract_add_fusion), kind=kOutput, calls=%fused_computation.2 | convolution fusion | flops 11449584 | bytes 1075392 | tf_op jit(solution)/shard_map/while/body/eval_jaxpr/bhxyuvr,cdr->bhxucyvd/dot_general | solution.py:37
  29.0 21.6 %copy.53 = f32[1,12,2,6,12,2,6,12]{4,3,2,7,6,5,1,0:T(8,128)} copy(f32[1,12,2,6,12,2,6,12]{1,7,6,3,5,2,4,0:T(8,128)} %convolution_bitcast_fusion) | data formatting | bytes 1990656 | tf_op jit(solution)/shard_map/while/body/eval_jaxpr/broadcast_in_dim;while/body/eval_jaxpr/reshape | solution.py:91
  50.6 10.3 %reshape.295 = f32[12,144,144]{1,2,0:T(8,128)} reshape(f32[1,12,2,6,12,2,6,12]{4,3,2,7,6,5,1,0:T(8,128)} %copy.53) | data formatting | bytes 1990656 | tf_op jit(solution)/shard_map/while/body/eval_jaxpr/broadcast_in_dim;while/body/eval_jaxpr/reshape | solution.py:91
  60.9 0.1 fusion.26
  61.0 0.3 convolution_convert_fusion.5
  61.3 0.8 copy.35
  62.1 0.3 convolution_convert_fusion.1
  62.5 0.2 copy.30
  62.7 2.0 add_select_fusion
  64.7 1.6 fusion.55
  66.3 1.7 fusion.25
  67.9 2.1 convolution_bitcast_fusion.2
  70.1 4.4 %convolution_bitcast_fusion.3 = bf16[1,1,144,1,12,32]{2,5,4,3,1,0:T(8,128)(2,1)} fusion(bf16[1,1,144,3,12,32]{2,5,4,3,1,0:T(8,128)(2,1)S(1)} %bitcast.91, f32[12,144,144]{1,2,0:T(8,128)} %fusion.25, f32[12,144,144]{1,2,0:T(8,128)} %get-tuple-element.63, f32[12,144]{1,0:T(8,128)S(1)} %get-tuple-element.62), kind=kOutput, calls=%fused_computation.14 | convolution fusion | flops 17668944 | bytes 7417856 | tf_op jit(solution)/shard_map/while/body/eval_jaxpr/bwhij,bwihe->bwjhe/dot_general | solution.py:119
  74.4 4.4 %convolution_bitcast_fusion.4 = bf16[1,1,144,1,12,32]{2,5,4,3,1,0:T(8,128)(2,1)} fusion(bf16[1,1,144,3,12,32]{2,5,4,3,1,0:T(8,128)(2,1)S(1)} %bitcast.92, f32[12,144,144]{1,2,0:T(8,128)} %fusion.25, f32[12,144,144]{1,2,0:T(8,128)} %get-tuple-element.63, f32[12,144]{1,0:T(8,128)S(1)} %get-tuple-element.62), kind=kOutput, calls=%fused_computation.15 | convolution fusion | flops 17668944 | bytes 7417856 | tf_op jit(solution)/shard_map/while/body/eval_jaxpr/bwhij,bwjhe->bwihe/dot_general | solution.py:116
  78.8 1.2 convolution_convert_fusion.3
  80.0 1.2 convolution_convert_fusion.2
  81.2 1.3 maximum_convert_fusion
  82.5 0.5 convolution_convert_fusion
  83.0 1.1 pad_maximum_fusion
  84.1 0.0 all-reduce.3.cloned.1.call-update
  84.1 0.0 reduce-scatter.2.cloned.1.call-start
  84.2 21.9 %all-reduce.3.cloned.1.call-done = bf16[384,1536]{1,0:T(8,128)(2,1)} async-done(((bf16[384,1536]{1,0:T(8,128)(2,1)}), bf16[384,1536]{1,0:T(8,128)(2,1)}) %all-reduce.3.cloned.1.call-update) | async-done | bytes 1179664 | tf_op jit(solution)/shard_map/psum | solution.py:212
  106.1 3.1 convert_element_type.107
  109.2 0.0 reduce-scatter.2.cloned.1.call-update
  109.2 0.0 all-reduce.5.cloned.1.call-start
  109.3 0.5 convolution_convert_fusion.4
  109.8 2.0 collective-permute-start.2
  111.8 3.6 %subtract_multiply_fusion = f32[12,144,144]{1,2,0:T(8,128)} fusion(f32[12,144,144]{1,2,0:T(8,128)} %fusion.25, f32[12,144,144]{1,2,0:T(8,128)S(1)} %copy-done.2, f32[12,144]{1,0:T(8,128)S(1)} %get-tuple-element.62), kind=kOutput, calls=%fused_computation.6 | output fusion | flops 1246031 | bytes 2992896 | tf_op jit(solution)/shard_map/while/body/eval_jaxpr/sub | solution.py:112
  115.4 10.1 %reshape.296 = f32[12,2,6,12,2,6,12]{3,2,1,6,5,4,0:T(8,128)} reshape(f32[12,144,144]{1,2,0:T(8,128)} %subtract_multiply_fusion) | data formatting | bytes 1990656 | tf_op jit(solution)/shard_map/reshape.74
  125.5 20.8 %copy.42 = f32[12,2,6,12,2,6,12]{6,0,3,5,4,2,1:T(8,128)} copy(f32[12,2,6,12,2,6,12]{3,2,1,6,5,4,0:T(8,128)} %reshape.296) | data formatting | bytes 1990656 | tf_op jit(solution)/shard_map/reshape.74
  146.4 0.1 collective-permute-start.3
  146.5 13.0 %convolution_bitcast_fusion.1 = f32[1,12,2,2,6,6,23]{6,1,5,3,4,2,0:T(8,128)S(1)} fusion(f32[12,2,6,12,2,6,12]{6,0,3,5,4,2,1:T(8,128)} %copy.42, s32[12,12]{1,0:T(8,128)S(1)} %subtract_add_fusion), kind=kOutput, calls=%fused_computation.11 | convolution fusion | flops 68680944 | bytes 1154880 | tf_op jit(solution)/shard_map/while/body/eval_jaxpr/bhxucyvd,cdr->bhxyuvr/dot_general | solution.py:47
  159.5 0.0 copy-start.1
  159.5 0.0 copy-start.7
  159.5 0.3 copy.43
  159.8 0.0 copy-start.4
  159.8 1.4 squeeze.19
  161.3 0.0 all-reduce.5.cloned.1.call-update
  161.4 0.3 fusion.23
  161.7 0.2 fusion.20
  161.9 0.7 copy.44
  162.6 41.4 %psum.29 = bf16[384]{0:T(512)(128)(2,1)S(1)} all-reduce(f32[384]{0:T(512)S(1)} %get-tuple-element.36), channel_id=1, replica_groups=mesh['lon'=16,'lat'=2] {'lon'}, use_global_device_ids=true, to_apply=%region_10.11 | all-reduce | flops 384 | bytes 2304 | tf_op jit(solution)/shard_map/psum | solution.py:203
  204.0 2.4 psum.30
  206.5 0.6 convert_multiply_fusion.2
  207.1 34.4 %reduce-scatter.2.cloned.1.call-done = f32[24,1536]{1,0:T(8,128)} async-done(((f32[384,1536]{1,0:T(8,128)}), f32[24,1536]{1,0:T(8,128)}) %reduce-scatter.2.cloned.1.call-update) | async-done | bytes 147472 | tf_op jit(solution)/shard_map/reduce_scatter | solution.py:215
  241.5 1.5 fusion.31
  243.0 1.4 fusion.47
  244.4 108.2 %all-reduce.5.cloned.1.call-done = f32[1,12,3312]{2,0,1:T(1,128)} async-done(((f32[1,12,3312]{2,0,1:T(1,128)}), f32[1,12,3312]{2,0,1:T(1,128)}) %all-reduce.5.cloned.1.call-update) | async-done | bytes 158992 | tf_op jit(solution)/shard_map/psum | solution.py:203
  352.6 1.6 copy.74
  (30 shorter events, 0.3 us)
Async XLA Ops:
  7.2 55.0 %copy-start = (bf16[384,1152]{1,0:T(8,128)(2,1)S(1)}, bf16[384,1152]{1,0:T(8,128)(2,1)}, u32[]{:S(2)}) copy-start(bf16[384,1152]{1,0:T(8,128)(2,1)} %param.10) | copy-start | bytes 2654212
  7.2 11.4 %copy-start.6 = (bf16[1,12,3312]{2,1,0:T(8,128)(2,1)S(1)}, bf16[1,12,3312]{2,1,0:T(8,128)(2,1)}, u32[]{:S(2)}) copy-start(bf16[1,12,3312]{2,1,0:T(8,128)(2,1)} %param.12) | copy-start | bytes 238468
  7.2 12.2 %copy-start.8 = (s32[2,6,12]{2,0,1:T(2,128)S(1)}, s32[2,6,12]{2,0,1:T(2,128)}, u32[]{:S(2)}) copy-start(s32[2,6,12]{2,0,1:T(2,128)} %param.13) | copy-start | bytes 1732
  7.2 98.9 %all-reduce.3.cloned.1.call-start = ((), (), s32[]{:S(2)}) async-start(), calls=%async_computation.1 | async-start | bytes 2359296 | tf_op jit(solution)/shard_map/psum | solution.py:212
  11.6 10.1 %collective-permute-start = (bf16[2,2,6,6,384]{4,3,2,1,0:T(8,128)(2,1)S(1)}, bf16[2,2,6,6,384]{4,3,2,1,0:T(8,128)(2,1)S(1)}, u32[]{:S(2)}, u32[]{:S(2)}) collective-permute-start(bf16[2,2,6,6,384]{4,3,2,1,0:T(8,128)(2,1)S(1)} %get-tuple-element.57), channel_id=1, source_target_pairs={{0,30},{2,0},{4,2},{6,4},{8,6},{10,8},{12,10},{14,12},{16,14},{18,... | collective-permute-start | bytes 331784 | tf_op jit(solution)/shard_map/ppermute | solution.py:22
  21.8 39.1 %collective-permute-start.1 = (bf16[2,2,3,12,384]{4,3,2,1,0:T(8,128)(2,1)S(1)}, bf16[2,2,3,12,384]{4,3,2,1,0:T(8,128)(2,1)S(1)}, u32[]{:S(2)}, u32[]{:S(2)}) collective-permute-start(bf16[2,2,3,12,384]{4,3,2,1,0:T(8,128)(2,1)S(1)} %get-tuple-element.55), channel_id=1, source_target_pairs={{0,1},{1,0},{2,3},{3,2},{4,5},{5,4},{6,7},{7,6},{8,9},{9,8},{10,11... | collective-permute-start | bytes 331784 | tf_op jit(solution)/shard_map/ppermute | solution.py:22
  50.6 10.4 %copy-start.5 = (bf16[384,384]{1,0:T(8,128)(2,1)S(1)}, bf16[384,384]{1,0:T(8,128)(2,1)}, u32[]{:S(2)}) copy-start(bf16[384,384]{1,0:T(8,128)(2,1)} %param.11) | copy-start | bytes 884740
  64.7 1.6 copy-start.3
  84.1 157.3 %reduce-scatter.2.cloned.1.call-start = ((), (), s32[]{:S(2)}) async-start(), calls=%async_computation.2 | async-start | bytes 2506752 | tf_op jit(solution)/shard_map/reduce_scatter | solution.py:215
  109.2 2.6 copy-start.2
  109.2 243.4 %all-reduce.5.cloned.1.call-start = ((), (), s32[]{:S(2)}) async-start(), calls=%async_computation.3 | async-start | bytes 319488 | tf_op jit(solution)/shard_map/psum | solution.py:203
  109.8 36.6 %collective-permute-start.2 = (bf16[2,6,6,384]{3,2,1,0:T(8,128)(2,1)S(1)}, bf16[2,6,6,384]{3,2,1,0:T(8,128)(2,1)S(1)}, u32[]{:S(2)}, u32[]{:S(2)}) collective-permute-start(bf16[2,6,6,384]{3,2,1,0:T(8,128)(2,1)S(1)} %get-tuple-element.60), channel_id=1, source_target_pairs={{0,2},{2,4},{4,6},{6,8},{8,10},{10,12},{12,14},{14,16},{16,18},{18... | collective-permute-start | bytes 165896 | tf_op jit(solution)/shard_map/ppermute | solution.py:22
  146.4 14.9 %collective-permute-start.3 = (bf16[2,3,12,384]{3,2,1,0:T(8,128)(2,1)S(1)}, bf16[2,3,12,384]{3,2,1,0:T(8,128)(2,1)S(1)}, u32[]{:S(2)}, u32[]{:S(2)}) collective-permute-start(bf16[2,3,12,384]{3,2,1,0:T(8,128)(2,1)S(1)} %fusion.44), channel_id=1, source_target_pairs={{0,1},{1,0},{2,3},{3,2},{4,5},{5,4},{6,7},{7,6},{8,9},{9,8},{10,11... | collective-permute-start | bytes 165896 | tf_op jit(solution)/shard_map/ppermute | solution.py:22
  159.5 1.9 copy-start.1
  159.5 1.9 copy-start.7
  159.8 1.8 copy-start.4
Sparse Core Ops, SparseCore 0:
  84.3 21.7 all-reduce.2
  111.8 129.6 reduce-scatter.1
  247.4 105.1 all-reduce.4
where the time goes:
time: 362 us; the launch traced here: 361 us
  waiting for transfers between devices  167 us (46%)
  local copies, waits for them, and re-layouts  70 us (19%)
  blocking collectives  43.9 us (12%)
  matrix products  38.7 us (11%)
  other arithmetic  18.2 us (5%)
  between operations  14.1 us (4%)
  starting transfers between devices  9.22 us (3%)
    psum x1, waiting for transfers between devices, on_device(): grad_gain, grad_table = lax.psum((grad_gain, grad_table), 'lon')  108 us
    psum x1, blocking collectives, on_device(): grad_gain, grad_table = lax.psum((grad_gain, grad_table), 'lon')  41.4 us
    reduce_scatter x1, waiting for transfers between devices, on_device(): shares = lax.psum_scatter(joined, 'lon', scatter_dimension=0, tiled=True)  34.4 us
    reshape x2, local copies, waits for them, and re-layouts, window_grads(): scores = scores + expand_bias(bias_rows)[:, None]  31.9 us
    another operation x3, local copies, waits for them, and re-layouts  31.8 us
    psum x1, waiting for transfers between devices, on_device(): lax.psum(joined.astype(jnp.bfloat16), 'lat').astype(jnp.float32)  21.9 us
    dot_general x1, matrix products, fold_bias(): jnp.einsum('bhxucyvd,cdr->bhxyuvr', shaped, longitude_onehot(WIN_LON), pr...  13 us
    ppermute x4, starting transfers between devices, from_behind(): return lax.ppermute(value, axis, pairs)  9.1 us
  transfers between devices with their start and end apart: 7, of which 4 were waited for; matrix products, arithmetic and copies ran while one was open for 26% of the time, Pallas kernels for 0%

commit v1 on v0

v1 whole, which is shorter than its diff:
```python
import functools
import math

import jax
import jax.numpy as jnp
from jax import lax
from jax.experimental import pallas as pl
from jax.experimental.pallas import tpu as pltpu
from jax.sharding import PartitionSpec as P

HEADS = 12
LEV = 2
WIN_LAT = 6
WIN_LON = 12
PLANE = LEV * WIN_LAT
CELLS = PLANE * WIN_LON
SPAN = (2 * WIN_LON - 1) * PLANE
WIDE = 384
LANES = 128
QUARTER = LEV * (WIN_LAT // 2) * (WIN_LON // 2)

norm_eps = 1e-05
masked_score = -1000000000.0
f32 = jnp.float32
bf16 = jnp.bfloat16

QUARTERS = ((0, 0), (0, 1), (1, 0), (1, 1))


def segments():
    reach = SPAN // PLANE
    first = 0
    for level_i in range(LEV):
        for level_j in range(LEV):
            for row_i in range(WIN_LAT):
                for row_j in range(WIN_LAT):
                    yield first, level_i * WIN_LAT + row_i, level_j * WIN_LAT + row_j
                    first += reach


def rounded_up(value, step):
    return -(-value // step) * step


class Packet:
    def __init__(self, lon_count, features):
        self.lon_count = lon_count
        self.weight_rows = features // lon_count
        self.weight_used = 6 * self.weight_rows
        self.weight_size = rounded_up(self.weight_used, 16)
        self.table_tiles = -(-PLANE * SPAN // LANES)
        self.table_rows = HEADS * self.table_tiles
        self.table_size = rounded_up(self.table_rows, 4 * 16)
        self.quarter = self.table_size // 4


def nt_dot(left, right):
    return lax.dot_general(left, right, (((1,), (1,)), ((), ())), preferred_element_type=f32)


def nn_dot(left, right):
    return jnp.dot(left, right, preferred_element_type=f32)


def fetch(sources, targets, sems):
    copies = [pltpu.make_async_copy(src, dst, sems.at[at]) for at, (src, dst) in enumerate(zip(sources, targets))]
    for copy in copies:
        copy.start()
    return copies


def load_kernel(field_src, cot_src, *refs):
    out_refs, (field_ref, cot_ref, sems) = refs[:4], refs[4:]
    for copy in fetch((field_src, cot_src), (field_ref, cot_ref), sems):
        copy.wait()
    half_rows, half_cols = WIN_LAT // 2, WIN_LON // 2
    for (lat_half, lon_half), out_ref in zip(QUARTERS, out_refs):
        first_row, first_col = (1 - lat_half) * half_rows, (1 - lon_half) * half_cols
        pieces = []
        for ref in (field_ref, cot_ref):
            for row in range(half_rows):
                for col in range(half_cols):
                    pieces.append(ref[first_row + row, first_col + col].astype(f32))
        out_ref[...] = jnp.concatenate(pieces, axis=0).astype(bf16)


def one_hot(flags):
    return flags.astype(f32).astype(bf16)


def counted(shape, axis):
    return lax.broadcasted_iota(jnp.int32, shape, axis)


def cell_source(cell, stride):
    col, level, row = lax.div(cell, PLANE), lax.rem(lax.div(cell, WIN_LAT), LEV), lax.rem(cell, WIN_LAT)
    half_rows, half_cols = WIN_LAT // 2, WIN_LON // 2
    quarter = 2 * lax.div(row, half_rows) + lax.div(col, half_cols)
    place = lax.rem(row, half_rows) * half_cols + lax.rem(col, half_cols)
    return quarter * stride + place * LEV + lax.rem(level + LEV // 2, LEV)


def unpack_kernel(own_ref, lon_ref, lat_ref, diag_ref, out_ref):
    half_rows, half_cols = WIN_LAT // 2, WIN_LON // 2
    sources = ((own_ref, 0), (lon_ref, 0), (lat_ref, 0), (diag_ref, QUARTER))
    for (lat_half, lon_half), (ref, start) in zip(QUARTERS, sources):
        first_row, first_col = (1 - lat_half) * half_rows, (1 - lon_half) * half_cols
        cells = ref[...].astype(f32)[start : start + QUARTER]
        for row in range(half_rows):
            for col in range(half_cols):
                first = (row * half_cols + col) * LEV
                out_ref[first_row + row, first_col + col] = cells[first : first + LEV].astype(bf16)


def bias_kernel(
    table_src,
    regions_src,
    win_src,
    wout_src,
    gain_src,
    out_ref,
    win_t_ref,
    lanes_ref,
    rows_ref,
    eye_ref,
    place_ref,
    place_t_ref,
    win_ref,
    wout_ref,
    gain_ref,
    stage,
    full,
    table_ref,
    regions_ref,
    sems,
):
    sources = (table_src, regions_src, win_src, wout_src, gain_src)
    copies = fetch(sources, (table_ref, regions_ref, win_ref, wout_ref, gain_ref), sems)
    features = win_ref.shape[0]
    square = (features, features)
    eye = one_hot(counted(square, 0) == counted(square, 1))
    eye_ref[...] = eye
    source, lane = cell_source(counted((CELLS, 1), 0), 2 * QUARTER), counted((CELLS, 2 * CELLS), 1)
    place_ref[:CELLS] = one_hot(source == lane)
    place_ref[CELLS:] = one_hot(source + QUARTER == lane)
    place_t_ref[...] = one_hot(cell_source(counted((1, CELLS), 1), QUARTER) == counted((CELLS, CELLS), 0))
    lane = counted((1, WIDE), 1)
    target = jnp.where(lane < SPAN, lax.rem(lane, PLANE) * (SPAN // PLANE) + lax.div(lane, PLANE), -1)
    lanes_ref[...] = one_hot(target == counted((WIDE, WIDE), 0))
    sixteens = HEADS * 16
    row = counted((sixteens, 1), 0)
    target = jnp.where(lax.rem(row, 16) < PLANE, lax.rem(row, 16) * 16 + lax.div(row, 16), -1)
    rows_ref[...] = one_hot(target == counted((sixteens, sixteens), 1))

    stage[...] = jnp.zeros(stage.shape, f32)
    reach = SPAN // PLANE
    for copy in copies:
        copy.wait()
    for block in range(3):
        cols = slice(block * features, (block + 1) * features)
        win_t_ref[cols] = nt_dot(eye, win_ref[:, cols]).astype(bf16)
    table = table_ref[...].astype(f32)
    for first, plane_i, plane_j in segments():
        stage[16 * plane_j : 16 * plane_j + HEADS, reach * plane_i : reach * (plane_i + 1)] = table[
            :, first : first + reach
        ]
    moved = nn_dot(stage[...].astype(bf16), lanes_ref[...]).astype(bf16)
    rows = nn_dot(rows_ref[...], moved)

    region_rows = [regions_ref[row, level : level + 1, :] for level in range(LEV) for row in range(WIN_LAT)]
    region_grid = jnp.concatenate(region_rows, axis=0).astype(f32).astype(bf16)
    cell, lane = counted((CELLS, PLANE), 0), counted((CELLS, PLANE), 1)
    by_plane = nn_dot(one_hot(lax.rem(cell, PLANE) == lane), region_grid)
    region_col = jnp.sum(jnp.where(lax.div(cell, PLANE) == lane, by_plane, 0.0), axis=1, keepdims=True)
    across = counted((CELLS, CELLS), 0) == counted((CELLS, CELLS), 1)
    region_row = jnp.sum(jnp.where(across, region_col, 0.0), axis=0, keepdims=True)
    same = region_col == region_row

    for col in range(WIN_LON):
        shift = PLANE * (WIN_LON - 1 - col)
        moved = rows if shift == 0 else pltpu.roll(rows, WIDE - shift, 1)
        for head in range(HEADS):
            full[head, PLANE * col : PLANE * (col + 1), :] = moved[16 * head : 16 * head + PLANE, :CELLS]
    for head in range(HEADS):
        out_ref[head] = jnp.where(same, full[head], masked_score).astype(bf16)


def window_kernel(
    packet,
    place_id,
    own_ref,
    lon_ref,
    lat_ref,
    diag_ref,
    gain_ref,
    win_ref,
    win_t_ref,
    wout_ref,
    bias_ref,
    place_ref,
    eye_ref,
    keep_ref,
    send_ref,
    scores_ref,
    right,
    normalized_ref,
    inv_std_ref,
    cot_ref,
    left,
):
    features = win_ref.shape[0]
    head_dim = features // HEADS
    group_heads = LANES // head_dim
    score_scale = head_dim ** (-0.5)
    quarters = (own_ref, lon_ref, lat_ref, diag_ref)
    eye = eye_ref[...]
    stacked = jnp.concatenate([ref[...].astype(f32) for ref in quarters], axis=0).astype(bf16)
    placed = nn_dot(place_ref[...], stacked)
    field = placed[:CELLS]
    cot = placed[CELLS:].astype(bf16)
    cot_ref[...] = cot
    gain = gain_ref[...].reshape(1, features)

    centred = field - jnp.mean(field, axis=-1, keepdims=True)
    inv_std = lax.rsqrt(jnp.mean(centred * centred, axis=-1, keepdims=True) + norm_eps)
    normalized = centred * inv_std
    normalized_ref[...] = normalized
    inv_std_ref[...] = inv_std
    normed = (normalized * gain).astype(bf16)

    projected_t = nt_dot(win_t_ref[...], normed).astype(bf16)
    keys_values = nn_dot(normed, win_ref[:, features:]).astype(bf16)
    grad_att_t = nt_dot(wout_ref[...], cot).astype(bf16)
    left[0] = nt_dot(eye, normed).astype(bf16)
    right[3] = nt_dot(eye, cot).astype(bf16)

    def spread(head_rows, slot):
        parts = []
        if slot:
            parts.append(jnp.zeros((slot * head_dim, CELLS), bf16))
        parts.append(head_rows)
        if slot < group_heads - 1:
            parts.append(jnp.zeros(((group_heads - 1 - slot) * head_dim, CELLS), bf16))
        return jnp.concatenate(parts, axis=0)

    def rows_of(head):
        return slice(head * head_dim, (head + 1) * head_dim)

    def part(head, index):
        return projected_t[index * features + head * head_dim : index * features + (head + 1) * head_dim]

    def scores_of(head):
        group, slot = divmod(head, group_heads)
        keys = keys_values[:, group * LANES : (group + 1) * LANES]
        values = keys_values[:, features + group * LANES : features + (group + 1) * LANES]
        scores = nn_dot(keys, spread(part(head, 0), slot))
        return scores, nn_dot(values, spread(grad_att_t[rows_of(head)], slot))

    def softmax_of(head, scores, grad_probs):
        scores = scores * score_scale + bias_ref[head].astype(f32)
        grown = jnp.exp(scores - jnp.max(scores, axis=0, keepdims=True))
        probs = grown * (1.0 / jnp.sum(grown, axis=0, keepdims=True))
        weighted = probs * grad_probs
        grad_scores = weighted - probs * jnp.sum(weighted, axis=0, keepdims=True)
        return probs.astype(bf16), (grad_scores * score_scale).astype(bf16)

    def products_of(head, probs_low, scores_low):
        rows = rows_of(head)
        scores_ref[head] = scores_low
        left[1, rows] = nn_dot(part(head, 2), probs_low).astype(bf16)
        right[0, rows] = nn_dot(part(head, 1), scores_low).astype(bf16)
        right[1, rows] = nt_dot(part(head, 0), scores_low).astype(bf16)
        right[2, rows] = nt_dot(grad_att_t[rows], probs_low).astype(bf16)

    raw, soft = {}, {}
    for turn in range(HEADS + 2):
        if turn < HEADS:
            raw[turn] = scores_of(turn)
        if turn >= 2:
            products_of(turn - 2, *soft.pop(turn - 2))
        if 1 <= turn <= HEADS:
            soft[turn - 1] = softmax_of(turn - 1, *raw.pop(turn - 1))

    odd = lax.rem(place_id[1], 2)

    for out_ref, half in ((send_ref, 1 - odd), (keep_ref, odd)):
        low = nt_dot(left[0], right[2 * half])
        high = nt_dot(left[half], right[2 * half + 1])
        for owner in range(packet.lon_count):
            rows = slice(owner * packet.weight_rows, (owner + 1) * packet.weight_rows)
            pieces = [
                block[rows, tile * LANES : (tile + 1) * LANES] for block in (low, high) for tile in range(3)
            ]
            if packet.weight_size > packet.weight_used:
                pieces.append(jnp.zeros((packet.weight_size - packet.weight_used, LANES), f32))
            first = owner * packet.weight_size
            out_ref[first : first + packet.weight_size] = jnp.concatenate(pieces, axis=0).astype(bf16)


def field_kernel(
    win_ref,
    grad_projected_ref,
    normalized_ref,
    inv_std_ref,
    cot_ref,
    gain_ref,
    place_t_ref,
    eye_ref,
    back_own_ref,
    back_lon_ref,
    back_lat_ref,
    gain_out_ref,
):
    features = win_ref.shape[0]
    grad_shifted_t = sum(
        nn_dot(win_ref[:, block * features : (block + 1) * features], grad_projected_ref[block]) for block in range(3)
    ).astype(bf16)
    grad_normed = nt_dot(eye_ref[:CELLS, :CELLS], grad_shifted_t)
    normalized = normalized_ref[...]
    scaled = grad_normed * gain_ref[...].reshape(1, features)
    grad_field = cot_ref[...].astype(f32) + inv_std_ref[...] * (
        scaled
        - jnp.mean(scaled, axis=-1, keepdims=True)
        - normalized * jnp.mean(scaled * normalized, axis=-1, keepdims=True)
    )
    back = nn_dot(place_t_ref[...], grad_field.astype(bf16))
    quarters = [back[quarter * QUARTER : (quarter + 1) * QUARTER] for quarter in range(4)]
    back_own_ref[...] = quarters[0].astype(bf16)
    back_lon_ref[...] = jnp.concatenate([quarters[1], quarters[3]], axis=0).astype(bf16)
    back_lat_ref[...] = quarters[2].astype(bf16)
    gain_sum = jnp.sum(grad_normed * normalized, axis=0, keepdims=True)
    gain_rows = [gain_sum[:, tile * LANES : (tile + 1) * LANES] for tile in range(3)]
    gain_out_ref[...] = jnp.concatenate(gain_rows + [jnp.zeros((13, LANES), f32)], axis=0).astype(bf16)


def fold_kernel(packet, scores_ref, lanes_ref, rows_ref, out_ref, wide, table, flat):
    wide[...] = jnp.zeros(wide.shape, f32)
    table[...] = jnp.zeros(table.shape, f32)
    flat[...] = jnp.zeros(flat.shape, f32)
    for head in range(HEADS):
        wide[head % 2, :, :CELLS] = scores_ref[head].astype(f32)
        total = wide[head % 2, :PLANE, :]
        for col in range(1, WIN_LON):
            total = pltpu.roll(total, PLANE, 1) + wide[head % 2, PLANE * col : PLANE * (col + 1), :]
        table[16 * head : 16 * head + PLANE, :] = total
    moved = nn_dot(rows_ref[...], table[...].astype(bf16)).astype(bf16)
    moved = nt_dot(moved, lanes_ref[...])
    reach = SPAN // PLANE
    for first, plane_i, plane_j in segments():
        flat[:HEADS, first : first + reach] = moved[
            16 * plane_j : 16 * plane_j + HEADS, reach * plane_i : reach * (plane_i + 1)
        ]
    tiles = [flat[:HEADS, tile * LANES : (tile + 1) * LANES] for tile in range(packet.table_tiles)]
    tiles.append(jnp.zeros((packet.table_size - packet.table_rows, LANES), f32))
    out_ref[...] = jnp.concatenate(tiles, axis=0).astype(bf16)


def first_exchange_kernel(packet, place_id, keep_ref, recv_ref, table_ref, *out_refs):
    low = lax.rem(place_id[0], 4)
    size, quarter = packet.weight_size, packet.quarter
    for step, out_ref in enumerate(out_refs):
        digit = lax.bitwise_xor(low, step)
        for upper in range(packet.lon_count // 4):
            rows = pl.ds(pl.multiple_of((upper * 4 + digit) * size, 16), size)
            out_ref[upper * size : (upper + 1) * size] = keep_ref[rows] + recv_ref[rows]
        first = packet.lon_count // 4 * size
        out_ref[first:] = table_ref[pl.ds(pl.multiple_of(digit * quarter, 16), quarter)]


def summed(refs, rows):
    terms = [ref[rows] for ref in refs]
    while len(terms) > 1:
        terms = [left + right for left, right in zip(terms[::2], terms[1::2])]
    return terms[0]


def next_exchange_kernel(packet, shift, gains, place_id, *refs):
    gain_refs, held, out_refs = refs[:gains], refs[gains:-4], refs[-4:]
    size, quarter = packet.weight_size, packet.quarter
    digit = lax.rem(lax.shift_right_logical(place_id[0], shift), 4)
    groups = (out_refs[0].shape[0] - quarter - 16) // size
    rest = 4 * groups * size
    table = summed(held, slice(rest, rest + quarter))
    gain = summed(gain_refs, slice(0, 16)) if gains else summed(held, slice(rest + quarter, rest + quarter + 16))
    for step, out_ref in enumerate(out_refs):
        for upper in range(groups):
            owner = upper * 4 + lax.bitwise_xor(digit, step)
            out_ref[upper * size : (upper + 1) * size] = summed(held, pl.ds(pl.multiple_of(owner * size, 16), size))
        out_ref[groups * size : groups * size + quarter] = table
        out_ref[groups * size + quarter :] = gain


def last_sum_kernel(packet, a_ref, b_ref, c_ref, d_ref, weight_ref, table_ref):
    refs = (a_ref, b_ref, c_ref, d_ref)
    weight_ref[...] = summed(refs, slice(0, packet.weight_size))
    table_ref[...] = summed(refs, slice(packet.weight_size, packet.weight_size + packet.quarter + 16))


def finish_kernel(
    packet,
    table_scale,
    factor,
    place_id,
    weights_ref,
    other_weights_ref,
    a_ref,
    b_ref,
    c_ref,
    d_ref,
    grad_in_ref,
    grad_out_ref,
    grad_table_ref,
    grad_gain_ref,
    quarters,
):
    odd = lax.rem(place_id[1], 2) == 1
    own, other = weights_ref[...].astype(f32) * factor, other_weights_ref[...].astype(f32) * factor
    halves = (jnp.where(odd, other, own), jnp.where(odd, own, other))
    size = packet.weight_rows
    tiles = [half[tile * size : (tile + 1) * size] for half in halves for tile in range(6)]
    grad_in_ref[...] = jnp.concatenate(tiles[:9], axis=1).astype(bf16)
    grad_out_ref[...] = jnp.concatenate(tiles[9:], axis=1).astype(bf16)

    low = lax.rem(place_id[0], 4)
    parts = (a_ref, b_ref, c_ref, d_ref)
    for step, ref in enumerate(parts):
        quarters[lax.bitwise_xor(low, step)] = ref[: packet.quarter].astype(f32)
    total = quarters[...].reshape(packet.table_size, LANES)
    for tile in range(packet.table_tiles):
        first = tile * LANES
        width = min(LANES, grad_table_ref.shape[2] - first)
        block = total[HEADS * tile : HEADS * (tile + 1), :width] * table_scale
        for head in range(HEADS):
            grad_table_ref[head, :, first : first + width] = block[head : head + 1]
    gain = sum(ref[packet.quarter :].astype(f32) for ref in parts) * factor
    grad_gain_ref[...] = jnp.concatenate([gain[tile : tile + 1] for tile in range(3)], axis=1).reshape(
        grad_gain_ref.shape
    )


def whole(count):
    return [pl.BlockSpec(memory_space=pltpu.VMEM)] * count


scalars = pl.BlockSpec(memory_space=pltpu.SMEM)


def call(kernel, name, in_specs, outs, scratch=(), flops=0, moved=0):
    return pl.pallas_call(
        kernel,
        name=name,
        out_shape=outs,
        in_specs=in_specs,
        out_specs=jax.tree.map(lambda _: pl.BlockSpec(memory_space=pltpu.VMEM), outs),
        scratch_shapes=list(scratch),
        compiler_params=pltpu.CompilerParams(vmem_limit_bytes=20 * 1024 * 1024),
        cost_estimate=pl.CostEstimate(flops=flops, bytes_accessed=moved, transcendentals=0),
    )


def on_device(lon_count, lat_count, latent_field, cotangent, norm_gain, input_weight, output_weight, bias_table, regions):
    features = latent_field.shape[3]
    head_dim = features // HEADS
    packet = Packet(lon_count, features)
    place_id = jnp.stack([lax.axis_index("lon"), lax.axis_index("lat")]).astype(jnp.int32)

    def move(value, lon_step, lat_step):
        pairs = []
        for lon in range(lon_count):
            for lat in range(lat_count):
                target = ((lon + lon_step) % lon_count) * lat_count + (lat + lat_step) % lat_count
                pairs.append((lon * lat_count + lat, target))
        return lax.ppermute(value, ("lon", "lat"), pairs)

    def swap(value, axis, mask):
        count = lon_count if axis == "lon" else lat_count
        return lax.ppermute(value, axis, [(source, source ^ mask) for source in range(count)])

    struct = jax.ShapeDtypeStruct
    def in_hbm(*arrays):
        return [pltpu.with_memory_space_constraint(array, pltpu.HBM) for array in arrays]

    def space_for(array):
        return pltpu.VMEM(array.shape, array.dtype)

    hbm = pl.BlockSpec(memory_space=pltpu.HBM)
    field, cot = jnp.transpose(latent_field, (1, 2, 0, 3)), jnp.transpose(cotangent, (1, 2, 0, 3))
    own, to_lon, to_lat, to_diag = call(
        load_kernel,
        "load",
        [hbm] * 2,
        [struct((2 * QUARTER, features), bf16)] * 4,
        [space_for(field), space_for(cot), pltpu.SemaphoreType.DMA((2,))],
        moved=1 << 20,
    )(*in_hbm(field, cot))
    from_lon = move(to_lon, -1, 0)
    from_diag = move(to_diag, -1, -1)
    from_lat = move(to_lat, 0, -1)

    table, region_grid = bias_table[0], jnp.transpose(regions, (1, 0, 2))
    bias_full, input_weight_t, lane_moves, row_moves, eye, place, place_t, weight_in, weight_out, gain = call(
        bias_kernel,
        "expand_bias",
        [hbm] * 5,
        [
            struct((HEADS, CELLS, CELLS), bf16),
            struct((3 * features, features), bf16),
            struct((WIDE, WIDE), bf16),
            struct((HEADS * 16, HEADS * 16), bf16),
            struct((features, features), bf16),
            struct((2 * CELLS, 2 * CELLS), bf16),
            struct((CELLS, CELLS), bf16),
            struct(input_weight.shape, bf16),
            struct(output_weight.shape, bf16),
            struct(norm_gain.shape, f32),
        ],
        [
            pltpu.VMEM((HEADS * 16, WIDE), f32),
            pltpu.VMEM((HEADS, CELLS, CELLS), f32),
            space_for(table),
            space_for(region_grid),
            pltpu.SemaphoreType.DMA((5,)),
        ],
        moved=1 << 21,
    )(*in_hbm(table, region_grid, input_weight, output_weight, norm_gain))

    half_sum = struct((lon_count * packet.weight_size, LANES), bf16)
    results = call(
        functools.partial(window_kernel, packet),
        "window",
        [scalars] + whole(11),
        [
            half_sum,
            half_sum,
            struct((HEADS, CELLS, CELLS), bf16),
            struct((4, features, CELLS), bf16),
            struct((CELLS, features), f32),
            struct((CELLS, 1), f32),
            struct((CELLS, features), bf16),
        ],
        [pltpu.VMEM((2, features, CELLS), bf16)],
        flops=10**9,
        moved=5 << 20,
    )(
        place_id,
        own,
        from_lon,
        from_lat,
        from_diag,
        gain,
        weight_in,
        input_weight_t,
        weight_out,
        bias_full,
        place,
        eye,
    )
    keep, send, scores_low, *saved = results

    received = swap(send, "lat", 1)
    table_part = call(
        functools.partial(fold_kernel, packet),
        "fold_table",
        whole(3),
        struct((packet.table_size, LANES), bf16),
        [
            pltpu.VMEM((2, CELLS, WIDE), f32),
            pltpu.VMEM((HEADS * 16, WIDE), f32),
            pltpu.VMEM((16, packet.table_tiles * LANES), f32),
        ],
        moved=1 << 21,
    )(scores_low, lane_moves, row_moves)

    groups = lon_count // 4
    parts = call(
        functools.partial(first_exchange_kernel, packet),
        "add_lat",
        [scalars] + whole(3),
        [struct((groups * packet.weight_size + packet.quarter, LANES), bf16)] * 4,
        moved=2 << 20,
    )(place_id, keep, received, table_part)
    parts, saved = lax.optimization_barrier((parts, saved))

    def trade(parts, shift):
        return [swap(parts[step], "lon", step << shift) for step in (3, 2, 1)] + [parts[0]]

    held = trade(parts, 0)
    piece = struct((QUARTER, features), bf16)
    back_own, back_lon, back_lat, gain_part = call(
        field_kernel,
        "grad_field",
        whole(8),
        [piece, struct((2 * QUARTER, features), bf16), piece, struct((16, LANES), bf16)],
        flops=10**8,
        moved=5 << 20,
    )(weight_in, *saved, gain, place_t, eye)
    home_lat = move(back_lat, 0, 1)
    gain_other = swap(gain_part, "lat", 1)
    held, home_lat, gain_other = lax.optimization_barrier((held, home_lat, gain_other))
    gains = [gain_part, gain_other]
    home_lon = move(back_lon, 1, 0)
    home_diag = move(home_lon, 0, 1)
    for shift in range(2, lon_count.bit_length() - 1, 2):
        groups //= 4
        parts = call(
            functools.partial(next_exchange_kernel, packet, shift, len(gains)),
            "add_lon",
            [scalars] + whole(len(gains) + 4),
            [struct((groups * packet.weight_size + packet.quarter + 16, LANES), bf16)] * 4,
            moved=1 << 20,
        )(place_id, *gains, *held)
        gains = []
        held = trade(parts, shift)
    weight_sum, table_sum = call(
        functools.partial(last_sum_kernel, packet),
        "add_last",
        whole(4),
        [struct((packet.weight_size, LANES), bf16), struct((packet.quarter + 16, LANES), bf16)],
        moved=1 << 18,
    )(*held)
    table_parts = trade([table_sum] * 4, 0)[::-1]
    for bit in range(1, lat_count.bit_length() - 1):
        weight_sum = weight_sum + swap(weight_sum, "lat", 1 << bit)
    weight_other = swap(weight_sum, "lat", 1)

    cells_in_all = latent_field.shape[0] * latent_field.shape[1] * latent_field.shape[2]
    factor = 1.0 / math.sqrt(cells_in_all * lon_count * lat_count)
    grad_input_weight, grad_output_weight, grad_table, gain_sum = call(
        functools.partial(finish_kernel, packet, math.sqrt(head_dim), factor),
        "finish",
        [scalars] + whole(6),
        [
            struct((packet.weight_rows, 3 * features), bf16),
            struct((packet.weight_rows, features), bf16),
            struct((HEADS, 1, PLANE * SPAN), f32),
            struct((features,), f32),
        ],
        [pltpu.VMEM((4, packet.quarter, LANES), f32)],
        moved=1 << 19,
    )(place_id, weight_sum, weight_other, *table_parts)
    for bit in range(1, lat_count.bit_length() - 1):
        gain_sum = gain_sum + swap(gain_sum, "lat", 1 << bit)

    grad_field = call(
        unpack_kernel, "unpack_quarters", whole(4), struct((WIN_LAT, WIN_LON, LEV, features), bf16), moved=4 << 20
    )(back_own, home_lon, home_lat, home_diag)
    return (
        jnp.transpose(grad_field, (2, 0, 1, 3)),
        grad_input_weight,
        grad_output_weight,
        gain_sum,
        jnp.transpose(grad_table, (1, 0, 2)),
    )


def solution(mesh):
    in_specs = (
        P(None, "lat", "lon", None),
        P(None, "lat", "lon", None),
        P(),
        P(),
        P(),
        P("lat", None, None),
        P(None, "lat", "lon"),
    )
    out_specs = (
        P(None, "lat", "lon", None),
        P("lon", None),
        P("lon", None),
        P(),
        P("lat", None, None),
    )
    return jax.shard_map(
        functools.partial(on_device, mesh.shape["lon"], mesh.shape["lat"]),
        mesh=mesh,
        in_specs=in_specs,
        out_specs=out_specs,
        check_vma=False,
    )
```

time: 362 us -> 48 us (0.13)
  waiting for transfers between devices: 167 us -> 10.8 us
  local copies, waits for them, and re-layouts: 70 us -> 0 us
  blocking collectives: 43.9 us -> 0 us
  matrix products: 38.7 us -> 0 us
  other arithmetic: 18.2 us -> 0.07 us
  Pallas kernels: 0 us -> 14.8 us
  between operations: 14.1 us -> 0.74 us
  starting transfers between devices: 9.22 us -> 21.4 us
    psum x2 -> x0, waiting for transfers between devices: 130 us -> none  [the longest x1 108 us: on_device(): grad_gain, grad_table = lax.psum((grad_gain, grad_table), 'lon')]
    psum x2 -> x0, blocking collectives: 43.9 us -> none  [the longest x1 41.4 us: on_device(): grad_gain, grad_table = lax.psum((grad_gain, grad_table), 'lon')]
    dot_general x13 -> x0, matrix products: 38.7 us -> none  [the longest x1 13 us: fold_bias(): jnp.einsum('bhxucyvd,cdr->bhxyuvr', shaped, longitude_onehot(WIN_LON), pr...]
    reduce_scatter x1 -> x0, waiting for transfers between devices: 34.4 us -> none  [on_device(): shares = lax.psum_scatter(joined, 'lon', scatter_dimension=0, tiled=True)]
    reshape x2 -> x0, local copies, waits for them, and re-layouts: 31.9 us -> none  [window_grads(): scores = scores + expand_bias(bias_rows)[:, None]]
    another operation x4 -> x0, local copies, waits for them, and re-layouts: 31.8 us -> none
    pallas_call x0 -> x10, Pallas kernels: none -> 14.8 us  [the longest x1 3.89 us: on_device(): call(functools.partial(window_kernel, packet), 'window', [scalars] + whol...]
    ppermute x4 -> x18, starting transfers between devices: 9.1 us -> 21.4 us  [the longest x12 12.2 us: swap(): lax.ppermute(value, axis, [(source, source ^ mask) for source in range(co...]
  transfers between devices with their start and end apart: 7 -> 18, of which waited for: 4 -> 10; matrix products, arithmetic and copies ran while one was open for 26% -> 0% of each run, Pallas kernels for 0% -> 16%
where the time goes in v1:
time: 48 us; the launch traced here: 47.8 us
  starting transfers between devices  21.4 us (45%)
  Pallas kernels  14.8 us (31%)
  waiting for transfers between devices  10.8 us (22%)
  between operations  0.74 us (2%)
    ppermute x12, starting transfers between devices, swap(): lax.ppermute(value, axis, [(source, source ^ mask) for source in range(co...  12.2 us
    ppermute x12, waiting for transfers between devices, swap(): lax.ppermute(value, axis, [(source, source ^ mask) for source in range(co...  10.8 us
    ppermute x6, starting transfers between devices, move(): return lax.ppermute(value, ('lon', 'lat'), pairs)  9.19 us
    pallas_call x1, Pallas kernels, on_device(): call(functools.partial(window_kernel, packet), 'window', [scalars] + whol...  3.89 us
    pallas_call x1, Pallas kernels, on_device(): call(bias_kernel, 'expand_bias', [hbm] * 5, [struct((HEADS, CELLS, CELLS)...  3.5 us
    pallas_call x1, Pallas kernels, on_device(): call(functools.partial(fold_kernel, packet), 'fold_table', whole(3), stru...  1.9 us
    pallas_call x1, Pallas kernels, on_device(): call(functools.partial(finish_kernel, packet, math.sqrt(head_dim), factor...  1.33 us
    pallas_call x1, Pallas kernels, on_device(): call(load_kernel, 'load', [hbm] * 2, [struct((2 * QUARTER, features), bf1...  1.13 us
  transfers between devices with their start and end apart: 18, of which 10 were waited for; matrix products, arithmetic and copies ran while one was open for 0% of the time, Pallas kernels for 16%

profile of v1, /device:TPU:0, one launch (start us, length us, event | category | flops | bytes accessed | tf_op | source)
XLA Modules:
  0.0 47.8 jit_solution(7792889821091018019)
XLA Ops:
  0.6 1.1 %load.1 = (bf16[72,384]{1,0:T(8,128)(2,1)S(1)}, bf16[72,384]{1,0:T(8,128)(2,1)S(1)}, bf16[72,384]{1,0:T(8,128)(2,1)S(1)}, bf16[72,384]{1,0:T(8,128)(2,1)S(1)}) custom-call(bf16[6,12,2,384]{3,2,1,0:T(2,128)(2,1)} %bitcast.8, bf16[6,12,2,384]{3,2,1,0:T(2,128)(2,1)} %bitcast.9), custom_call_target="tpu_custom_call" | custom-call | bytes 1048576 | tf_op jit(solution)/shard_map/load/pallas_call | solution.py:488
  1.8 7.0 %collective-permute-start = (bf16[72,384]{1,0:T(8,128)(2,1)S(1)}, bf16[72,384]{1,0:T(8,128)(2,1)S(1)}, u32[]{:S(2)}, u32[]{:S(2)}) collective-permute-start(bf16[72,384]{1,0:T(8,128)(2,1)S(1)} %get-tuple-element.60), channel_id=1, source_target_pairs={{0,30},{1,31},{2,0},{3,1},{4,2},{5,3},{6,4},{7,5},{8,6},{9,7},{10,... | collective-permute-start | bytes 165896 | tf_op jit(solution)/shard_map/ppermute | solution.py:473
  8.8 0.0 collective-permute-start.1
  8.8 0.6 %collective-permute-start.2 = (bf16[72,384]{1,0:T(8,128)(2,1)S(1)}, bf16[72,384]{1,0:T(8,128)(2,1)S(1)}, u32[]{:S(2)}, u32[]{:S(2)}) collective-permute-start(bf16[72,384]{1,0:T(8,128)(2,1)S(1)} %get-tuple-element.62), channel_id=1, source_target_pairs={{0,31},{1,30},{2,1},{3,0},{4,3},{5,2},{6,5},{7,4},{8,7},{9,6},{10,... | collective-permute-start | bytes 165896 | tf_op jit(solution)/shard_map/ppermute | solution.py:473
  9.4 0.1 pad_add_fusion.place_id
  9.5 3.5 %expand_bias.1 = (bf16[12,144,144]{2,1,0:T(8,128)(2,1)S(1)}, bf16[1152,384]{1,0:T(8,128)(2,1)S(1)}, bf16[384,384]{1,0:T(8,128)(2,1)S(1)}, bf16[192,192]{1,0:T(8,...) custom-call(bf16[12,3312]{1,0:T(8,128)(2,1)} %bitcast.11, ...), custom_call_target="tpu_custom_call" | custom-call | bytes 2097152 | tf_op jit(solution)/shard_map/expand_bias/pallas_call | solution.py:501
  13.0 0.0 collective-permute-done.lon_ref
  13.0 0.0 collective-permute-done.1.lat_ref
  13.0 0.0 collective-permute-done.2.diag_ref
  13.0 3.9 %window.1 = (bf16[2304,128]{1,0:T(8,128)(2,1)S(1)}, bf16[2304,128]{1,0:T(8,128)(2,1)S(1)}, bf16[12,144,144]{2,1,0:T(8,128)(2,1)S(1)}, bf16[4,384,144]{2,1,0:T(8,...) custom-call(s32[2]{0:T(128)S(1)} %pad_add_fusion.place_id, ...), custom_call_target="tpu_custom_call" | custom-call | flops 1000000000 | bytes 5242880 | tf_op jit(solution)/shard_map/window/pallas_call | solution.py:528
  16.9 0.1 collective-permute-start.3
  17.0 1.9 %fold_table.1.table_ref = bf16[320,128]{1,0:T(8,128)(2,1)S(1)} custom-call(bf16[12,144,144]{2,1,0:T(8,128)(2,1)S(1)} %get-tuple-element.71.scores_ref, bf16[384,384]{1,0:T(8,128)(2,1)S(1)} %get-tuple-element.72.lanes_ref, bf16[192,192]{1,0:T(8,128)(2,1)S(1)} %get-tuple-element.73.rows_ref), custom_call_target="tpu_custom_call" | custom-call | bytes 2097152 | tf_op jit(solution)/shard_map/fold_table/pallas_call | solution.py:561
  18.9 0.1 collective-permute-done.3.recv_ref
  19.0 0.7 %add_lat.1 = (bf16[656,128]{1,0:T(8,128)(2,1)S(1)}, bf16[656,128]{1,0:T(8,128)(2,1)S(1)}, bf16[656,128]{1,0:T(8,128)(2,1)S(1)}, bf16[656,128]{1,0:T(8,128)(2,1)S(1)}) custom-call(s32[2]{0:T(128)S(1)} %pad_add_fusion.place_id, bf16[2304,128]{1,0:T(8,128)(2,1)S(1)} %get-tuple-element.69.keep_ref, bf16[2304,128]{1,0:T(8,128)(2,1)S(1)} %collective-permute-done.3.recv_ref, ...), custom_call_target="tpu_custom_call" | custom-call | bytes 2097152 | tf_op jit(solution)/shard_map/add_lat/pallas_call | solution.py:575
  19.7 0.1 collective-permute-start.5
  19.8 2.9 %collective-permute-start.6 = (bf16[656,128]{1,0:T(8,128)(2,1)S(1)}, bf16[656,128]{1,0:T(8,128)(2,1)S(1)}, u32[]{:S(2)}, u32[]{:S(2)}) collective-permute-start(bf16[656,128]{1,0:T(8,128)(2,1)S(1)} %get-tuple-element.90), channel_id=1, source_target_pairs={{0,4},{2,6},{4,0},{6,2},{8,12},{10,14},{12,8},{14,10},{16,20},{18,... | collective-permute-start | bytes 503816 | tf_op jit(solution)/shard_map/ppermute | solution.py:477
  22.7 0.5 %collective-permute-start.7 = (bf16[656,128]{1,0:T(8,128)(2,1)S(1)}, bf16[656,128]{1,0:T(8,128)(2,1)S(1)}, u32[]{:S(2)}, u32[]{:S(2)}) collective-permute-start(bf16[656,128]{1,0:T(8,128)(2,1)S(1)} %get-tuple-element.91), channel_id=1, source_target_pairs={{0,2},{2,0},{4,6},{6,4},{8,10},{10,8},{12,14},{14,12},{16,18},{18,... | collective-permute-start | bytes 503816 | tf_op jit(solution)/shard_map/ppermute | solution.py:477
  23.2 1.0 %grad_field.1 = (bf16[36,384]{1,0:T(8,128)(2,1)S(1)}, bf16[72,384]{1,0:T(8,128)(2,1)S(1)}, bf16[36,384]{1,0:T(8,128)(2,1)S(1)}, bf16[16,128]{1,0:T(8,128)(2,1)S(1)}) custom-call(bf16[384,1152]{1,0:T(8,128)(2,1)S(1)} %get-tuple-element.58.win_ref, bf16[4,384,144]{2,1,0:T(8,128)(2,1)S(1)} %get-tuple-element.82.grad_projected_ref, ...), custom_call_target="tpu_custom_call" | custom-call | flops 100000000 | bytes 5242880 | tf_op jit(solution)/shard_map/grad_field/pallas_call | solution.py:589
  24.2 0.1 collective-permute-start.8
  24.3 0.5 %collective-permute-start.9 = (bf16[16,128]{1,0:T(8,128)(2,1)S(1)}, bf16[16,128]{1,0:T(8,128)(2,1)S(1)}, u32[]{:S(2)}, u32[]{:S(2)}) collective-permute-start(bf16[16,128]{1,0:T(8,128)(2,1)S(1)} %get-tuple-element.94.refs_0_), channel_id=1, source_target_pairs={{0,1},{1,0},{2,3},{3,2},{4,5},{5,4},{6,7},{7,6},{8,9},{9,8},{10,11... | collective-permute-start | bytes 12296 | tf_op jit(solution)/shard_map/ppermute | solution.py:477
  24.8 0.8 %collective-permute-done.9.refs_1_ = bf16[16,128]{1,0:T(8,128)(2,1)S(1)} collective-permute-done((bf16[16,128]{1,0:T(8,128)(2,1)S(1)}, bf16[16,128]{1,0:T(8,128)(2,1)S(1)}, u32[]{:S(2)}, u32[]{:S(2)}) %collective-permute-start.9) | collective-permute-done | bytes 4128 | tf_op jit(solution)/shard_map/ppermute | solution.py:477
  25.6 1.5 %collective-permute-start.4 = (bf16[72,384]{1,0:T(8,128)(2,1)S(1)}, bf16[72,384]{1,0:T(8,128)(2,1)S(1)}, u32[]{:S(2)}, u32[]{:S(2)}) collective-permute-start(bf16[72,384]{1,0:T(8,128)(2,1)S(1)} %get-tuple-element.88), channel_id=1, source_target_pairs={{0,2},{1,3},{2,4},{3,5},{4,6},{5,7},{6,8},{7,9},{8,10},{9,11},{10,... | collective-permute-start | bytes 165896 | tf_op jit(solution)/shard_map/ppermute | solution.py:473
  27.1 0.0 collective-permute-done.8.lat_ref
  27.1 0.7 %collective-permute-done.5.refs_2_ = bf16[656,128]{1,0:T(8,128)(2,1)S(1)} collective-permute-done((bf16[656,128]{1,0:T(8,128)(2,1)S(1)}, bf16[656,128]{1,0:T(8,128)(2,1)S(1)}, u32[]{:S(2)}, u32[]{:S(2)}) %collective-permute-start.5) | collective-permute-done | bytes 167968 | tf_op jit(solution)/shard_map/ppermute | solution.py:477
  27.8 3.1 %collective-permute-done.6.refs_3_ = bf16[656,128]{1,0:T(8,128)(2,1)S(1)} collective-permute-done((bf16[656,128]{1,0:T(8,128)(2,1)S(1)}, bf16[656,128]{1,0:T(8,128)(2,1)S(1)}, u32[]{:S(2)}, u32[]{:S(2)}) %collective-permute-start.6) | collective-permute-done | bytes 167968 | tf_op jit(solution)/shard_map/ppermute | solution.py:477
  30.9 0.0 collective-permute-done.7.refs_4_
  30.9 0.6 %add_lon.1 = (bf16[240,128]{1,0:T(8,128)(2,1)S(1)}, bf16[240,128]{1,0:T(8,128)(2,1)S(1)}, bf16[240,128]{1,0:T(8,128)(2,1)S(1)}, bf16[240,128]{1,0:T(8,128)(2,1)S(1)}) custom-call(s32[2]{0:T(128)S(1)} %pad_add_fusion.place_id, bf16[16,128]{1,0:T(8,128)(2,1)S(1)} %get-tuple-element.94.refs_0_, bf16[16,128]{1,0:T(8,128)(2,1)S(1)} %collective-permute-done.9.refs_1_, ...), custom_call_target="tpu_custom_call" | custom-call | bytes 1048576 | tf_op jit(solution)/shard_map/add_lon/pallas_call | solution.py:605
  31.5 3.2 %collective-permute-start.11 = (bf16[240,128]{1,0:T(8,128)(2,1)S(1)}, bf16[240,128]{1,0:T(8,128)(2,1)S(1)}, u32[]{:S(2)}, u32[]{:S(2)}) collective-permute-start(bf16[240,128]{1,0:T(8,128)(2,1)S(1)} %get-tuple-element.101), channel_id=1, source_target_pairs={{0,24},{2,26},{4,28},{6,30},{8,16},{10,18},{12,20},{14,22},{16,8},... | collective-permute-start | bytes 184328 | tf_op jit(solution)/shard_map/ppermute | solution.py:477
  34.7 0.0 collective-permute-start.12
  34.7 1.3 %collective-permute-start.13 = (bf16[240,128]{1,0:T(8,128)(2,1)S(1)}, bf16[240,128]{1,0:T(8,128)(2,1)S(1)}, u32[]{:S(2)}, u32[]{:S(2)}) collective-permute-start(bf16[240,128]{1,0:T(8,128)(2,1)S(1)} %get-tuple-element.103), channel_id=1, source_target_pairs={{0,8},{2,10},{4,12},{6,14},{8,0},{10,2},{12,4},{14,6},{16,24},{18,... | collective-permute-start | bytes 184328 | tf_op jit(solution)/shard_map/ppermute | solution.py:477
  35.9 0.0 collective-permute-done.4.lon_ref
  35.9 0.0 collective-permute-start.10
  35.9 2.1 %collective-permute-done.11.a_ref = bf16[240,128]{1,0:T(8,128)(2,1)S(1)} collective-permute-done((bf16[240,128]{1,0:T(8,128)(2,1)S(1)}, bf16[240,128]{1,0:T(8,128)(2,1)S(1)}, u32[]{:S(2)}, u32[]{:S(2)}) %collective-permute-start.11) | collective-permute-done | bytes 61472 | tf_op jit(solution)/shard_map/ppermute | solution.py:477
  38.1 1.9 %collective-permute-done.12.b_ref = bf16[240,128]{1,0:T(8,128)(2,1)S(1)} collective-permute-done((bf16[240,128]{1,0:T(8,128)(2,1)S(1)}, bf16[240,128]{1,0:T(8,128)(2,1)S(1)}, u32[]{:S(2)}, u32[]{:S(2)}) %collective-permute-start.12) | collective-permute-done | bytes 61472 | tf_op jit(solution)/shard_map/ppermute | solution.py:477
  40.0 0.2 collective-permute-done.13.c_ref
  40.3 0.1 collective-permute-start.14
  40.4 1.1 %collective-permute-start.17 = (bf16[96,128]{1,0:T(8,128)(2,1)S(1)}, bf16[96,128]{1,0:T(8,128)(2,1)S(1)}, u32[]{:S(2)}, u32[]{:S(2)}) collective-permute-start(bf16[96,128]{1,0:T(8,128)(2,1)S(1)} %get-tuple-element.106.a_ref), channel_id=1, source_target_pairs={{0,6},{2,4},{4,2},{6,0},{8,14},{10,12},{12,10},{14,8},{16,22},{18,... | collective-permute-start | bytes 73736 | tf_op jit(solution)/shard_map/ppermute | solution.py:477
  41.5 1.2 %collective-permute-start.16 = (bf16[96,128]{1,0:T(8,128)(2,1)S(1)}, bf16[96,128]{1,0:T(8,128)(2,1)S(1)}, u32[]{:S(2)}, u32[]{:S(2)}) collective-permute-start(bf16[96,128]{1,0:T(8,128)(2,1)S(1)} %get-tuple-element.106.a_ref), channel_id=1, source_target_pairs={{0,4},{2,6},{4,0},{6,2},{8,12},{10,14},{12,8},{14,10},{16,20},{18,... | collective-permute-start | bytes 73736 | tf_op jit(solution)/shard_map/ppermute | solution.py:477
  42.6 1.3 %collective-permute-start.15 = (bf16[96,128]{1,0:T(8,128)(2,1)S(1)}, bf16[96,128]{1,0:T(8,128)(2,1)S(1)}, u32[]{:S(2)}, u32[]{:S(2)}) collective-permute-start(bf16[96,128]{1,0:T(8,128)(2,1)S(1)} %get-tuple-element.106.a_ref), channel_id=1, source_target_pairs={{0,2},{2,0},{4,6},{6,4},{8,10},{10,8},{12,14},{14,12},{16,18},{18,... | collective-permute-start | bytes 73736 | tf_op jit(solution)/shard_map/ppermute | solution.py:477
  43.9 0.0 collective-permute-done.10.diag_ref
  43.9 0.7 %unpack_quarters.1 = bf16[6,12,2,384]{3,2,1,0:T(2,128)(2,1)} custom-call(bf16[36,384]{1,0:T(8,128)(2,1)S(1)} %get-tuple-element.87.own_ref, bf16[72,384]{1,0:T(8,128)(2,1)S(1)} %collective-permute-done.4.lon_ref, bf16[36,384]{1,0:T(8,128)(2,1)S(1)} %collective-permute-done.8.lat_ref, bf16[72,384]{1,0:T(8,128)(2,1)S(1)} %collective-permute-done.10.diag_ref), custom_call_target="tpu_custom_call" | custom-call | bytes 4194304 | tf_op jit(solution)/shard_map/unpack_quarters/pallas_call | solution.py:644
  44.6 0.6 %collective-permute-done.17.d_ref = bf16[96,128]{1,0:T(8,128)(2,1)S(1)} collective-permute-done((bf16[96,128]{1,0:T(8,128)(2,1)S(1)}, bf16[96,128]{1,0:T(8,128)(2,1)S(1)}, u32[]{:S(2)}, u32[]{:S(2)}) %collective-permute-start.17) | collective-permute-done | bytes 24608 | tf_op jit(solution)/shard_map/ppermute | solution.py:477
  45.2 0.3 collective-permute-done.16.c_ref
  45.4 1.1 %collective-permute-done.15.b_ref = bf16[96,128]{1,0:T(8,128)(2,1)S(1)} collective-permute-done((bf16[96,128]{1,0:T(8,128)(2,1)S(1)}, bf16[96,128]{1,0:T(8,128)(2,1)S(1)}, u32[]{:S(2)}, u32[]{:S(2)}) %collective-permute-start.15) | collective-permute-done | bytes 24608 | tf_op jit(solution)/shard_map/ppermute | solution.py:477
  46.5 0.0 collective-permute-done.14.other_weights_ref
  46.5 1.3 %finish.1 = (bf16[24,1152]{1,0:T(8,128)(2,1)}, bf16[24,384]{1,0:T(8,128)(2,1)}, f32[12,1,3312]{2,1,0:T(1,128)}, f32[384]{0:T(512)}) custom-call(s32[2]{0:T(128)S(1)} %pad_add_fusion.place_id, bf16[144,128]{1,0:T(8,128)(2,1)S(1)} %get-tuple-element.105.weights_ref, bf16[144,128]{1,0:T(8,128)(2,1)S(1)} %collective-permute-done.14.other_weights_ref, ...), custom_call_target="tpu_custom_call" | custom-call | bytes 524288 | tf_op jit(solution)/shard_map/finish/pallas_call | solution.py:628
  (1 shorter events, 0.0 us)
Async XLA Ops:
  1.8 11.2 %collective-permute-start = (bf16[72,384]{1,0:T(8,128)(2,1)S(1)}, bf16[72,384]{1,0:T(8,128)(2,1)S(1)}, u32[]{:S(2)}, u32[]{:S(2)}) collective-permute-start(bf16[72,384]{1,0:T(8,128)(2,1)S(1)} %get-tuple-element.60), channel_id=1, source_target_pairs={{0,30},{1,31},{2,0},{3,1},{4,2},{5,3},{6,4},{7,5},{8,6},{9,7},{10,... | collective-permute-start | bytes 165896 | tf_op jit(solution)/shard_map/ppermute | solution.py:473
  8.8 4.2 %collective-permute-start.1 = (bf16[72,384]{1,0:T(8,128)(2,1)S(1)}, bf16[72,384]{1,0:T(8,128)(2,1)S(1)}, u32[]{:S(2)}, u32[]{:S(2)}) collective-permute-start(bf16[72,384]{1,0:T(8,128)(2,1)S(1)} %get-tuple-element.61), channel_id=1, source_target_pairs={{0,1},{1,0},{2,3},{3,2},{4,5},{5,4},{6,7},{7,6},{8,9},{9,8},{10,11... | collective-permute-start | bytes 165896 | tf_op jit(solution)/shard_map/ppermute | solution.py:473
  8.8 4.3 %collective-permute-start.2 = (bf16[72,384]{1,0:T(8,128)(2,1)S(1)}, bf16[72,384]{1,0:T(8,128)(2,1)S(1)}, u32[]{:S(2)}, u32[]{:S(2)}) collective-permute-start(bf16[72,384]{1,0:T(8,128)(2,1)S(1)} %get-tuple-element.62), channel_id=1, source_target_pairs={{0,31},{1,30},{2,1},{3,0},{4,3},{5,2},{6,5},{7,4},{8,7},{9,6},{10,... | collective-permute-start | bytes 165896 | tf_op jit(solution)/shard_map/ppermute | solution.py:473
  16.9 2.1 %collective-permute-start.3 = (bf16[2304,128]{1,0:T(8,128)(2,1)S(1)}, bf16[2304,128]{1,0:T(8,128)(2,1)S(1)}, u32[]{:S(2)}, u32[]{:S(2)}) collective-permute-start(bf16[2304,128]{1,0:T(8,128)(2,1)S(1)} %get-tuple-element.70), channel_id=1, source_target_pairs={{0,1},{1,0},{2,3},{3,2},{4,5},{5,4},{6,7},{7,6},{8,9},{9,8},{10,11... | collective-permute-start | bytes 1769480 | tf_op jit(solution)/shard_map/ppermute | solution.py:477
  19.7 8.1 %collective-permute-start.5 = (bf16[656,128]{1,0:T(8,128)(2,1)S(1)}, bf16[656,128]{1,0:T(8,128)(2,1)S(1)}, u32[]{:S(2)}, u32[]{:S(2)}) collective-permute-start(bf16[656,128]{1,0:T(8,128)(2,1)S(1)} %get-tuple-element.89), channel_id=1, source_target_pairs={{0,6},{2,4},{4,2},{6,0},{8,14},{10,12},{12,10},{14,8},{16,22},{18,... | collective-permute-start | bytes 503816 | tf_op jit(solution)/shard_map/ppermute | solution.py:477
  19.8 11.1 %collective-permute-start.6 = (bf16[656,128]{1,0:T(8,128)(2,1)S(1)}, bf16[656,128]{1,0:T(8,128)(2,1)S(1)}, u32[]{:S(2)}, u32[]{:S(2)}) collective-permute-start(bf16[656,128]{1,0:T(8,128)(2,1)S(1)} %get-tuple-element.90), channel_id=1, source_target_pairs={{0,4},{2,6},{4,0},{6,2},{8,12},{10,14},{12,8},{14,10},{16,20},{18,... | collective-permute-start | bytes 503816 | tf_op jit(solution)/shard_map/ppermute | solution.py:477
  22.7 8.2 %collective-permute-start.7 = (bf16[656,128]{1,0:T(8,128)(2,1)S(1)}, bf16[656,128]{1,0:T(8,128)(2,1)S(1)}, u32[]{:S(2)}, u32[]{:S(2)}) collective-permute-start(bf16[656,128]{1,0:T(8,128)(2,1)S(1)} %get-tuple-element.91), channel_id=1, source_target_pairs={{0,2},{2,0},{4,6},{6,4},{8,10},{10,8},{12,14},{14,12},{16,18},{18,... | collective-permute-start | bytes 503816 | tf_op jit(solution)/shard_map/ppermute | solution.py:477
  24.2 2.9 %collective-permute-start.8 = (bf16[36,384]{1,0:T(8,128)(2,1)S(1)}, bf16[36,384]{1,0:T(8,128)(2,1)S(1)}, u32[]{:S(2)}, u32[]{:S(2)}) collective-permute-start(bf16[36,384]{1,0:T(8,128)(2,1)S(1)} %get-tuple-element.93), channel_id=1, source_target_pairs={{0,1},{1,0},{2,3},{3,2},{4,5},{5,4},{6,7},{7,6},{8,9},{9,8},{10,11... | collective-permute-start | bytes 82952 | tf_op jit(solution)/shard_map/ppermute | solution.py:473
  24.3 1.3 %collective-permute-start.9 = (bf16[16,128]{1,0:T(8,128)(2,1)S(1)}, bf16[16,128]{1,0:T(8,128)(2,1)S(1)}, u32[]{:S(2)}, u32[]{:S(2)}) collective-permute-start(bf16[16,128]{1,0:T(8,128)(2,1)S(1)} %get-tuple-element.94.refs_0_), channel_id=1, source_target_pairs={{0,1},{1,0},{2,3},{3,2},{4,5},{5,4},{6,7},{7,6},{8,9},{9,8},{10,11... | collective-permute-start | bytes 12296 | tf_op jit(solution)/shard_map/ppermute | solution.py:477
  25.6 10.3 %collective-permute-start.4 = (bf16[72,384]{1,0:T(8,128)(2,1)S(1)}, bf16[72,384]{1,0:T(8,128)(2,1)S(1)}, u32[]{:S(2)}, u32[]{:S(2)}) collective-permute-start(bf16[72,384]{1,0:T(8,128)(2,1)S(1)} %get-tuple-element.88), channel_id=1, source_target_pairs={{0,2},{1,3},{2,4},{3,5},{4,6},{5,7},{6,8},{7,9},{8,10},{9,11},{10,... | collective-permute-start | bytes 165896 | tf_op jit(solution)/shard_map/ppermute | solution.py:473
  31.5 6.6 %collective-permute-start.11 = (bf16[240,128]{1,0:T(8,128)(2,1)S(1)}, bf16[240,128]{1,0:T(8,128)(2,1)S(1)}, u32[]{:S(2)}, u32[]{:S(2)}) collective-permute-start(bf16[240,128]{1,0:T(8,128)(2,1)S(1)} %get-tuple-element.101), channel_id=1, source_target_pairs={{0,24},{2,26},{4,28},{6,30},{8,16},{10,18},{12,20},{14,22},{16,8},... | collective-permute-start | bytes 184328 | tf_op jit(solution)/shard_map/ppermute | solution.py:477
  34.7 5.3 %collective-permute-start.12 = (bf16[240,128]{1,0:T(8,128)(2,1)S(1)}, bf16[240,128]{1,0:T(8,128)(2,1)S(1)}, u32[]{:S(2)}, u32[]{:S(2)}) collective-permute-start(bf16[240,128]{1,0:T(8,128)(2,1)S(1)} %get-tuple-element.102), channel_id=1, source_target_pairs={{0,16},{2,18},{4,20},{6,22},{8,24},{10,26},{12,28},{14,30},{16,0},... | collective-permute-start | bytes 184328 | tf_op jit(solution)/shard_map/ppermute | solution.py:477
  34.7 5.6 %collective-permute-start.13 = (bf16[240,128]{1,0:T(8,128)(2,1)S(1)}, bf16[240,128]{1,0:T(8,128)(2,1)S(1)}, u32[]{:S(2)}, u32[]{:S(2)}) collective-permute-start(bf16[240,128]{1,0:T(8,128)(2,1)S(1)} %get-tuple-element.103), channel_id=1, source_target_pairs={{0,8},{2,10},{4,12},{6,14},{8,0},{10,2},{12,4},{14,6},{16,24},{18,... | collective-permute-start | bytes 184328 | tf_op jit(solution)/shard_map/ppermute | solution.py:477
  35.9 8.0 %collective-permute-start.10 = (bf16[72,384]{1,0:T(8,128)(2,1)S(1)}, bf16[72,384]{1,0:T(8,128)(2,1)S(1)}, u32[]{:S(2)}, u32[]{:S(2)}) collective-permute-start(bf16[72,384]{1,0:T(8,128)(2,1)S(1)} %collective-permute-done.4.lon_ref), channel_id=1, source_target_pairs={{0,1},{1,0},{2,3},{3,2},{4,5},{5,4},{6,7},{7,6},{8,9},{9,8},{10,11... | collective-permute-start | bytes 165896 | tf_op jit(solution)/shard_map/ppermute | solution.py:473
  40.3 6.2 %collective-permute-start.14 = (bf16[144,128]{1,0:T(8,128)(2,1)S(1)}, bf16[144,128]{1,0:T(8,128)(2,1)S(1)}, u32[]{:S(2)}, u32[]{:S(2)}) collective-permute-start(bf16[144,128]{1,0:T(8,128)(2,1)S(1)} %get-tuple-element.105.weights_ref), channel_id=1, source_target_pairs={{0,1},{1,0},{2,3},{3,2},{4,5},{5,4},{6,7},{7,6},{8,9},{9,8},{10,11... | collective-permute-start | bytes 110600 | tf_op jit(solution)/shard_map/ppermute | solution.py:477
  40.4 4.8 %collective-permute-start.17 = (bf16[96,128]{1,0:T(8,128)(2,1)S(1)}, bf16[96,128]{1,0:T(8,128)(2,1)S(1)}, u32[]{:S(2)}, u32[]{:S(2)}) collective-permute-start(bf16[96,128]{1,0:T(8,128)(2,1)S(1)} %get-tuple-element.106.a_ref), channel_id=1, source_target_pairs={{0,6},{2,4},{4,2},{6,0},{8,14},{10,12},{12,10},{14,8},{16,22},{18,... | collective-permute-start | bytes 73736 | tf_op jit(solution)/shard_map/ppermute | solution.py:477
  41.5 4.0 %collective-permute-start.16 = (bf16[96,128]{1,0:T(8,128)(2,1)S(1)}, bf16[96,128]{1,0:T(8,128)(2,1)S(1)}, u32[]{:S(2)}, u32[]{:S(2)}) collective-permute-start(bf16[96,128]{1,0:T(8,128)(2,1)S(1)} %get-tuple-element.106.a_ref), channel_id=1, source_target_pairs={{0,4},{2,6},{4,0},{6,2},{8,12},{10,14},{12,8},{14,10},{16,20},{18,... | collective-permute-start | bytes 73736 | tf_op jit(solution)/shard_map/ppermute | solution.py:477
  42.6 3.8 %collective-permute-start.15 = (bf16[96,128]{1,0:T(8,128)(2,1)S(1)}, bf16[96,128]{1,0:T(8,128)(2,1)S(1)}, u32[]{:S(2)}, u32[]{:S(2)}) collective-permute-start(bf16[96,128]{1,0:T(8,128)(2,1)S(1)} %get-tuple-element.106.a_ref), channel_id=1, source_target_pairs={{0,2},{2,0},{4,6},{6,4},{8,10},{10,8},{12,14},{14,12},{16,18},{18,... | collective-permute-start | bytes 73736 | tf_op jit(solution)/shard_map/ppermute | solution.py:477

commit v2 on v1

--- a/solution.py
+++ b/solution.py
@@ -70,8 +70,9 @@
 
 
 def load_kernel(field_src, cot_src, *refs):
-    out_refs, (field_ref, cot_ref, sems) = refs[:4], refs[4:]
-    for copy in fetch((field_src, cot_src), (field_ref, cot_ref), sems):
+    sources, out_refs, targets, (field_ref, cot_ref, sems) = refs[:3], refs[3:7], refs[7:10], refs[10:]
+    copies = fetch((field_src, cot_src) + sources, (field_ref, cot_ref) + targets, sems)
+    for copy in copies[:2]:
         copy.wait()
     half_rows, half_cols = WIN_LAT // 2, WIN_LON // 2
     for (lat_half, lon_half), out_ref in zip(QUARTERS, out_refs):
@@ -82,6 +83,8 @@
                 for col in range(half_cols):
                     pieces.append(ref[first_row + row, first_col + col].astype(f32))
         out_ref[...] = jnp.concatenate(pieces, axis=0).astype(bf16)
+    for copy in copies[2:]:
+        copy.wait()
 
 
 def one_hot(flags):
@@ -113,11 +116,10 @@
 
 
 def bias_kernel(
-    table_src,
-    regions_src,
+    table_ref,
+    regions_ref,
     win_src,
     wout_src,
-    gain_src,
     out_ref,
     win_t_ref,
     lanes_ref,
@@ -127,15 +129,11 @@
     place_t_ref,
     win_ref,
     wout_ref,
-    gain_ref,
     stage,
     full,
-    table_ref,
-    regions_ref,
     sems,
 ):
-    sources = (table_src, regions_src, win_src, wout_src, gain_src)
-    copies = fetch(sources, (table_ref, regions_ref, win_ref, wout_ref, gain_ref), sems)
+    copies = fetch((win_src, wout_src), (win_ref, wout_ref), sems)
     features = win_ref.shape[0]
     square = (features, features)
     eye = one_hot(counted(square, 0) == counted(square, 1))
@@ -154,11 +152,6 @@
 
     stage[...] = jnp.zeros(stage.shape, f32)
     reach = SPAN // PLANE
-    for copy in copies:
-        copy.wait()
-    for block in range(3):
-        cols = slice(block * features, (block + 1) * features)
-        win_t_ref[cols] = nt_dot(eye, win_ref[:, cols]).astype(bf16)
     table = table_ref[...].astype(f32)
     for first, plane_i, plane_j in segments():
         stage[16 * plane_j : 16 * plane_j + HEADS, reach * plane_i : reach * (plane_i + 1)] = table[
@@ -183,11 +176,15 @@
             full[head, PLANE * col : PLANE * (col + 1), :] = moved[16 * head : 16 * head + PLANE, :CELLS]
     for head in range(HEADS):
         out_ref[head] = jnp.where(same, full[head], masked_score).astype(bf16)
+    for copy in copies:
+        copy.wait()
+    for block in range(3):
+        cols = slice(block * features, (block + 1) * features)
+        win_t_ref[cols] = nt_dot(eye, win_ref[:, cols]).astype(bf16)
 
 
 def window_kernel(
     packet,
-    place_id,
     own_ref,
     lon_ref,
     lat_ref,
@@ -281,7 +278,7 @@
         if 1 <= turn <= HEADS:
             soft[turn - 1] = softmax_of(turn - 1, *raw.pop(turn - 1))
 
-    odd = lax.rem(place_id[1], 2)
+    odd = lax.rem(lax.axis_index("lat"), 2)
 
     for out_ref, half in ((send_ref, 1 - odd), (keep_ref, odd)):
         low = nt_dot(left[0], right[2 * half])
@@ -355,8 +352,8 @@
     out_ref[...] = jnp.concatenate(tiles, axis=0).astype(bf16)
 
 
-def first_exchange_kernel(packet, place_id, keep_ref, recv_ref, table_ref, *out_refs):
-    low = lax.rem(place_id[0], 4)
+def first_exchange_kernel(packet, keep_ref, recv_ref, table_ref, *out_refs):
+    low = lax.rem(lax.axis_index("lon"), 4)
     size, quarter = packet.weight_size, packet.quarter
     for step, out_ref in enumerate(out_refs):
         digit = lax.bitwise_xor(low, step)
@@ -374,10 +371,10 @@
     return terms[0]
 
 
-def next_exchange_kernel(packet, shift, gains, place_id, *refs):
+def next_exchange_kernel(packet, shift, gains, *refs):
     gain_refs, held, out_refs = refs[:gains], refs[gains:-4], refs[-4:]
     size, quarter = packet.weight_size, packet.quarter
-    digit = lax.rem(lax.shift_right_logical(place_id[0], shift), 4)
+    digit = lax.rem(lax.shift_right_logical(lax.axis_index("lon"), shift), 4)
     groups = (out_refs[0].shape[0] - quarter - 16) // size
     rest = 4 * groups * size
     table = summed(held, slice(rest, rest + quarter))
@@ -400,7 +397,6 @@
     packet,
     table_scale,
     factor,
-    place_id,
     weights_ref,
     other_weights_ref,
     a_ref,
@@ -413,7 +409,7 @@
     grad_gain_ref,
     quarters,
 ):
-    odd = lax.rem(place_id[1], 2) == 1
+    odd = lax.rem(lax.axis_index("lat"), 2) == 1
     own, other = weights_ref[...].astype(f32) * factor, other_weights_ref[...].astype(f32) * factor
     halves = (jnp.where(odd, other, own), jnp.where(odd, own, other))
     size = packet.weight_rows
@@ -421,7 +417,7 @@
     grad_in_ref[...] = jnp.concatenate(tiles[:9], axis=1).astype(bf16)
     grad_out_ref[...] = jnp.concatenate(tiles[9:], axis=1).astype(bf16)
 
-    low = lax.rem(place_id[0], 4)
+    low = lax.rem(lax.axis_index("lon"), 4)
     parts = (a_ref, b_ref, c_ref, d_ref)
     for step, ref in enumerate(parts):
         quarters[lax.bitwise_xor(low, step)] = ref[: packet.quarter].astype(f32)
@@ -442,9 +438,6 @@
     return [pl.BlockSpec(memory_space=pltpu.VMEM)] * count
 
 
-scalars = pl.BlockSpec(memory_space=pltpu.SMEM)
-
-
 def call(kernel, name, in_specs, outs, scratch=(), flops=0, moved=0):
     return pl.pallas_call(
         kernel,
@@ -462,7 +455,6 @@
     features = latent_field.shape[3]
     head_dim = features // HEADS
     packet = Packet(lon_count, features)
-    place_id = jnp.stack([lax.axis_index("lon"), lax.axis_index("lat")]).astype(jnp.int32)
 
     def move(value, lon_step, lat_step):
         pairs = []
@@ -485,23 +477,23 @@
 
     hbm = pl.BlockSpec(memory_space=pltpu.HBM)
     field, cot = jnp.transpose(latent_field, (1, 2, 0, 3)), jnp.transpose(cotangent, (1, 2, 0, 3))
-    own, to_lon, to_lat, to_diag = call(
+    small = (bias_table[0], jnp.transpose(regions, (1, 0, 2)), norm_gain)
+    own, to_lon, to_lat, to_diag, table, region_grid, gain = call(
         load_kernel,
         "load",
-        [hbm] * 2,
-        [struct((2 * QUARTER, features), bf16)] * 4,
-        [space_for(field), space_for(cot), pltpu.SemaphoreType.DMA((2,))],
+        [hbm] * 5,
+        [struct((2 * QUARTER, features), bf16)] * 4 + [struct(array.shape, array.dtype) for array in small],
+        [space_for(field), space_for(cot), pltpu.SemaphoreType.DMA((5,))],
         moved=1 << 20,
-    )(*in_hbm(field, cot))
+    )(*in_hbm(field, cot, *small))
     from_lon = move(to_lon, -1, 0)
     from_diag = move(to_diag, -1, -1)
     from_lat = move(to_lat, 0, -1)
 
-    table, region_grid = bias_table[0], jnp.transpose(regions, (1, 0, 2))
-    bias_full, input_weight_t, lane_moves, row_moves, eye, place, place_t, weight_in, weight_out, gain = call(
+    bias_full, input_weight_t, lane_moves, row_moves, eye, place, place_t, weight_in, weight_out = call(
         bias_kernel,
         "expand_bias",
-        [hbm] * 5,
+        whole(2) + [hbm] * 2,
         [
             struct((HEADS, CELLS, CELLS), bf16),
             struct((3 * features, features), bf16),
@@ -512,23 +504,20 @@
             struct((CELLS, CELLS), bf16),
             struct(input_weight.shape, bf16),
             struct(output_weight.shape, bf16),
-            struct(norm_gain.shape, f32),
         ],
         [
             pltpu.VMEM((HEADS * 16, WIDE), f32),
             pltpu.VMEM((HEADS, CELLS, CELLS), f32),
-            space_for(table),
-            space_for(region_grid),
-            pltpu.SemaphoreType.DMA((5,)),
+            pltpu.SemaphoreType.DMA((2,)),
         ],
         moved=1 << 21,
-    )(*in_hbm(table, region_grid, input_weight, output_weight, norm_gain))
+    )(table, region_grid, *in_hbm(input_weight, output_weight))
 
     half_sum = struct((lon_count * packet.weight_size, LANES), bf16)
     results = call(
         functools.partial(window_kernel, packet),
         "window",
-        [scalars] + whole(11),
+        whole(11),
         [
             half_sum,
             half_sum,
@@ -542,8 +531,7 @@
         flops=10**9,
         moved=5 << 20,
     )(
-        place_id,
-        own,
+            own,
         from_lon,
         from_lat,
         from_diag,
@@ -575,10 +563,10 @@
     parts = call(
         functools.partial(first_exchange_kernel, packet),
         "add_lat",
-        [scalars] + whole(3),
+        whole(3),
         [struct((groups * packet.weight_size + packet.quarter, LANES), bf16)] * 4,
         moved=2 << 20,
-    )(place_id, keep, received, table_part)
+    )(keep, received, table_part)
     parts, saved = lax.optimization_barrier((parts, saved))
 
     def trade(parts, shift):
@@ -605,10 +593,10 @@
         parts = call(
             functools.partial(next_exchange_kernel, packet, shift, len(gains)),
             "add_lon",
-            [scalars] + whole(len(gains) + 4),
+            whole(len(gains) + 4),
             [struct((groups * packet.weight_size + packet.quarter + 16, LANES), bf16)] * 4,
             moved=1 << 20,
-        )(place_id, *gains, *held)
+        )(*gains, *held)
         gains = []
         held = trade(parts, shift)
     weight_sum, table_sum = call(
@@ -628,7 +616,7 @@
     grad_input_weight, grad_output_weight, grad_table, gain_sum = call(
         functools.partial(finish_kernel, packet, math.sqrt(head_dim), factor),
         "finish",
-        [scalars] + whole(6),
+        whole(6),
         [
             struct((packet.weight_rows, 3 * features), bf16),
             struct((packet.weight_rows, features), bf16),
@@ -637,7 +625,7 @@
         ],
         [pltpu.VMEM((4, packet.quarter, LANES), f32)],
         moved=1 << 19,
-    )(place_id, weight_sum, weight_other, *table_parts)
+    )(weight_sum, weight_other, *table_parts)
     for bit in range(1, lat_count.bit_length() - 1):
         gain_sum = gain_sum + swap(gain_sum, "lat", 1 << bit)
 

time: 48 us -> 45.9 us (0.956)
  Pallas kernels: 14.8 us -> 12.3 us
    pallas_call x4, Pallas kernels: 9.2 us -> 7.8 us  [the longest x1 3.35 us: on_device(): call(functools.partial(window_kernel, packet), 'window', whole(11), [half...]
    pallas_call x1, Pallas kernels: 1.33 us -> 0.79 us  [on_device(): call(functools.partial(finish_kernel, packet, math.sqrt(head_dim), factor...]
    pallas_call x1, Pallas kernels: 0.63 us -> 0.09 us  [on_device(): call(functools.partial(next_exchange_kernel, packet, shift, len(gains)),...]
  transfers between devices with their start and end apart: 18 -> 18, of which waited for: 10 -> 8; matrix products, arithmetic and copies ran while one was open for 0% -> 0% of each run, Pallas kernels for 16% -> 15%
where the time goes in v2:
time: 45.9 us; the launch traced here: 45.7 us
  starting transfers between devices  21.4 us (47%)
  Pallas kernels  12.3 us (27%)
  waiting for transfers between devices  11.2 us (24%)
  between operations  0.75 us (2%)
    ppermute x12, starting transfers between devices, swap(): lax.ppermute(value, axis, [(source, source ^ mask) for source in range(co...  12.4 us
    ppermute x12, waiting for transfers between devices, swap(): lax.ppermute(value, axis, [(source, source ^ mask) for source in range(co...  11.2 us
    ppermute x6, starting transfers between devices, move(): return lax.ppermute(value, ('lon', 'lat'), pairs)  9.02 us
    pallas_call x1, Pallas kernels, on_device(): call(functools.partial(window_kernel, packet), 'window', whole(11), [half...  3.35 us
    pallas_call x1, Pallas kernels, on_device(): call(bias_kernel, 'expand_bias', whole(2) + [hbm] * 2, [struct((HEADS, CE...  3.14 us
    pallas_call x1, Pallas kernels, on_device(): call(functools.partial(fold_kernel, packet), 'fold_table', whole(3), stru...  1.91 us
    pallas_call x1, Pallas kernels, on_device(): call(load_kernel, 'load', [hbm] * 5, [struct((2 * QUARTER, features), bf1...  1.16 us
    pallas_call x1, Pallas kernels, on_device(): call(field_kernel, 'grad_field', whole(8), [piece, struct((2 * QUARTER, f...  1 us
  transfers between devices with their start and end apart: 18, of which 8 were waited for; matrix products, arithmetic and copies ran while one was open for 0% of the time, Pallas kernels for 15%

profile of v2, /device:TPU:0, one launch (start us, length us, event | category | flops | bytes accessed | tf_op | source)
XLA Modules:
  0.0 45.7 jit_solution(13551050283054120691)
XLA Ops:
  0.6 1.2 %load.1 = (bf16[72,384]{1,0:T(8,128)(2,1)S(1)}, bf16[72,384]{1,0:T(8,128)(2,1)S(1)}, bf16[72,384]{1,0:T(8,128)(2,1)S(1)}, bf16[72,384]{1,0:T(8,128)(2,1)S(1)}, b...) custom-call(bf16[6,12,2,384]{3,2,1,0:T(2,128)(2,1)} %bitcast.7, ...), custom_call_target="tpu_custom_call" | custom-call | bytes 1048576 | tf_op jit(solution)/shard_map/load/pallas_call | solution.py:481
  1.8 7.0 %collective-permute-start = (bf16[72,384]{1,0:T(8,128)(2,1)S(1)}, bf16[72,384]{1,0:T(8,128)(2,1)S(1)}, u32[]{:S(2)}, u32[]{:S(2)}) collective-permute-start(bf16[72,384]{1,0:T(8,128)(2,1)S(1)} %get-tuple-element.64), channel_id=1, source_target_pairs={{0,30},{1,31},{2,0},{3,1},{4,2},{5,3},{6,4},{7,5},{8,6},{9,7},{10,... | collective-permute-start | bytes 165896 | tf_op jit(solution)/shard_map/ppermute | solution.py:465
  8.8 0.0 collective-permute-start.1
  8.8 0.6 %collective-permute-start.2 = (bf16[72,384]{1,0:T(8,128)(2,1)S(1)}, bf16[72,384]{1,0:T(8,128)(2,1)S(1)}, u32[]{:S(2)}, u32[]{:S(2)}) collective-permute-start(bf16[72,384]{1,0:T(8,128)(2,1)S(1)} %get-tuple-element.66), channel_id=1, source_target_pairs={{0,31},{1,30},{2,1},{3,0},{4,3},{5,2},{6,5},{7,4},{8,7},{9,6},{10,... | collective-permute-start | bytes 165896 | tf_op jit(solution)/shard_map/ppermute | solution.py:465
  9.4 3.1 %expand_bias.1 = (bf16[12,144,144]{2,1,0:T(8,128)(2,1)S(1)}, bf16[1152,384]{1,0:T(8,128)(2,1)S(1)}, bf16[384,384]{1,0:T(8,128)(2,1)S(1)}, bf16[192,192]{1,0:T(8,...) custom-call(bf16[12,3312]{1,0:T(8,128)(2,1)S(1)} %get-tuple-element., ...), custom_call_target="tpu_custom_call" | custom-call | bytes 2097152 | tf_op jit(solution)/shard_map/expand_bias/pallas_call | solution.py:493
  12.6 0.0 collective-permute-done.lon_ref
  12.6 0.0 collective-permute-done.1.lat_ref
  12.6 0.0 collective-permute-done.2.diag_ref
  12.6 3.3 %window.1 = (bf16[2304,128]{1,0:T(8,128)(2,1)S(1)}, bf16[2304,128]{1,0:T(8,128)(2,1)S(1)}, bf16[12,144,144]{2,1,0:T(8,128)(2,1)S(1)}, bf16[4,384,144]{2,1,0:T(8,...) custom-call(bf16[72,384]{1,0:T(8,128)(2,1)S(1)} %get-tuple-element.63.own_ref, ...), custom_call_target="tpu_custom_call" | custom-call | flops 1000000000 | bytes 5242880 | tf_op jit(solution)/shard_map/window/pallas_call | solution.py:517
  16.0 0.3 collective-permute-start.3
  16.3 1.9 %fold_table.1.table_ref = bf16[320,128]{1,0:T(8,128)(2,1)S(1)} custom-call(bf16[12,144,144]{2,1,0:T(8,128)(2,1)S(1)} %get-tuple-element.75.scores_ref, bf16[384,384]{1,0:T(8,128)(2,1)S(1)} %get-tuple-element.76.lanes_ref, bf16[192,192]{1,0:T(8,128)(2,1)S(1)} %get-tuple-element.77.rows_ref), custom_call_target="tpu_custom_call" | custom-call | bytes 2097152 | tf_op jit(solution)/shard_map/fold_table/pallas_call | solution.py:549
  18.2 0.0 collective-permute-done.3.recv_ref
  18.2 0.1 add_lat.1
  18.4 0.1 collective-permute-start.5
  18.4 2.8 %collective-permute-start.6 = (bf16[656,128]{1,0:T(8,128)(2,1)S(1)}, bf16[656,128]{1,0:T(8,128)(2,1)S(1)}, u32[]{:S(2)}, u32[]{:S(2)}) collective-permute-start(bf16[656,128]{1,0:T(8,128)(2,1)S(1)} %get-tuple-element.94), channel_id=1, source_target_pairs={{0,4},{2,6},{4,0},{6,2},{8,12},{10,14},{12,8},{14,10},{16,20},{18,... | collective-permute-start | bytes 503816 | tf_op jit(solution)/shard_map/ppermute | solution.py:469
  21.2 0.7 %collective-permute-start.7 = (bf16[656,128]{1,0:T(8,128)(2,1)S(1)}, bf16[656,128]{1,0:T(8,128)(2,1)S(1)}, u32[]{:S(2)}, u32[]{:S(2)}) collective-permute-start(bf16[656,128]{1,0:T(8,128)(2,1)S(1)} %get-tuple-element.95), channel_id=1, source_target_pairs={{0,2},{2,0},{4,6},{6,4},{8,10},{10,8},{12,14},{14,12},{16,18},{18,... | collective-permute-start | bytes 503816 | tf_op jit(solution)/shard_map/ppermute | solution.py:469
  21.9 1.0 %grad_field.1 = (bf16[36,384]{1,0:T(8,128)(2,1)S(1)}, bf16[72,384]{1,0:T(8,128)(2,1)S(1)}, bf16[36,384]{1,0:T(8,128)(2,1)S(1)}, bf16[16,128]{1,0:T(8,128)(2,1)S(1)}) custom-call(bf16[384,1152]{1,0:T(8,128)(2,1)S(1)} %get-tuple-element.62.win_ref, bf16[4,384,144]{2,1,0:T(8,128)(2,1)S(1)} %get-tuple-element.86.grad_projected_ref, ...), custom_call_target="tpu_custom_call" | custom-call | flops 100000000 | bytes 5242880 | tf_op jit(solution)/shard_map/grad_field/pallas_call | solution.py:577
  22.9 0.1 collective-permute-start.8
  23.0 0.5 %collective-permute-start.9 = (bf16[16,128]{1,0:T(8,128)(2,1)S(1)}, bf16[16,128]{1,0:T(8,128)(2,1)S(1)}, u32[]{:S(2)}, u32[]{:S(2)}) collective-permute-start(bf16[16,128]{1,0:T(8,128)(2,1)S(1)} %get-tuple-element.98.refs_0_), channel_id=1, source_target_pairs={{0,1},{1,0},{2,3},{3,2},{4,5},{5,4},{6,7},{7,6},{8,9},{9,8},{10,11... | collective-permute-start | bytes 12296 | tf_op jit(solution)/shard_map/ppermute | solution.py:469
  23.5 0.8 %collective-permute-done.9.refs_1_ = bf16[16,128]{1,0:T(8,128)(2,1)S(1)} collective-permute-done((bf16[16,128]{1,0:T(8,128)(2,1)S(1)}, bf16[16,128]{1,0:T(8,128)(2,1)S(1)}, u32[]{:S(2)}, u32[]{:S(2)}) %collective-permute-start.9) | collective-permute-done | bytes 4128 | tf_op jit(solution)/shard_map/ppermute | solution.py:469
  24.3 1.3 %collective-permute-start.4 = (bf16[72,384]{1,0:T(8,128)(2,1)S(1)}, bf16[72,384]{1,0:T(8,128)(2,1)S(1)}, u32[]{:S(2)}, u32[]{:S(2)}) collective-permute-start(bf16[72,384]{1,0:T(8,128)(2,1)S(1)} %get-tuple-element.92), channel_id=1, source_target_pairs={{0,2},{1,3},{2,4},{3,5},{4,6},{5,7},{6,8},{7,9},{8,10},{9,11},{10,... | collective-permute-start | bytes 165896 | tf_op jit(solution)/shard_map/ppermute | solution.py:465
  25.6 0.0 collective-permute-done.8.lat_ref
  25.6 0.9 %collective-permute-done.5.refs_2_ = bf16[656,128]{1,0:T(8,128)(2,1)S(1)} collective-permute-done((bf16[656,128]{1,0:T(8,128)(2,1)S(1)}, bf16[656,128]{1,0:T(8,128)(2,1)S(1)}, u32[]{:S(2)}, u32[]{:S(2)}) %collective-permute-start.5) | collective-permute-done | bytes 167968 | tf_op jit(solution)/shard_map/ppermute | solution.py:469
  26.5 2.9 %collective-permute-done.6.refs_3_ = bf16[656,128]{1,0:T(8,128)(2,1)S(1)} collective-permute-done((bf16[656,128]{1,0:T(8,128)(2,1)S(1)}, bf16[656,128]{1,0:T(8,128)(2,1)S(1)}, u32[]{:S(2)}, u32[]{:S(2)}) %collective-permute-start.6) | collective-permute-done | bytes 167968 | tf_op jit(solution)/shard_map/ppermute | solution.py:469
  29.4 0.0 collective-permute-done.7.refs_4_
  29.4 0.1 add_lon.1
  29.5 3.7 %collective-permute-start.11 = (bf16[240,128]{1,0:T(8,128)(2,1)S(1)}, bf16[240,128]{1,0:T(8,128)(2,1)S(1)}, u32[]{:S(2)}, u32[]{:S(2)}) collective-permute-start(bf16[240,128]{1,0:T(8,128)(2,1)S(1)} %get-tuple-element.105), channel_id=1, source_target_pairs={{0,24},{2,26},{4,28},{6,30},{8,16},{10,18},{12,20},{14,22},{16,8},... | collective-permute-start | bytes 184328 | tf_op jit(solution)/shard_map/ppermute | solution.py:469
  33.1 0.0 collective-permute-start.12
  33.1 0.8 %collective-permute-start.13 = (bf16[240,128]{1,0:T(8,128)(2,1)S(1)}, bf16[240,128]{1,0:T(8,128)(2,1)S(1)}, u32[]{:S(2)}, u32[]{:S(2)}) collective-permute-start(bf16[240,128]{1,0:T(8,128)(2,1)S(1)} %get-tuple-element.107), channel_id=1, source_target_pairs={{0,8},{2,10},{4,12},{6,14},{8,0},{10,2},{12,4},{14,6},{16,24},{18,... | collective-permute-start | bytes 184328 | tf_op jit(solution)/shard_map/ppermute | solution.py:469
  33.9 0.0 collective-permute-done.4.lon_ref
  33.9 0.0 collective-permute-start.10
  33.9 2.1 %collective-permute-done.11.a_ref = bf16[240,128]{1,0:T(8,128)(2,1)S(1)} collective-permute-done((bf16[240,128]{1,0:T(8,128)(2,1)S(1)}, bf16[240,128]{1,0:T(8,128)(2,1)S(1)}, u32[]{:S(2)}, u32[]{:S(2)}) %collective-permute-start.11) | collective-permute-done | bytes 61472 | tf_op jit(solution)/shard_map/ppermute | solution.py:469
  36.1 2.2 %collective-permute-done.12.b_ref = bf16[240,128]{1,0:T(8,128)(2,1)S(1)} collective-permute-done((bf16[240,128]{1,0:T(8,128)(2,1)S(1)}, bf16[240,128]{1,0:T(8,128)(2,1)S(1)}, u32[]{:S(2)}, u32[]{:S(2)}) %collective-permute-start.12) | collective-permute-done | bytes 61472 | tf_op jit(solution)/shard_map/ppermute | solution.py:469
  38.3 0.3 collective-permute-done.13.c_ref
  38.6 0.1 collective-permute-start.14
  38.7 0.7 %collective-permute-start.17 = (bf16[96,128]{1,0:T(8,128)(2,1)S(1)}, bf16[96,128]{1,0:T(8,128)(2,1)S(1)}, u32[]{:S(2)}, u32[]{:S(2)}) collective-permute-start(bf16[96,128]{1,0:T(8,128)(2,1)S(1)} %get-tuple-element.110.a_ref), channel_id=1, source_target_pairs={{0,6},{2,4},{4,2},{6,0},{8,14},{10,12},{12,10},{14,8},{16,22},{18,... | collective-permute-start | bytes 73736 | tf_op jit(solution)/shard_map/ppermute | solution.py:469
  39.5 1.6 %collective-permute-start.16 = (bf16[96,128]{1,0:T(8,128)(2,1)S(1)}, bf16[96,128]{1,0:T(8,128)(2,1)S(1)}, u32[]{:S(2)}, u32[]{:S(2)}) collective-permute-start(bf16[96,128]{1,0:T(8,128)(2,1)S(1)} %get-tuple-element.110.a_ref), channel_id=1, source_target_pairs={{0,4},{2,6},{4,0},{6,2},{8,12},{10,14},{12,8},{14,10},{16,20},{18,... | collective-permute-start | bytes 73736 | tf_op jit(solution)/shard_map/ppermute | solution.py:469
  41.1 1.2 %collective-permute-start.15 = (bf16[96,128]{1,0:T(8,128)(2,1)S(1)}, bf16[96,128]{1,0:T(8,128)(2,1)S(1)}, u32[]{:S(2)}, u32[]{:S(2)}) collective-permute-start(bf16[96,128]{1,0:T(8,128)(2,1)S(1)} %get-tuple-element.110.a_ref), channel_id=1, source_target_pairs={{0,2},{2,0},{4,6},{6,4},{8,10},{10,8},{12,14},{14,12},{16,18},{18,... | collective-permute-start | bytes 73736 | tf_op jit(solution)/shard_map/ppermute | solution.py:469
  42.3 0.0 collective-permute-done.10.diag_ref
  42.3 0.7 %unpack_quarters.1 = bf16[6,12,2,384]{3,2,1,0:T(2,128)(2,1)} custom-call(bf16[36,384]{1,0:T(8,128)(2,1)S(1)} %get-tuple-element.91.own_ref, bf16[72,384]{1,0:T(8,128)(2,1)S(1)} %collective-permute-done.4.lon_ref, bf16[36,384]{1,0:T(8,128)(2,1)S(1)} %collective-permute-done.8.lat_ref, bf16[72,384]{1,0:T(8,128)(2,1)S(1)} %collective-permute-done.10.diag_ref), custom_call_target="tpu_custom_call" | custom-call | bytes 4194304 | tf_op jit(solution)/shard_map/unpack_quarters/pallas_call | solution.py:632
  43.0 0.7 %collective-permute-done.17.d_ref = bf16[96,128]{1,0:T(8,128)(2,1)S(1)} collective-permute-done((bf16[96,128]{1,0:T(8,128)(2,1)S(1)}, bf16[96,128]{1,0:T(8,128)(2,1)S(1)}, u32[]{:S(2)}, u32[]{:S(2)}) %collective-permute-start.17) | collective-permute-done | bytes 24608 | tf_op jit(solution)/shard_map/ppermute | solution.py:469
  43.6 0.0 collective-permute-done.16.c_ref
  43.6 1.3 %collective-permute-done.15.b_ref = bf16[96,128]{1,0:T(8,128)(2,1)S(1)} collective-permute-done((bf16[96,128]{1,0:T(8,128)(2,1)S(1)}, bf16[96,128]{1,0:T(8,128)(2,1)S(1)}, u32[]{:S(2)}, u32[]{:S(2)}) %collective-permute-start.15) | collective-permute-done | bytes 24608 | tf_op jit(solution)/shard_map/ppermute | solution.py:469
  44.9 0.0 collective-permute-done.14.other_weights_ref
  44.9 0.8 %finish.1 = (bf16[24,1152]{1,0:T(8,128)(2,1)}, bf16[24,384]{1,0:T(8,128)(2,1)}, f32[12,1,3312]{2,1,0:T(1,128)}, f32[384]{0:T(512)}) custom-call(bf16[144,128]{1,0:T(8,128)(2,1)S(1)} %get-tuple-element.109.weights_ref, bf16[144,128]{1,0:T(8,128)(2,1)S(1)} %collective-permute-done.14.other_weights_ref, bf16[96,128]{1,0:T(8,128)(2,1)S(1)} %get-tuple-element.110.a_ref, ...), custom_call_target="tpu_custom_call" | custom-call | bytes 524288 | tf_op jit(solution)/shard_map/finish/pallas_call | solution.py:616
  (1 shorter events, 0.0 us)
Async XLA Ops:
  1.8 10.8 %collective-permute-start = (bf16[72,384]{1,0:T(8,128)(2,1)S(1)}, bf16[72,384]{1,0:T(8,128)(2,1)S(1)}, u32[]{:S(2)}, u32[]{:S(2)}) collective-permute-start(bf16[72,384]{1,0:T(8,128)(2,1)S(1)} %get-tuple-element.64), channel_id=1, source_target_pairs={{0,30},{1,31},{2,0},{3,1},{4,2},{5,3},{6,4},{7,5},{8,6},{9,7},{10,... | collective-permute-start | bytes 165896 | tf_op jit(solution)/shard_map/ppermute | solution.py:465
  8.8 3.8 %collective-permute-start.1 = (bf16[72,384]{1,0:T(8,128)(2,1)S(1)}, bf16[72,384]{1,0:T(8,128)(2,1)S(1)}, u32[]{:S(2)}, u32[]{:S(2)}) collective-permute-start(bf16[72,384]{1,0:T(8,128)(2,1)S(1)} %get-tuple-element.65), channel_id=1, source_target_pairs={{0,1},{1,0},{2,3},{3,2},{4,5},{5,4},{6,7},{7,6},{8,9},{9,8},{10,11... | collective-permute-start | bytes 165896 | tf_op jit(solution)/shard_map/ppermute | solution.py:465
  8.8 3.8 %collective-permute-start.2 = (bf16[72,384]{1,0:T(8,128)(2,1)S(1)}, bf16[72,384]{1,0:T(8,128)(2,1)S(1)}, u32[]{:S(2)}, u32[]{:S(2)}) collective-permute-start(bf16[72,384]{1,0:T(8,128)(2,1)S(1)} %get-tuple-element.66), channel_id=1, source_target_pairs={{0,31},{1,30},{2,1},{3,0},{4,3},{5,2},{6,5},{7,4},{8,7},{9,6},{10,... | collective-permute-start | bytes 165896 | tf_op jit(solution)/shard_map/ppermute | solution.py:465
  16.0 2.2 %collective-permute-start.3 = (bf16[2304,128]{1,0:T(8,128)(2,1)S(1)}, bf16[2304,128]{1,0:T(8,128)(2,1)S(1)}, u32[]{:S(2)}, u32[]{:S(2)}) collective-permute-start(bf16[2304,128]{1,0:T(8,128)(2,1)S(1)} %get-tuple-element.74), channel_id=1, source_target_pairs={{0,1},{1,0},{2,3},{3,2},{4,5},{5,4},{6,7},{7,6},{8,9},{9,8},{10,11... | collective-permute-start | bytes 1769480 | tf_op jit(solution)/shard_map/ppermute | solution.py:469
  18.4 8.1 %collective-permute-start.5 = (bf16[656,128]{1,0:T(8,128)(2,1)S(1)}, bf16[656,128]{1,0:T(8,128)(2,1)S(1)}, u32[]{:S(2)}, u32[]{:S(2)}) collective-permute-start(bf16[656,128]{1,0:T(8,128)(2,1)S(1)} %get-tuple-element.93), channel_id=1, source_target_pairs={{0,6},{2,4},{4,2},{6,0},{8,14},{10,12},{12,10},{14,8},{16,22},{18,... | collective-permute-start | bytes 503816 | tf_op jit(solution)/shard_map/ppermute | solution.py:469
  18.4 10.9 %collective-permute-start.6 = (bf16[656,128]{1,0:T(8,128)(2,1)S(1)}, bf16[656,128]{1,0:T(8,128)(2,1)S(1)}, u32[]{:S(2)}, u32[]{:S(2)}) collective-permute-start(bf16[656,128]{1,0:T(8,128)(2,1)S(1)} %get-tuple-element.94), channel_id=1, source_target_pairs={{0,4},{2,6},{4,0},{6,2},{8,12},{10,14},{12,8},{14,10},{16,20},{18,... | collective-permute-start | bytes 503816 | tf_op jit(solution)/shard_map/ppermute | solution.py:469
  21.2 8.2 %collective-permute-start.7 = (bf16[656,128]{1,0:T(8,128)(2,1)S(1)}, bf16[656,128]{1,0:T(8,128)(2,1)S(1)}, u32[]{:S(2)}, u32[]{:S(2)}) collective-permute-start(bf16[656,128]{1,0:T(8,128)(2,1)S(1)} %get-tuple-element.95), channel_id=1, source_target_pairs={{0,2},{2,0},{4,6},{6,4},{8,10},{10,8},{12,14},{14,12},{16,18},{18,... | collective-permute-start | bytes 503816 | tf_op jit(solution)/shard_map/ppermute | solution.py:469
  22.9 2.7 %collective-permute-start.8 = (bf16[36,384]{1,0:T(8,128)(2,1)S(1)}, bf16[36,384]{1,0:T(8,128)(2,1)S(1)}, u32[]{:S(2)}, u32[]{:S(2)}) collective-permute-start(bf16[36,384]{1,0:T(8,128)(2,1)S(1)} %get-tuple-element.97), channel_id=1, source_target_pairs={{0,1},{1,0},{2,3},{3,2},{4,5},{5,4},{6,7},{7,6},{8,9},{9,8},{10,11... | collective-permute-start | bytes 82952 | tf_op jit(solution)/shard_map/ppermute | solution.py:465
  23.0 1.3 %collective-permute-start.9 = (bf16[16,128]{1,0:T(8,128)(2,1)S(1)}, bf16[16,128]{1,0:T(8,128)(2,1)S(1)}, u32[]{:S(2)}, u32[]{:S(2)}) collective-permute-start(bf16[16,128]{1,0:T(8,128)(2,1)S(1)} %get-tuple-element.98.refs_0_), channel_id=1, source_target_pairs={{0,1},{1,0},{2,3},{3,2},{4,5},{5,4},{6,7},{7,6},{8,9},{9,8},{10,11... | collective-permute-start | bytes 12296 | tf_op jit(solution)/shard_map/ppermute | solution.py:469
  24.3 9.6 %collective-permute-start.4 = (bf16[72,384]{1,0:T(8,128)(2,1)S(1)}, bf16[72,384]{1,0:T(8,128)(2,1)S(1)}, u32[]{:S(2)}, u32[]{:S(2)}) collective-permute-start(bf16[72,384]{1,0:T(8,128)(2,1)S(1)} %get-tuple-element.92), channel_id=1, source_target_pairs={{0,2},{1,3},{2,4},{3,5},{4,6},{5,7},{6,8},{7,9},{8,10},{9,11},{10,... | collective-permute-start | bytes 165896 | tf_op jit(solution)/shard_map/ppermute | solution.py:465
  29.5 6.6 %collective-permute-start.11 = (bf16[240,128]{1,0:T(8,128)(2,1)S(1)}, bf16[240,128]{1,0:T(8,128)(2,1)S(1)}, u32[]{:S(2)}, u32[]{:S(2)}) collective-permute-start(bf16[240,128]{1,0:T(8,128)(2,1)S(1)} %get-tuple-element.105), channel_id=1, source_target_pairs={{0,24},{2,26},{4,28},{6,30},{8,16},{10,18},{12,20},{14,22},{16,8},... | collective-permute-start | bytes 184328 | tf_op jit(solution)/shard_map/ppermute | solution.py:469
  33.1 5.2 %collective-permute-start.12 = (bf16[240,128]{1,0:T(8,128)(2,1)S(1)}, bf16[240,128]{1,0:T(8,128)(2,1)S(1)}, u32[]{:S(2)}, u32[]{:S(2)}) collective-permute-start(bf16[240,128]{1,0:T(8,128)(2,1)S(1)} %get-tuple-element.106), channel_id=1, source_target_pairs={{0,16},{2,18},{4,20},{6,22},{8,24},{10,26},{12,28},{14,30},{16,0},... | collective-permute-start | bytes 184328 | tf_op jit(solution)/shard_map/ppermute | solution.py:469
  33.1 5.5 %collective-permute-start.13 = (bf16[240,128]{1,0:T(8,128)(2,1)S(1)}, bf16[240,128]{1,0:T(8,128)(2,1)S(1)}, u32[]{:S(2)}, u32[]{:S(2)}) collective-permute-start(bf16[240,128]{1,0:T(8,128)(2,1)S(1)} %get-tuple-element.107), channel_id=1, source_target_pairs={{0,8},{2,10},{4,12},{6,14},{8,0},{10,2},{12,4},{14,6},{16,24},{18,... | collective-permute-start | bytes 184328 | tf_op jit(solution)/shard_map/ppermute | solution.py:469
  33.9 8.3 %collective-permute-start.10 = (bf16[72,384]{1,0:T(8,128)(2,1)S(1)}, bf16[72,384]{1,0:T(8,128)(2,1)S(1)}, u32[]{:S(2)}, u32[]{:S(2)}) collective-permute-start(bf16[72,384]{1,0:T(8,128)(2,1)S(1)} %collective-permute-done.4.lon_ref), channel_id=1, source_target_pairs={{0,1},{1,0},{2,3},{3,2},{4,5},{5,4},{6,7},{7,6},{8,9},{9,8},{10,11... | collective-permute-start | bytes 165896 | tf_op jit(solution)/shard_map/ppermute | solution.py:465
  38.6 6.3 %collective-permute-start.14 = (bf16[144,128]{1,0:T(8,128)(2,1)S(1)}, bf16[144,128]{1,0:T(8,128)(2,1)S(1)}, u32[]{:S(2)}, u32[]{:S(2)}) collective-permute-start(bf16[144,128]{1,0:T(8,128)(2,1)S(1)} %get-tuple-element.109.weights_ref), channel_id=1, source_target_pairs={{0,1},{1,0},{2,3},{3,2},{4,5},{5,4},{6,7},{7,6},{8,9},{9,8},{10,11... | collective-permute-start | bytes 110600 | tf_op jit(solution)/shard_map/ppermute | solution.py:469
  38.7 4.9 %collective-permute-start.17 = (bf16[96,128]{1,0:T(8,128)(2,1)S(1)}, bf16[96,128]{1,0:T(8,128)(2,1)S(1)}, u32[]{:S(2)}, u32[]{:S(2)}) collective-permute-start(bf16[96,128]{1,0:T(8,128)(2,1)S(1)} %get-tuple-element.110.a_ref), channel_id=1, source_target_pairs={{0,6},{2,4},{4,2},{6,0},{8,14},{10,12},{12,10},{14,8},{16,22},{18,... | collective-permute-start | bytes 73736 | tf_op jit(solution)/shard_map/ppermute | solution.py:469
  39.5 4.1 %collective-permute-start.16 = (bf16[96,128]{1,0:T(8,128)(2,1)S(1)}, bf16[96,128]{1,0:T(8,128)(2,1)S(1)}, u32[]{:S(2)}, u32[]{:S(2)}) collective-permute-start(bf16[96,128]{1,0:T(8,128)(2,1)S(1)} %get-tuple-element.110.a_ref), channel_id=1, source_target_pairs={{0,4},{2,6},{4,0},{6,2},{8,12},{10,14},{12,8},{14,10},{16,20},{18,... | collective-permute-start | bytes 73736 | tf_op jit(solution)/shard_map/ppermute | solution.py:469
  41.1 3.8 %collective-permute-start.15 = (bf16[96,128]{1,0:T(8,128)(2,1)S(1)}, bf16[96,128]{1,0:T(8,128)(2,1)S(1)}, u32[]{:S(2)}, u32[]{:S(2)}) collective-permute-start(bf16[96,128]{1,0:T(8,128)(2,1)S(1)} %get-tuple-element.110.a_ref), channel_id=1, source_target_pairs={{0,2},{2,0},{4,6},{6,4},{8,10},{10,8},{12,14},{14,12},{16,18},{18,... | collective-permute-start | bytes 73736 | tf_op jit(solution)/shard_map/ppermute | solution.py:469

commit v3 on v2

--- a/solution.py
+++ b/solution.py
@@ -69,21 +69,65 @@
     return copies
 
 
-def load_kernel(field_src, cot_src, *refs):
-    sources, out_refs, targets, (field_ref, cot_ref, sems) = refs[:3], refs[3:7], refs[7:10], refs[10:]
-    copies = fetch((field_src, cot_src) + sources, (field_ref, cot_ref) + targets, sems)
-    for copy in copies[:2]:
+class Route:
+    def __init__(self, lon_count, lat_count):
+        self.lon_count, self.lat_count = lon_count, lat_count
+        self.middle = lon_count // 2
+        middle, last = self.middle, lon_count - 1
+        self.near = [(lon + 1, lon) for lon in range(middle)] + [(0, middle)]
+        self.near += [(lon - 1, lon) for lon in range(middle + 2, lon_count)]
+        self.joint = [(middle, middle + 1), (last, middle)]
+
+    def move(self, value, pairs, lat_step):
+        count = self.lat_count
+        pairs = [(src * count + lat, dst * count + (lat + lat_step) % count) for src, dst in pairs for lat in range(count)]
+        return lax.ppermute(value, ("lon", "lat"), pairs)
+
+    def west(self, own, near, joint, joint_at):
+        lon = lax.axis_index("lon")
+        by_joint = (lon == self.middle) | (lon == joint_at)
+        return jnp.where(lon < self.middle, own, jnp.where(by_joint, joint, near))
+
+    def east(self, own, near):
+        return jnp.where(lax.axis_index("lon") <= self.middle, near, own)
+
+
+SAME = 80
+
+
+def load_kernel(route, field_src, cot_src, *refs):
+    sources, out_refs, (table_ref, gain_ref) = refs[:3], refs[3:9], refs[9:11]
+    field_ref, cot_ref, regions_ref, sems = refs[11:]
+    copies = fetch((field_src, cot_src) + sources, (field_ref, cot_ref, regions_ref, table_ref, gain_ref), sems)
+    for copy in copies[:3]:
         copy.wait()
     half_rows, half_cols = WIN_LAT // 2, WIN_LON // 2
-    for (lat_half, lon_half), out_ref in zip(QUARTERS, out_refs):
-        first_row, first_col = (1 - lat_half) * half_rows, (1 - lon_half) * half_cols
-        pieces = []
-        for ref in (field_ref, cot_ref):
-            for row in range(half_rows):
-                for col in range(half_cols):
-                    pieces.append(ref[first_row + row, first_col + col].astype(f32))
+    features = field_ref.shape[3]
+    lon = lax.axis_index("lon")
+    own_col = jnp.where(lon < route.middle, half_cols, 0)
+    far_col = jnp.where(lon <= route.middle, 0, half_cols)
+    ids = [regions_ref[row, level : level + 1, :].astype(f32) for level in range(LEV) for row in range(WIN_LAT)]
+    ids.append(jnp.zeros((1, features - CELLS), f32))
+    tail = jnp.concatenate([jnp.concatenate(ids, axis=1), jnp.zeros((SAME - 2 * QUARTER - 1, features), f32)], axis=0)
+    wanted = (
+        (half_rows, own_col),
+        (half_rows, far_col),
+        (0, far_col),
+        (0, own_col),
+        (half_rows, half_cols),
+        (0, half_cols),
+    )
+    for (first_row, first_col), out_ref in zip(wanted, out_refs):
+        pieces = [
+            ref[first_row + row, first_col + col].astype(f32)
+            for ref in (field_ref, cot_ref)
+            for row in range(half_rows)
+            for col in range(half_cols)
+        ]
+        if out_ref.shape[0] == SAME:
+            pieces.append(tail)
         out_ref[...] = jnp.concatenate(pieces, axis=0).astype(bf16)
-    for copy in copies[2:]:
+    for copy in copies[3:]:
         copy.wait()
 
 
@@ -103,12 +147,21 @@
     return quarter * stride + place * LEV + lax.rem(level + LEV // 2, LEV)
 
 
-def unpack_kernel(own_ref, lon_ref, lat_ref, diag_ref, out_ref):
+def unpack_kernel(route, own_ref, near_ref, joint_ref, lat_ref, near_diag_ref, joint_diag_ref, out_ref):
     half_rows, half_cols = WIN_LAT // 2, WIN_LON // 2
-    sources = ((own_ref, 0), (lon_ref, 0), (lat_ref, 0), (diag_ref, QUARTER))
-    for (lat_half, lon_half), (ref, start) in zip(QUARTERS, sources):
+    last = route.lon_count - 1
+    own, lat = own_ref[...].astype(f32), lat_ref[...].astype(f32)
+    near, joint = near_ref[...].astype(f32)[:QUARTER], joint_ref[...].astype(f32)[:QUARTER]
+    near_diag = near_diag_ref[...].astype(f32)[QUARTER:]
+    joint_diag = joint_diag_ref[...].astype(f32)[QUARTER:]
+    quarters = (
+        route.west(own, near, joint, last),
+        route.east(own, near),
+        route.west(lat, near_diag, joint_diag, last),
+        route.east(lat, near_diag),
+    )
+    for (lat_half, lon_half), cells in zip(QUARTERS, quarters):
         first_row, first_col = (1 - lat_half) * half_rows, (1 - lon_half) * half_cols
-        cells = ref[...].astype(f32)[start : start + QUARTER]
         for row in range(half_rows):
             for col in range(half_cols):
                 first = (row * half_cols + col) * LEV
@@ -117,7 +170,6 @@
 
 def bias_kernel(
     table_ref,
-    regions_ref,
     win_src,
     wout_src,
     out_ref,
@@ -160,22 +212,13 @@
     moved = nn_dot(stage[...].astype(bf16), lanes_ref[...]).astype(bf16)
     rows = nn_dot(rows_ref[...], moved)
 
-    region_rows = [regions_ref[row, level : level + 1, :] for level in range(LEV) for row in range(WIN_LAT)]
-    region_grid = jnp.concatenate(region_rows, axis=0).astype(f32).astype(bf16)
-    cell, lane = counted((CELLS, PLANE), 0), counted((CELLS, PLANE), 1)
-    by_plane = nn_dot(one_hot(lax.rem(cell, PLANE) == lane), region_grid)
-    region_col = jnp.sum(jnp.where(lax.div(cell, PLANE) == lane, by_plane, 0.0), axis=1, keepdims=True)
-    across = counted((CELLS, CELLS), 0) == counted((CELLS, CELLS), 1)
-    region_row = jnp.sum(jnp.where(across, region_col, 0.0), axis=0, keepdims=True)
-    same = region_col == region_row
-
     for col in range(WIN_LON):
         shift = PLANE * (WIN_LON - 1 - col)
         moved = rows if shift == 0 else pltpu.roll(rows, WIDE - shift, 1)
         for head in range(HEADS):
             full[head, PLANE * col : PLANE * (col + 1), :] = moved[16 * head : 16 * head + PLANE, :CELLS]
     for head in range(HEADS):
-        out_ref[head] = jnp.where(same, full[head], masked_score).astype(bf16)
+        out_ref[head] = full[head].astype(bf16)
     for copy in copies:
         copy.wait()
     for block in range(3):
@@ -184,11 +227,14 @@
 
 
 def window_kernel(
+    route,
     packet,
     own_ref,
-    lon_ref,
+    near_ref,
+    near_diag_ref,
     lat_ref,
-    diag_ref,
+    joint_ref,
+    joint_diag_ref,
     gain_ref,
     win_ref,
     win_t_ref,
@@ -209,9 +255,23 @@
     head_dim = features // HEADS
     group_heads = LANES // head_dim
     score_scale = head_dim ** (-0.5)
-    quarters = (own_ref, lon_ref, lat_ref, diag_ref)
     eye = eye_ref[...]
-    stacked = jnp.concatenate([ref[...].astype(f32) for ref in quarters], axis=0).astype(bf16)
+    messages = (own_ref, near_ref, near_diag_ref, lat_ref, joint_ref, joint_diag_ref)
+    own, near, near_diag, lat, joint, joint_diag = [ref[...].astype(f32) for ref in messages]
+    west = route.west(own, near, joint, route.middle + 1)
+    quarters = [
+        west[: 2 * QUARTER],
+        route.east(own, near)[: 2 * QUARTER],
+        route.west(lat, near_diag, joint_diag, route.middle + 1),
+        route.east(lat, near_diag),
+    ]
+    stacked = jnp.concatenate(quarters, axis=0).astype(bf16)
+    cell, lane = counted((CELLS, CELLS), 0), counted((CELLS, CELLS), 1)
+    source = lax.rem(cell, PLANE) * WIN_LON + lax.div(cell, PLANE)
+    ids = west[2 * QUARTER : 2 * QUARTER + 1, :CELLS]
+    region_col = jnp.sum(jnp.where(source == lane, ids, 0.0), axis=1, keepdims=True)
+    region_row = jnp.sum(jnp.where(cell == lane, region_col, 0.0), axis=0, keepdims=True)
+    same = region_col == region_row
     placed = nn_dot(place_ref[...], stacked)
     field = placed[:CELLS]
     cot = placed[CELLS:].astype(bf16)
@@ -254,7 +314,7 @@
         return scores, nn_dot(values, spread(grad_att_t[rows_of(head)], slot))
 
     def softmax_of(head, scores, grad_probs):
-        scores = scores * score_scale + bias_ref[head].astype(f32)
+        scores = jnp.where(same, scores * score_scale + bias_ref[head].astype(f32), masked_score)
         grown = jnp.exp(scores - jnp.max(scores, axis=0, keepdims=True))
         probs = grown * (1.0 / jnp.sum(grown, axis=0, keepdims=True))
         weighted = probs * grad_probs
@@ -295,6 +355,7 @@
 
 
 def field_kernel(
+    route,
     win_ref,
     grad_projected_ref,
     normalized_ref,
@@ -304,7 +365,8 @@
     place_t_ref,
     eye_ref,
     back_own_ref,
-    back_lon_ref,
+    back_near_ref,
+    back_joint_ref,
     back_lat_ref,
     gain_out_ref,
 ):
@@ -322,9 +384,13 @@
     )
     back = nn_dot(place_t_ref[...], grad_field.astype(bf16))
     quarters = [back[quarter * QUARTER : (quarter + 1) * QUARTER] for quarter in range(4)]
-    back_own_ref[...] = quarters[0].astype(bf16)
-    back_lon_ref[...] = jnp.concatenate([quarters[1], quarters[3]], axis=0).astype(bf16)
-    back_lat_ref[...] = quarters[2].astype(bf16)
+    west, east = jnp.concatenate(quarters[::2], axis=0), jnp.concatenate(quarters[1::2], axis=0)
+    lon = lax.axis_index("lon")
+    kept = jnp.where(lon < route.middle, west, east)
+    back_own_ref[...] = kept[:QUARTER].astype(bf16)
+    back_near_ref[...] = jnp.where(lon <= route.middle, east, west).astype(bf16)
+    back_joint_ref[...] = west.astype(bf16)
+    back_lat_ref[...] = kept[QUARTER:].astype(bf16)
     gain_sum = jnp.sum(grad_normed * normalized, axis=0, keepdims=True)
     gain_rows = [gain_sum[:, tile * LANES : (tile + 1) * LANES] for tile in range(3)]
     gain_out_ref[...] = jnp.concatenate(gain_rows + [jnp.zeros((13, LANES), f32)], axis=0).astype(bf16)
@@ -456,13 +522,9 @@
     head_dim = features // HEADS
     packet = Packet(lon_count, features)
 
-    def move(value, lon_step, lat_step):
-        pairs = []
-        for lon in range(lon_count):
-            for lat in range(lat_count):
-                target = ((lon + lon_step) % lon_count) * lat_count + (lat + lat_step) % lat_count
-                pairs.append((lon * lat_count + lat, target))
-        return lax.ppermute(value, ("lon", "lat"), pairs)
+    route = Route(lon_count, lat_count)
+    everyone = [(lon, lon) for lon in range(lon_count)]
+    backward, joint_backward = [[(dst, src) for src, dst in pairs] for pairs in (route.near, route.joint)]
 
     def swap(value, axis, mask):
         count = lon_count if axis == "lon" else lat_count
@@ -477,23 +539,26 @@
 
     hbm = pl.BlockSpec(memory_space=pltpu.HBM)
     field, cot = jnp.transpose(latent_field, (1, 2, 0, 3)), jnp.transpose(cotangent, (1, 2, 0, 3))
-    small = (bias_table[0], jnp.transpose(regions, (1, 0, 2)), norm_gain)
-    own, to_lon, to_lat, to_diag, table, region_grid, gain = call(
-        load_kernel,
+    small = (jnp.transpose(regions, (1, 0, 2)), bias_table[0], norm_gain)
+    same, others = struct((SAME, features), bf16), struct((2 * QUARTER, features), bf16)
+    own, far, far_others, to_lat, west, west_others, table, gain = call(
+        functools.partial(load_kernel, route),
         "load",
         [hbm] * 5,
-        [struct((2 * QUARTER, features), bf16)] * 4 + [struct(array.shape, array.dtype) for array in small],
-        [space_for(field), space_for(cot), pltpu.SemaphoreType.DMA((5,))],
+        [same, same, others, others, same, others] + [struct(array.shape, array.dtype) for array in small[1:]],
+        [space_for(field), space_for(cot), space_for(small[0]), pltpu.SemaphoreType.DMA((5,))],
         moved=1 << 20,
     )(*in_hbm(field, cot, *small))
-    from_lon = move(to_lon, -1, 0)
-    from_diag = move(to_diag, -1, -1)
-    from_lat = move(to_lat, 0, -1)
+    from_near = route.move(far, route.near, 0)
+    from_near_diag = route.move(far_others, route.near, -1)
+    from_joint = route.move(west, route.joint, 0)
+    from_joint_diag = route.move(west_others, route.joint, -1)
+    from_lat = route.move(to_lat, everyone, -1)
 
     bias_full, input_weight_t, lane_moves, row_moves, eye, place, place_t, weight_in, weight_out = call(
         bias_kernel,
         "expand_bias",
-        whole(2) + [hbm] * 2,
+        whole(1) + [hbm] * 2,
         [
             struct((HEADS, CELLS, CELLS), bf16),
             struct((3 * features, features), bf16),
@@ -511,13 +576,13 @@
             pltpu.SemaphoreType.DMA((2,)),
         ],
         moved=1 << 21,
-    )(table, region_grid, *in_hbm(input_weight, output_weight))
+    )(table, *in_hbm(input_weight, output_weight))
 
     half_sum = struct((lon_count * packet.weight_size, LANES), bf16)
     results = call(
-        functools.partial(window_kernel, packet),
+        functools.partial(window_kernel, route, packet),
         "window",
-        whole(11),
+        whole(13),
         [
             half_sum,
             half_sum,
@@ -532,9 +597,11 @@
         moved=5 << 20,
     )(
             own,
-        from_lon,
+        from_near,
+        from_near_diag,
         from_lat,
-        from_diag,
+        from_joint,
+        from_joint_diag,
         gain,
         weight_in,
         input_weight_t,
@@ -574,20 +641,22 @@
 
     held = trade(parts, 0)
     piece = struct((QUARTER, features), bf16)
-    back_own, back_lon, back_lat, gain_part = call(
-        field_kernel,
+    back_own, back_near, back_joint, back_lat, gain_part = call(
+        functools.partial(field_kernel, route),
         "grad_field",
         whole(8),
-        [piece, struct((2 * QUARTER, features), bf16), piece, struct((16, LANES), bf16)],
+        [piece, others, others, piece, struct((16, LANES), bf16)],
         flops=10**8,
         moved=5 << 20,
     )(weight_in, *saved, gain, place_t, eye)
-    home_lat = move(back_lat, 0, 1)
+    home_lat = route.move(back_lat, everyone, 1)
     gain_other = swap(gain_part, "lat", 1)
     held, home_lat, gain_other = lax.optimization_barrier((held, home_lat, gain_other))
     gains = [gain_part, gain_other]
-    home_lon = move(back_lon, 1, 0)
-    home_diag = move(home_lon, 0, 1)
+    home_near = route.move(back_near, backward, 0)
+    home_joint = route.move(back_joint, joint_backward, 0)
+    home_near_diag = route.move(home_near, everyone, 1)
+    home_joint_diag = route.move(home_joint, everyone, 1)
     for shift in range(2, lon_count.bit_length() - 1, 2):
         groups //= 4
         parts = call(
@@ -630,8 +699,12 @@
         gain_sum = gain_sum + swap(gain_sum, "lat", 1 << bit)
 
     grad_field = call(
-        unpack_kernel, "unpack_quarters", whole(4), struct((WIN_LAT, WIN_LON, LEV, features), bf16), moved=4 << 20
-    )(back_own, home_lon, home_lat, home_diag)
+        functools.partial(unpack_kernel, route),
+        "unpack_quarters",
+        whole(6),
+        struct((WIN_LAT, WIN_LON, LEV, features), bf16),
+        moved=4 << 20,
+    )(back_own, home_near, home_joint, home_lat, home_near_diag, home_joint_diag)
     return (
         jnp.transpose(grad_field, (2, 0, 1, 3)),
         grad_input_weight,

time: 45.9 us -> 51.9 us (1.13)
  starting transfers between devices: 21.4 us -> 29.6 us
  waiting for transfers between devices: 11.2 us -> 9.14 us
    ppermute x6 -> x10, starting transfers between devices: 9.02 us -> 17.2 us  [move(): return lax.ppermute(value, ('lon', 'lat'), pairs)]
    ppermute x12, waiting for transfers between devices: 11.2 us -> 9.11 us  [swap(): lax.ppermute(value, axis, [(source, source ^ mask) for source in range(co...]
  transfers between devices with their start and end apart: 18 -> 22, of which waited for: 8 -> 8; matrix products, arithmetic and copies ran while one was open for 0% -> 0% of each run, Pallas kernels for 15% -> 12%
where the time goes in v3:
time: 51.9 us; the launch traced here: 51.6 us
  starting transfers between devices  29.6 us (57%)
  Pallas kernels  12.1 us (23%)
  waiting for transfers between devices  9.14 us (18%)
  between operations  0.83 us (2%)
    ppermute x10, starting transfers between devices, move(): return lax.ppermute(value, ('lon', 'lat'), pairs)  17.2 us
    ppermute x12, starting transfers between devices, swap(): lax.ppermute(value, axis, [(source, source ^ mask) for source in range(co...  12.5 us
    ppermute x12, waiting for transfers between devices, swap(): lax.ppermute(value, axis, [(source, source ^ mask) for source in range(co...  9.11 us
    pallas_call x1, Pallas kernels, on_device(): call(functools.partial(window_kernel, route, packet), 'window', whole(13)...  3.5 us
    pallas_call x1, Pallas kernels, on_device(): call(bias_kernel, 'expand_bias', whole(1) + [hbm] * 2, [struct((HEADS, CE...  2.63 us
    pallas_call x1, Pallas kernels, on_device(): call(functools.partial(fold_kernel, packet), 'fold_table', whole(3), stru...  1.91 us
    pallas_call x1, Pallas kernels, on_device(): call(functools.partial(load_kernel, route), 'load', [hbm] * 5, [same, sam...  1.27 us
  transfers between devices with their start and end apart: 22, of which 8 were waited for; matrix products, arithmetic and copies ran while one was open for 0% of the time, Pallas kernels for 12%

profile of v3, /device:TPU:0, one launch (start us, length us, event | category | flops | bytes accessed | tf_op | source)
XLA Modules:
  0.0 51.6 jit_solution(16371614178499166055)
XLA Ops:
  0.6 1.3 %load.1 = (bf16[80,384]{1,0:T(8,128)(2,1)S(1)}, bf16[80,384]{1,0:T(8,128)(2,1)S(1)}, bf16[72,384]{1,0:T(8,128)(2,1)S(1)}, bf16[72,384]{1,0:T(8,128)(2,1)S(1)}, b...) custom-call(bf16[6,12,2,384]{3,2,1,0:T(2,128)(2,1)} %bitcast.7, ...), custom_call_target="tpu_custom_call" | custom-call | bytes 1048576 | tf_op jit(solution)/shard_map/load/pallas_call | solution.py:544
  1.9 5.9 %collective-permute-start = (bf16[80,384]{1,0:T(8,128)(2,1)S(1)}, bf16[80,384]{1,0:T(8,128)(2,1)S(1)}, u32[]{:S(2)}, u32[]{:S(2)}) collective-permute-start(bf16[80,384]{1,0:T(8,128)(2,1)S(1)} %get-tuple-element.65), channel_id=1, source_target_pairs={{2,0},{3,1},{4,2},{5,3},{6,4},{7,5},{8,6},{9,7},{10,8},{11,9},{12,... | collective-permute-start | bytes 184328 | tf_op jit(solution)/shard_map/ppermute | solution.py:84
  7.9 0.7 %collective-permute-start.3 = (bf16[80,384]{1,0:T(8,128)(2,1)S(1)}, bf16[80,384]{1,0:T(8,128)(2,1)S(1)}, u32[]{:S(2)}, u32[]{:S(2)}) collective-permute-start(bf16[80,384]{1,0:T(8,128)(2,1)S(1)} %get-tuple-element.68), channel_id=1, source_target_pairs={{16,18},{17,19},{30,16},{31,17}} | collective-permute-start | bytes 184328 | tf_op jit(solution)/shard_map/ppermute | solution.py:84
  8.5 5.0 %collective-permute-start.1 = (bf16[72,384]{1,0:T(8,128)(2,1)S(1)}, bf16[72,384]{1,0:T(8,128)(2,1)S(1)}, u32[]{:S(2)}, u32[]{:S(2)}) collective-permute-start(bf16[72,384]{1,0:T(8,128)(2,1)S(1)} %get-tuple-element.66), channel_id=1, source_target_pairs={{2,1},{3,0},{4,3},{5,2},{6,5},{7,4},{8,7},{9,6},{10,9},{11,8},{12,... | collective-permute-start | bytes 165896 | tf_op jit(solution)/shard_map/ppermute | solution.py:84
  13.6 1.3 %collective-permute-start.2 = (bf16[72,384]{1,0:T(8,128)(2,1)S(1)}, bf16[72,384]{1,0:T(8,128)(2,1)S(1)}, u32[]{:S(2)}, u32[]{:S(2)}) collective-permute-start(bf16[72,384]{1,0:T(8,128)(2,1)S(1)} %get-tuple-element.67), channel_id=1, source_target_pairs={{0,1},{1,0},{2,3},{3,2},{4,5},{5,4},{6,7},{7,6},{8,9},{9,8},{10,11... | collective-permute-start | bytes 165896 | tf_op jit(solution)/shard_map/ppermute | solution.py:84
  14.9 0.7 %collective-permute-start.4 = (bf16[72,384]{1,0:T(8,128)(2,1)S(1)}, bf16[72,384]{1,0:T(8,128)(2,1)S(1)}, u32[]{:S(2)}, u32[]{:S(2)}) collective-permute-start(bf16[72,384]{1,0:T(8,128)(2,1)S(1)} %get-tuple-element.69), channel_id=1, source_target_pairs={{16,19},{17,18},{30,17},{31,16}} | collective-permute-start | bytes 165896 | tf_op jit(solution)/shard_map/ppermute | solution.py:84
  15.5 2.6 %expand_bias.1 = (bf16[12,144,144]{2,1,0:T(8,128)(2,1)S(1)}, bf16[1152,384]{1,0:T(8,128)(2,1)S(1)}, bf16[384,384]{1,0:T(8,128)(2,1)S(1)}, bf16[192,192]{1,0:T(8,...) custom-call(bf16[12,3312]{1,0:T(8,128)(2,1)S(1)} %get-tuple-element., ...), custom_call_target="tpu_custom_call" | custom-call | bytes 2097152 | tf_op jit(solution)/shard_map/expand_bias/pallas_call | solution.py:558
  18.2 0.0 collective-permute-done.1.near_diag_ref
  18.2 0.0 collective-permute-done.2.lat_ref
  18.2 0.0 collective-permute-done.4.joint_diag_ref
  18.2 0.0 collective-permute-done.near_ref
  18.2 0.0 collective-permute-done.3.joint_ref
  18.2 3.5 %window.1 = (bf16[2304,128]{1,0:T(8,128)(2,1)S(1)}, bf16[2304,128]{1,0:T(8,128)(2,1)S(1)}, bf16[12,144,144]{2,1,0:T(8,128)(2,1)S(1)}, bf16[4,384,144]{2,1,0:T(8,...) custom-call(bf16[80,384]{1,0:T(8,128)(2,1)S(1)} %get-tuple-element.64.own_ref, ...), custom_call_target="tpu_custom_call" | custom-call | flops 1000000000 | bytes 5242880 | tf_op jit(solution)/shard_map/window/pallas_call | solution.py:582
  21.7 0.1 collective-permute-start.5
  21.8 1.9 %fold_table.1.table_ref = bf16[320,128]{1,0:T(8,128)(2,1)S(1)} custom-call(bf16[12,144,144]{2,1,0:T(8,128)(2,1)S(1)} %get-tuple-element.78.scores_ref, bf16[384,384]{1,0:T(8,128)(2,1)S(1)} %get-tuple-element.79.lanes_ref, bf16[192,192]{1,0:T(8,128)(2,1)S(1)} %get-tuple-element.80.rows_ref), custom_call_target="tpu_custom_call" | custom-call | bytes 2097152 | tf_op jit(solution)/shard_map/fold_table/pallas_call | solution.py:616
  23.7 0.1 collective-permute-done.5.recv_ref
  23.8 0.1 add_lat.1
  23.9 0.1 collective-permute-start.8
  24.0 0.1 collective-permute-start.9
  24.1 3.4 %collective-permute-start.10 = (bf16[656,128]{1,0:T(8,128)(2,1)S(1)}, bf16[656,128]{1,0:T(8,128)(2,1)S(1)}, u32[]{:S(2)}, u32[]{:S(2)}) collective-permute-start(bf16[656,128]{1,0:T(8,128)(2,1)S(1)} %get-tuple-element.99), channel_id=1, source_target_pairs={{0,2},{2,0},{4,6},{6,4},{8,10},{10,8},{12,14},{14,12},{16,18},{18,... | collective-permute-start | bytes 503816 | tf_op jit(solution)/shard_map/ppermute | solution.py:531
  27.5 1.0 %grad_field.1 = (bf16[36,384]{1,0:T(8,128)(2,1)S(1)}, bf16[72,384]{1,0:T(8,128)(2,1)S(1)}, bf16[72,384]{1,0:T(8,128)(2,1)S(1)}, bf16[36,384]{1,0:T(8,128)(2,1)S(1)}, bf16[16,128]{1,0:T(8,128)(2,1)S(1)}) custom-call(bf16[384,1152]{1,0:T(8,128)(2,1)S(1)} %get-tuple-element.63.win_ref, bf16[4,384,144]{2,1,0:T(8,128)(2,1)S(1)} %get-tuple-element.89.grad_projected_ref, ...), custom_call_target="tpu_custom_call" | custom-call | flops 100000000 | bytes 5242880 | tf_op jit(solution)/shard_map/grad_field/pallas_call | solution.py:644
  28.5 0.1 collective-permute-start.12
  28.6 0.5 collective-permute-start.11
  29.1 0.7 %collective-permute-done.12.refs_1_ = bf16[16,128]{1,0:T(8,128)(2,1)S(1)} collective-permute-done((bf16[16,128]{1,0:T(8,128)(2,1)S(1)}, bf16[16,128]{1,0:T(8,128)(2,1)S(1)}, u32[]{:S(2)}, u32[]{:S(2)}) %collective-permute-start.12) | collective-permute-done | bytes 4128 | tf_op jit(solution)/shard_map/ppermute | solution.py:531
  29.7 1.9 %collective-permute-start.6 = (bf16[72,384]{1,0:T(8,128)(2,1)S(1)}, bf16[72,384]{1,0:T(8,128)(2,1)S(1)}, u32[]{:S(2)}, u32[]{:S(2)}) collective-permute-start(bf16[72,384]{1,0:T(8,128)(2,1)S(1)} %get-tuple-element.95), channel_id=1, source_target_pairs={{0,2},{1,3},{2,4},{3,5},{4,6},{5,7},{6,8},{7,9},{8,10},{9,11},{10,... | collective-permute-start | bytes 165896 | tf_op jit(solution)/shard_map/ppermute | solution.py:84
  31.6 0.0 collective-permute-done.11.lat_ref
  31.6 0.7 %collective-permute-start.7 = (bf16[72,384]{1,0:T(8,128)(2,1)S(1)}, bf16[72,384]{1,0:T(8,128)(2,1)S(1)}, u32[]{:S(2)}, u32[]{:S(2)}) collective-permute-start(bf16[72,384]{1,0:T(8,128)(2,1)S(1)} %get-tuple-element.96), channel_id=1, source_target_pairs={{18,16},{19,17},{16,30},{17,31}} | collective-permute-start | bytes 165896 | tf_op jit(solution)/shard_map/ppermute | solution.py:84
  32.3 0.0 collective-permute-done.8.refs_2_
  32.3 2.0 %collective-permute-done.9.refs_3_ = bf16[656,128]{1,0:T(8,128)(2,1)S(1)} collective-permute-done((bf16[656,128]{1,0:T(8,128)(2,1)S(1)}, bf16[656,128]{1,0:T(8,128)(2,1)S(1)}, u32[]{:S(2)}, u32[]{:S(2)}) %collective-permute-start.9) | collective-permute-done | bytes 167968 | tf_op jit(solution)/shard_map/ppermute | solution.py:531
  34.3 0.0 collective-permute-done.10.refs_4_
  34.3 0.1 add_lon.1
  34.4 3.7 %collective-permute-start.15 = (bf16[240,128]{1,0:T(8,128)(2,1)S(1)}, bf16[240,128]{1,0:T(8,128)(2,1)S(1)}, u32[]{:S(2)}, u32[]{:S(2)}) collective-permute-start(bf16[240,128]{1,0:T(8,128)(2,1)S(1)} %get-tuple-element.109), channel_id=1, source_target_pairs={{0,24},{2,26},{4,28},{6,30},{8,16},{10,18},{12,20},{14,22},{16,8},... | collective-permute-start | bytes 184328 | tf_op jit(solution)/shard_map/ppermute | solution.py:531
  38.1 1.0 %collective-permute-start.16 = (bf16[240,128]{1,0:T(8,128)(2,1)S(1)}, bf16[240,128]{1,0:T(8,128)(2,1)S(1)}, u32[]{:S(2)}, u32[]{:S(2)}) collective-permute-start(bf16[240,128]{1,0:T(8,128)(2,1)S(1)} %get-tuple-element.110), channel_id=1, source_target_pairs={{0,16},{2,18},{4,20},{6,22},{8,24},{10,26},{12,28},{14,30},{16,0},... | collective-permute-start | bytes 184328 | tf_op jit(solution)/shard_map/ppermute | solution.py:531
  39.0 0.5 collective-permute-start.17
  39.5 0.0 collective-permute-done.6.near_ref
  39.5 0.0 collective-permute-start.13
  39.5 0.0 collective-permute-done.7.joint_ref
  39.5 0.5 collective-permute-start.14
  40.0 0.5 collective-permute-done.15.a_ref
  40.5 3.7 %collective-permute-done.16.b_ref = bf16[240,128]{1,0:T(8,128)(2,1)S(1)} collective-permute-done((bf16[240,128]{1,0:T(8,128)(2,1)S(1)}, bf16[240,128]{1,0:T(8,128)(2,1)S(1)}, u32[]{:S(2)}, u32[]{:S(2)}) %collective-permute-start.16) | collective-permute-done | bytes 61472 | tf_op jit(solution)/shard_map/ppermute | solution.py:531
  44.2 0.0 collective-permute-done.17.c_ref
  44.3 0.1 collective-permute-start.18
  44.3 1.8 %collective-permute-start.21 = (bf16[96,128]{1,0:T(8,128)(2,1)S(1)}, bf16[96,128]{1,0:T(8,128)(2,1)S(1)}, u32[]{:S(2)}, u32[]{:S(2)}) collective-permute-start(bf16[96,128]{1,0:T(8,128)(2,1)S(1)} %get-tuple-element.114.a_ref), channel_id=1, source_target_pairs={{0,6},{2,4},{4,2},{6,0},{8,14},{10,12},{12,10},{14,8},{16,22},{18,... | collective-permute-start | bytes 73736 | tf_op jit(solution)/shard_map/ppermute | solution.py:531
  46.2 0.8 %collective-permute-start.20 = (bf16[96,128]{1,0:T(8,128)(2,1)S(1)}, bf16[96,128]{1,0:T(8,128)(2,1)S(1)}, u32[]{:S(2)}, u32[]{:S(2)}) collective-permute-start(bf16[96,128]{1,0:T(8,128)(2,1)S(1)} %get-tuple-element.114.a_ref), channel_id=1, source_target_pairs={{0,4},{2,6},{4,0},{6,2},{8,12},{10,14},{12,8},{14,10},{16,20},{18,... | collective-permute-start | bytes 73736 | tf_op jit(solution)/shard_map/ppermute | solution.py:531
  47.0 0.0 collective-permute-done.13.near_diag_ref
  47.0 0.9 %collective-permute-start.19 = (bf16[96,128]{1,0:T(8,128)(2,1)S(1)}, bf16[96,128]{1,0:T(8,128)(2,1)S(1)}, u32[]{:S(2)}, u32[]{:S(2)}) collective-permute-start(bf16[96,128]{1,0:T(8,128)(2,1)S(1)} %get-tuple-element.114.a_ref), channel_id=1, source_target_pairs={{0,2},{2,0},{4,6},{6,4},{8,10},{10,8},{12,14},{14,12},{16,18},{18,... | collective-permute-start | bytes 73736 | tf_op jit(solution)/shard_map/ppermute | solution.py:531
  47.9 0.0 collective-permute-done.14.joint_diag_ref
  47.9 0.7 %unpack_quarters.1 = bf16[6,12,2,384]{3,2,1,0:T(2,128)(2,1)} custom-call(bf16[36,384]{1,0:T(8,128)(2,1)S(1)} %get-tuple-element.94.own_ref, bf16[72,384]{1,0:T(8,128)(2,1)S(1)} %collective-permute-done.6.near_ref, bf16[72,384]{1,0:T(8,128)(2,1)S(1)} %collective-permute-done.7.joint_ref, bf16[36,384]{1,0:T(8,128)(2,1)S(1)} %collective-permute-done.11.lat_ref, ...), custom_call_target="tpu_custom_call" | custom-call | bytes 4194304 | tf_op jit(solution)/shard_map/unpack_quarters/pallas_call | solution.py:701
  48.6 0.5 %collective-permute-done.21.d_ref = bf16[96,128]{1,0:T(8,128)(2,1)S(1)} collective-permute-done((bf16[96,128]{1,0:T(8,128)(2,1)S(1)}, bf16[96,128]{1,0:T(8,128)(2,1)S(1)}, u32[]{:S(2)}, u32[]{:S(2)}) %collective-permute-start.21) | collective-permute-done | bytes 24608 | tf_op jit(solution)/shard_map/ppermute | solution.py:531
  49.1 0.9 %collective-permute-done.20.c_ref = bf16[96,128]{1,0:T(8,128)(2,1)S(1)} collective-permute-done((bf16[96,128]{1,0:T(8,128)(2,1)S(1)}, bf16[96,128]{1,0:T(8,128)(2,1)S(1)}, u32[]{:S(2)}, u32[]{:S(2)}) %collective-permute-start.20) | collective-permute-done | bytes 24608 | tf_op jit(solution)/shard_map/ppermute | solution.py:531
  50.0 0.8 %collective-permute-done.19.b_ref = bf16[96,128]{1,0:T(8,128)(2,1)S(1)} collective-permute-done((bf16[96,128]{1,0:T(8,128)(2,1)S(1)}, bf16[96,128]{1,0:T(8,128)(2,1)S(1)}, u32[]{:S(2)}, u32[]{:S(2)}) %collective-permute-start.19) | collective-permute-done | bytes 24608 | tf_op jit(solution)/shard_map/ppermute | solution.py:531
  50.8 0.0 collective-permute-done.18.other_weights_ref
  50.8 0.8 %finish.1 = (bf16[24,1152]{1,0:T(8,128)(2,1)}, bf16[24,384]{1,0:T(8,128)(2,1)}, f32[12,1,3312]{2,1,0:T(1,128)}, f32[384]{0:T(512)}) custom-call(bf16[144,128]{1,0:T(8,128)(2,1)S(1)} %get-tuple-element.113.weights_ref, bf16[144,128]{1,0:T(8,128)(2,1)S(1)} %collective-permute-done.18.other_weights_ref, bf16[96,128]{1,0:T(8,128)(2,1)S(1)} %get-tuple-element.114.a_ref, ...), custom_call_target="tpu_custom_call" | custom-call | bytes 524288 | tf_op jit(solution)/shard_map/finish/pallas_call | solution.py:685
  (1 shorter events, 0.0 us)
Async XLA Ops:
  1.9 16.3 %collective-permute-start = (bf16[80,384]{1,0:T(8,128)(2,1)S(1)}, bf16[80,384]{1,0:T(8,128)(2,1)S(1)}, u32[]{:S(2)}, u32[]{:S(2)}) collective-permute-start(bf16[80,384]{1,0:T(8,128)(2,1)S(1)} %get-tuple-element.65), channel_id=1, source_target_pairs={{2,0},{3,1},{4,2},{5,3},{6,4},{7,5},{8,6},{9,7},{10,8},{11,9},{12,... | collective-permute-start | bytes 184328 | tf_op jit(solution)/shard_map/ppermute | solution.py:84
  7.9 10.3 %collective-permute-start.3 = (bf16[80,384]{1,0:T(8,128)(2,1)S(1)}, bf16[80,384]{1,0:T(8,128)(2,1)S(1)}, u32[]{:S(2)}, u32[]{:S(2)}) collective-permute-start(bf16[80,384]{1,0:T(8,128)(2,1)S(1)} %get-tuple-element.68), channel_id=1, source_target_pairs={{16,18},{17,19},{30,16},{31,17}} | collective-permute-start | bytes 184328 | tf_op jit(solution)/shard_map/ppermute | solution.py:84
  8.5 9.6 %collective-permute-start.1 = (bf16[72,384]{1,0:T(8,128)(2,1)S(1)}, bf16[72,384]{1,0:T(8,128)(2,1)S(1)}, u32[]{:S(2)}, u32[]{:S(2)}) collective-permute-start(bf16[72,384]{1,0:T(8,128)(2,1)S(1)} %get-tuple-element.66), channel_id=1, source_target_pairs={{2,1},{3,0},{4,3},{5,2},{6,5},{7,4},{8,7},{9,6},{10,9},{11,8},{12,... | collective-permute-start | bytes 165896 | tf_op jit(solution)/shard_map/ppermute | solution.py:84
  13.6 4.6 %collective-permute-start.2 = (bf16[72,384]{1,0:T(8,128)(2,1)S(1)}, bf16[72,384]{1,0:T(8,128)(2,1)S(1)}, u32[]{:S(2)}, u32[]{:S(2)}) collective-permute-start(bf16[72,384]{1,0:T(8,128)(2,1)S(1)} %get-tuple-element.67), channel_id=1, source_target_pairs={{0,1},{1,0},{2,3},{3,2},{4,5},{5,4},{6,7},{7,6},{8,9},{9,8},{10,11... | collective-permute-start | bytes 165896 | tf_op jit(solution)/shard_map/ppermute | solution.py:84
  14.9 3.3 %collective-permute-start.4 = (bf16[72,384]{1,0:T(8,128)(2,1)S(1)}, bf16[72,384]{1,0:T(8,128)(2,1)S(1)}, u32[]{:S(2)}, u32[]{:S(2)}) collective-permute-start(bf16[72,384]{1,0:T(8,128)(2,1)S(1)} %get-tuple-element.69), channel_id=1, source_target_pairs={{16,19},{17,18},{30,17},{31,16}} | collective-permute-start | bytes 165896 | tf_op jit(solution)/shard_map/ppermute | solution.py:84
  21.7 2.1 %collective-permute-start.5 = (bf16[2304,128]{1,0:T(8,128)(2,1)S(1)}, bf16[2304,128]{1,0:T(8,128)(2,1)S(1)}, u32[]{:S(2)}, u32[]{:S(2)}) collective-permute-start(bf16[2304,128]{1,0:T(8,128)(2,1)S(1)} %get-tuple-element.77), channel_id=1, source_target_pairs={{0,1},{1,0},{2,3},{3,2},{4,5},{5,4},{6,7},{7,6},{8,9},{9,8},{10,11... | collective-permute-start | bytes 1769480 | tf_op jit(solution)/shard_map/ppermute | solution.py:531
  23.9 8.4 %collective-permute-start.8 = (bf16[656,128]{1,0:T(8,128)(2,1)S(1)}, bf16[656,128]{1,0:T(8,128)(2,1)S(1)}, u32[]{:S(2)}, u32[]{:S(2)}) collective-permute-start(bf16[656,128]{1,0:T(8,128)(2,1)S(1)} %get-tuple-element.97), channel_id=1, source_target_pairs={{0,6},{2,4},{4,2},{6,0},{8,14},{10,12},{12,10},{14,8},{16,22},{18,... | collective-permute-start | bytes 503816 | tf_op jit(solution)/shard_map/ppermute | solution.py:531
  24.0 10.3 %collective-permute-start.9 = (bf16[656,128]{1,0:T(8,128)(2,1)S(1)}, bf16[656,128]{1,0:T(8,128)(2,1)S(1)}, u32[]{:S(2)}, u32[]{:S(2)}) collective-permute-start(bf16[656,128]{1,0:T(8,128)(2,1)S(1)} %get-tuple-element.98), channel_id=1, source_target_pairs={{0,4},{2,6},{4,0},{6,2},{8,12},{10,14},{12,8},{14,10},{16,20},{18,... | collective-permute-start | bytes 503816 | tf_op jit(solution)/shard_map/ppermute | solution.py:531
  24.1 10.2 %collective-permute-start.10 = (bf16[656,128]{1,0:T(8,128)(2,1)S(1)}, bf16[656,128]{1,0:T(8,128)(2,1)S(1)}, u32[]{:S(2)}, u32[]{:S(2)}) collective-permute-start(bf16[656,128]{1,0:T(8,128)(2,1)S(1)} %get-tuple-element.99), channel_id=1, source_target_pairs={{0,2},{2,0},{4,6},{6,4},{8,10},{10,8},{12,14},{14,12},{16,18},{18,... | collective-permute-start | bytes 503816 | tf_op jit(solution)/shard_map/ppermute | solution.py:531
  28.5 1.2 %collective-permute-start.12 = (bf16[16,128]{1,0:T(8,128)(2,1)S(1)}, bf16[16,128]{1,0:T(8,128)(2,1)S(1)}, u32[]{:S(2)}, u32[]{:S(2)}) collective-permute-start(bf16[16,128]{1,0:T(8,128)(2,1)S(1)} %get-tuple-element.102.refs_0_), channel_id=1, source_target_pairs={{0,1},{1,0},{2,3},{3,2},{4,5},{5,4},{6,7},{7,6},{8,9},{9,8},{10,11... | collective-permute-start | bytes 12296 | tf_op jit(solution)/shard_map/ppermute | solution.py:531
  28.6 3.1 %collective-permute-start.11 = (bf16[36,384]{1,0:T(8,128)(2,1)S(1)}, bf16[36,384]{1,0:T(8,128)(2,1)S(1)}, u32[]{:S(2)}, u32[]{:S(2)}) collective-permute-start(bf16[36,384]{1,0:T(8,128)(2,1)S(1)} %get-tuple-element.101), channel_id=1, source_target_pairs={{0,1},{1,0},{2,3},{3,2},{4,5},{5,4},{6,7},{7,6},{8,9},{9,8},{10,11... | collective-permute-start | bytes 82952 | tf_op jit(solution)/shard_map/ppermute | solution.py:84
  29.7 9.8 %collective-permute-start.6 = (bf16[72,384]{1,0:T(8,128)(2,1)S(1)}, bf16[72,384]{1,0:T(8,128)(2,1)S(1)}, u32[]{:S(2)}, u32[]{:S(2)}) collective-permute-start(bf16[72,384]{1,0:T(8,128)(2,1)S(1)} %get-tuple-element.95), channel_id=1, source_target_pairs={{0,2},{1,3},{2,4},{3,5},{4,6},{5,7},{6,8},{7,9},{8,10},{9,11},{10,... | collective-permute-start | bytes 165896 | tf_op jit(solution)/shard_map/ppermute | solution.py:84
  31.6 7.9 %collective-permute-start.7 = (bf16[72,384]{1,0:T(8,128)(2,1)S(1)}, bf16[72,384]{1,0:T(8,128)(2,1)S(1)}, u32[]{:S(2)}, u32[]{:S(2)}) collective-permute-start(bf16[72,384]{1,0:T(8,128)(2,1)S(1)} %get-tuple-element.96), channel_id=1, source_target_pairs={{18,16},{19,17},{16,30},{17,31}} | collective-permute-start | bytes 165896 | tf_op jit(solution)/shard_map/ppermute | solution.py:84
  34.4 6.1 %collective-permute-start.15 = (bf16[240,128]{1,0:T(8,128)(2,1)S(1)}, bf16[240,128]{1,0:T(8,128)(2,1)S(1)}, u32[]{:S(2)}, u32[]{:S(2)}) collective-permute-start(bf16[240,128]{1,0:T(8,128)(2,1)S(1)} %get-tuple-element.109), channel_id=1, source_target_pairs={{0,24},{2,26},{4,28},{6,30},{8,16},{10,18},{12,20},{14,22},{16,8},... | collective-permute-start | bytes 184328 | tf_op jit(solution)/shard_map/ppermute | solution.py:531
  38.1 6.2 %collective-permute-start.16 = (bf16[240,128]{1,0:T(8,128)(2,1)S(1)}, bf16[240,128]{1,0:T(8,128)(2,1)S(1)}, u32[]{:S(2)}, u32[]{:S(2)}) collective-permute-start(bf16[240,128]{1,0:T(8,128)(2,1)S(1)} %get-tuple-element.110), channel_id=1, source_target_pairs={{0,16},{2,18},{4,20},{6,22},{8,24},{10,26},{12,28},{14,30},{16,0},... | collective-permute-start | bytes 184328 | tf_op jit(solution)/shard_map/ppermute | solution.py:531
  39.0 5.2 %collective-permute-start.17 = (bf16[240,128]{1,0:T(8,128)(2,1)S(1)}, bf16[240,128]{1,0:T(8,128)(2,1)S(1)}, u32[]{:S(2)}, u32[]{:S(2)}) collective-permute-start(bf16[240,128]{1,0:T(8,128)(2,1)S(1)} %get-tuple-element.111), channel_id=1, source_target_pairs={{0,8},{2,10},{4,12},{6,14},{8,0},{10,2},{12,4},{14,6},{16,24},{18,... | collective-permute-start | bytes 184328 | tf_op jit(solution)/shard_map/ppermute | solution.py:531
  39.5 7.5 %collective-permute-start.13 = (bf16[72,384]{1,0:T(8,128)(2,1)S(1)}, bf16[72,384]{1,0:T(8,128)(2,1)S(1)}, u32[]{:S(2)}, u32[]{:S(2)}) collective-permute-start(bf16[72,384]{1,0:T(8,128)(2,1)S(1)} %collective-permute-done.6.near_ref), channel_id=1, source_target_pairs={{0,1},{1,0},{2,3},{3,2},{4,5},{5,4},{6,7},{7,6},{8,9},{9,8},{10,11... | collective-permute-start | bytes 165896 | tf_op jit(solution)/shard_map/ppermute | solution.py:84
  39.5 8.4 %collective-permute-start.14 = (bf16[72,384]{1,0:T(8,128)(2,1)S(1)}, bf16[72,384]{1,0:T(8,128)(2,1)S(1)}, u32[]{:S(2)}, u32[]{:S(2)}) collective-permute-start(bf16[72,384]{1,0:T(8,128)(2,1)S(1)} %collective-permute-done.7.joint_ref), channel_id=1, source_target_pairs={{0,1},{1,0},{2,3},{3,2},{4,5},{5,4},{6,7},{7,6},{8,9},{9,8},{10,11... | collective-permute-start | bytes 165896 | tf_op jit(solution)/shard_map/ppermute | solution.py:84
  44.3 6.6 %collective-permute-start.18 = (bf16[144,128]{1,0:T(8,128)(2,1)S(1)}, bf16[144,128]{1,0:T(8,128)(2,1)S(1)}, u32[]{:S(2)}, u32[]{:S(2)}) collective-permute-start(bf16[144,128]{1,0:T(8,128)(2,1)S(1)} %get-tuple-element.113.weights_ref), channel_id=1, source_target_pairs={{0,1},{1,0},{2,3},{3,2},{4,5},{5,4},{6,7},{7,6},{8,9},{9,8},{10,11... | collective-permute-start | bytes 110600 | tf_op jit(solution)/shard_map/ppermute | solution.py:531
  44.3 4.8 %collective-permute-start.21 = (bf16[96,128]{1,0:T(8,128)(2,1)S(1)}, bf16[96,128]{1,0:T(8,128)(2,1)S(1)}, u32[]{:S(2)}, u32[]{:S(2)}) collective-permute-start(bf16[96,128]{1,0:T(8,128)(2,1)S(1)} %get-tuple-element.114.a_ref), channel_id=1, source_target_pairs={{0,6},{2,4},{4,2},{6,0},{8,14},{10,12},{12,10},{14,8},{16,22},{18,... | collective-permute-start | bytes 73736 | tf_op jit(solution)/shard_map/ppermute | solution.py:531
  46.2 3.8 %collective-permute-start.20 = (bf16[96,128]{1,0:T(8,128)(2,1)S(1)}, bf16[96,128]{1,0:T(8,128)(2,1)S(1)}, u32[]{:S(2)}, u32[]{:S(2)}) collective-permute-start(bf16[96,128]{1,0:T(8,128)(2,1)S(1)} %get-tuple-element.114.a_ref), channel_id=1, source_target_pairs={{0,4},{2,6},{4,0},{6,2},{8,12},{10,14},{12,8},{14,10},{16,20},{18,... | collective-permute-start | bytes 73736 | tf_op jit(solution)/shard_map/ppermute | solution.py:531
  47.0 3.8 %collective-permute-start.19 = (bf16[96,128]{1,0:T(8,128)(2,1)S(1)}, bf16[96,128]{1,0:T(8,128)(2,1)S(1)}, u32[]{:S(2)}, u32[]{:S(2)}) collective-permute-start(bf16[96,128]{1,0:T(8,128)(2,1)S(1)} %get-tuple-element.114.a_ref), channel_id=1, source_target_pairs={{0,2},{2,0},{4,6},{6,4},{8,10},{10,8},{12,14},{14,12},{16,18},{18,... | collective-permute-start | bytes 73736 | tf_op jit(solution)/shard_map/ppermute | solution.py:531

commit v4 on v2

--- a/solution.py
+++ b/solution.py
@@ -69,21 +69,32 @@
     return copies
 
 
+SAME = 80
+
+
 def load_kernel(field_src, cot_src, *refs):
-    sources, out_refs, targets, (field_ref, cot_ref, sems) = refs[:3], refs[3:7], refs[7:10], refs[10:]
-    copies = fetch((field_src, cot_src) + sources, (field_ref, cot_ref) + targets, sems)
-    for copy in copies[:2]:
+    sources, out_refs, (table_ref, gain_ref) = refs[:3], refs[3:7], refs[7:9]
+    field_ref, cot_ref, regions_ref, sems = refs[9:]
+    copies = fetch((field_src, cot_src) + sources, (field_ref, cot_ref, regions_ref, table_ref, gain_ref), sems)
+    for copy in copies[:3]:
         copy.wait()
     half_rows, half_cols = WIN_LAT // 2, WIN_LON // 2
-    for (lat_half, lon_half), out_ref in zip(QUARTERS, out_refs):
-        first_row, first_col = (1 - lat_half) * half_rows, (1 - lon_half) * half_cols
-        pieces = []
-        for ref in (field_ref, cot_ref):
-            for row in range(half_rows):
-                for col in range(half_cols):
-                    pieces.append(ref[first_row + row, first_col + col].astype(f32))
+    features = field_ref.shape[3]
+    ids = [regions_ref[row, level : level + 1, :].astype(f32) for level in range(LEV) for row in range(WIN_LAT)]
+    ids.append(jnp.zeros((1, features - CELLS), f32))
+    tail = jnp.concatenate([jnp.concatenate(ids, axis=1), jnp.zeros((SAME - 2 * QUARTER - 1, features), f32)], axis=0)
+    wanted = ((half_rows, 0), (half_rows, half_cols), (0, half_cols), (0, 0))
+    for (first_row, first_col), out_ref in zip(wanted, out_refs):
+        pieces = [
+            ref[first_row + row, first_col + col].astype(f32)
+            for ref in (field_ref, cot_ref)
+            for row in range(half_rows)
+            for col in range(half_cols)
+        ]
+        if out_ref.shape[0] == SAME:
+            pieces.append(tail)
         out_ref[...] = jnp.concatenate(pieces, axis=0).astype(bf16)
-    for copy in copies[2:]:
+    for copy in copies[3:]:
         copy.wait()
 
 
@@ -103,12 +114,16 @@
     return quarter * stride + place * LEV + lax.rem(level + LEV // 2, LEV)
 
 
-def unpack_kernel(own_ref, lon_ref, lat_ref, diag_ref, out_ref):
+def unpack_kernel(own_ref, near_ref, lat_ref, near_diag_ref, out_ref):
     half_rows, half_cols = WIN_LAT // 2, WIN_LON // 2
-    sources = ((own_ref, 0), (lon_ref, 0), (lat_ref, 0), (diag_ref, QUARTER))
-    for (lat_half, lon_half), (ref, start) in zip(QUARTERS, sources):
+    quarters = (
+        near_ref[...].astype(f32)[:QUARTER],
+        own_ref[...].astype(f32),
+        near_diag_ref[...].astype(f32)[QUARTER:],
+        lat_ref[...].astype(f32),
+    )
+    for (lat_half, lon_half), cells in zip(QUARTERS, quarters):
         first_row, first_col = (1 - lat_half) * half_rows, (1 - lon_half) * half_cols
-        cells = ref[...].astype(f32)[start : start + QUARTER]
         for row in range(half_rows):
             for col in range(half_cols):
                 first = (row * half_cols + col) * LEV
@@ -117,7 +132,6 @@
 
 def bias_kernel(
     table_ref,
-    regions_ref,
     win_src,
     wout_src,
     out_ref,
@@ -160,42 +174,30 @@
     moved = nn_dot(stage[...].astype(bf16), lanes_ref[...]).astype(bf16)
     rows = nn_dot(rows_ref[...], moved)
 
-    region_rows = [regions_ref[row, level : level + 1, :] for level in range(LEV) for row in range(WIN_LAT)]
-    region_grid = jnp.concatenate(region_rows, axis=0).astype(f32).astype(bf16)
-    cell, lane = counted((CELLS, PLANE), 0), counted((CELLS, PLANE), 1)
-    by_plane = nn_dot(one_hot(lax.rem(cell, PLANE) == lane), region_grid)
-    region_col = jnp.sum(jnp.where(lax.div(cell, PLANE) == lane, by_plane, 0.0), axis=1, keepdims=True)
-    across = counted((CELLS, CELLS), 0) == counted((CELLS, CELLS), 1)
-    region_row = jnp.sum(jnp.where(across, region_col, 0.0), axis=0, keepdims=True)
-    same = region_col == region_row
-
     for col in range(WIN_LON):
         shift = PLANE * (WIN_LON - 1 - col)
         moved = rows if shift == 0 else pltpu.roll(rows, WIDE - shift, 1)
         for head in range(HEADS):
             full[head, PLANE * col : PLANE * (col + 1), :] = moved[16 * head : 16 * head + PLANE, :CELLS]
     for head in range(HEADS):
-        out_ref[head] = jnp.where(same, full[head], masked_score).astype(bf16)
+        out_ref[head] = full[head].astype(bf16)
     for copy in copies:
         copy.wait()
-    for block in range(3):
-        cols = slice(block * features, (block + 1) * features)
-        win_t_ref[cols] = nt_dot(eye, win_ref[:, cols]).astype(bf16)
+    win_t_ref[...] = nt_dot(eye, win_ref[:, :features]).astype(bf16)
 
 
 def window_kernel(
     packet,
     own_ref,
-    lon_ref,
+    near_ref,
+    near_diag_ref,
     lat_ref,
-    diag_ref,
     gain_ref,
     win_ref,
     win_t_ref,
     wout_ref,
     bias_ref,
     place_ref,
-    eye_ref,
     keep_ref,
     send_ref,
     scores_ref,
@@ -209,9 +211,15 @@
     head_dim = features // HEADS
     group_heads = LANES // head_dim
     score_scale = head_dim ** (-0.5)
-    quarters = (own_ref, lon_ref, lat_ref, diag_ref)
-    eye = eye_ref[...]
-    stacked = jnp.concatenate([ref[...].astype(f32) for ref in quarters], axis=0).astype(bf16)
+    near = near_ref[...].astype(f32)
+    west, east = [near[: 2 * QUARTER], near_diag_ref[...].astype(f32)], [own_ref[...].astype(f32), lat_ref[...].astype(f32)]
+    stacked = jnp.concatenate([west[0], east[0], west[1], east[1]], axis=0).astype(bf16)
+    cell, lane = counted((CELLS, CELLS), 0), counted((CELLS, CELLS), 1)
+    source = lax.rem(cell, PLANE) * WIN_LON + lax.div(cell, PLANE)
+    ids = near[2 * QUARTER : 2 * QUARTER + 1, :CELLS]
+    region_col = jnp.sum(jnp.where(source == lane, ids, 0.0), axis=1, keepdims=True)
+    region_row = jnp.sum(jnp.where(cell == lane, region_col, 0.0), axis=0, keepdims=True)
+    same = region_col == region_row
     placed = nn_dot(place_ref[...], stacked)
     field = placed[:CELLS]
     cot = placed[CELLS:].astype(bf16)
@@ -225,11 +233,13 @@
     inv_std_ref[...] = inv_std
     normed = (normalized * gain).astype(bf16)
 
-    projected_t = nt_dot(win_t_ref[...], normed).astype(bf16)
-    keys_values = nn_dot(normed, win_ref[:, features:]).astype(bf16)
+    query_t = nt_dot(win_t_ref[...], normed).astype(bf16)
+    wide_keys_values = nn_dot(normed, win_ref[:, features:])
+    keys_values = wide_keys_values.astype(bf16)
     grad_att_t = nt_dot(wout_ref[...], cot).astype(bf16)
-    left[0] = nt_dot(eye, normed).astype(bf16)
-    right[3] = nt_dot(eye, cot).astype(bf16)
+    key_value_t = jnp.transpose(wide_keys_values).astype(bf16)
+    left[0] = jnp.transpose(normed.astype(f32)).astype(bf16)
+    right[3] = jnp.transpose(placed[CELLS:]).astype(bf16)
 
     def spread(head_rows, slot):
         parts = []
@@ -244,7 +254,10 @@
         return slice(head * head_dim, (head + 1) * head_dim)
 
     def part(head, index):
-        return projected_t[index * features + head * head_dim : index * features + (head + 1) * head_dim]
+        if index == 0:
+            return query_t[rows_of(head)]
+        first = (index - 1) * features + head * head_dim
+        return key_value_t[first : first + head_dim]
 
     def scores_of(head):
         group, slot = divmod(head, group_heads)
@@ -254,7 +267,7 @@
         return scores, nn_dot(values, spread(grad_att_t[rows_of(head)], slot))
 
     def softmax_of(head, scores, grad_probs):
-        scores = scores * score_scale + bias_ref[head].astype(f32)
+        scores = jnp.where(same, scores * score_scale + bias_ref[head].astype(f32), masked_score)
         grown = jnp.exp(scores - jnp.max(scores, axis=0, keepdims=True))
         probs = grown * (1.0 / jnp.sum(grown, axis=0, keepdims=True))
         weighted = probs * grad_probs
@@ -304,7 +317,7 @@
     place_t_ref,
     eye_ref,
     back_own_ref,
-    back_lon_ref,
+    back_near_ref,
     back_lat_ref,
     gain_out_ref,
 ):
@@ -322,9 +335,9 @@
     )
     back = nn_dot(place_t_ref[...], grad_field.astype(bf16))
     quarters = [back[quarter * QUARTER : (quarter + 1) * QUARTER] for quarter in range(4)]
-    back_own_ref[...] = quarters[0].astype(bf16)
-    back_lon_ref[...] = jnp.concatenate([quarters[1], quarters[3]], axis=0).astype(bf16)
-    back_lat_ref[...] = quarters[2].astype(bf16)
+    back_own_ref[...] = quarters[1].astype(bf16)
+    back_near_ref[...] = jnp.concatenate(quarters[::2], axis=0).astype(bf16)
+    back_lat_ref[...] = quarters[3].astype(bf16)
     gain_sum = jnp.sum(grad_normed * normalized, axis=0, keepdims=True)
     gain_rows = [gain_sum[:, tile * LANES : (tile + 1) * LANES] for tile in range(3)]
     gain_out_ref[...] = jnp.concatenate(gain_rows + [jnp.zeros((13, LANES), f32)], axis=0).astype(bf16)
@@ -477,26 +490,27 @@
 
     hbm = pl.BlockSpec(memory_space=pltpu.HBM)
     field, cot = jnp.transpose(latent_field, (1, 2, 0, 3)), jnp.transpose(cotangent, (1, 2, 0, 3))
-    small = (bias_table[0], jnp.transpose(regions, (1, 0, 2)), norm_gain)
-    own, to_lon, to_lat, to_diag, table, region_grid, gain = call(
+    small = (jnp.transpose(regions, (1, 0, 2)), bias_table[0], norm_gain)
+    same, others = struct((SAME, features), bf16), struct((2 * QUARTER, features), bf16)
+    own, far, far_others, to_lat, table, gain = call(
         load_kernel,
         "load",
         [hbm] * 5,
-        [struct((2 * QUARTER, features), bf16)] * 4 + [struct(array.shape, array.dtype) for array in small],
-        [space_for(field), space_for(cot), pltpu.SemaphoreType.DMA((5,))],
+        [others, same, others, others] + [struct(array.shape, array.dtype) for array in small[1:]],
+        [space_for(field), space_for(cot), space_for(small[0]), pltpu.SemaphoreType.DMA((5,))],
         moved=1 << 20,
     )(*in_hbm(field, cot, *small))
-    from_lon = move(to_lon, -1, 0)
-    from_diag = move(to_diag, -1, -1)
+    from_near = move(far, 1, 0)
+    from_near_diag = move(far_others, 1, -1)
     from_lat = move(to_lat, 0, -1)
 
     bias_full, input_weight_t, lane_moves, row_moves, eye, place, place_t, weight_in, weight_out = call(
         bias_kernel,
         "expand_bias",
-        whole(2) + [hbm] * 2,
+        whole(1) + [hbm] * 2,
         [
             struct((HEADS, CELLS, CELLS), bf16),
-            struct((3 * features, features), bf16),
+            struct((features, features), bf16),
             struct((WIDE, WIDE), bf16),
             struct((HEADS * 16, HEADS * 16), bf16),
             struct((features, features), bf16),
@@ -511,13 +525,13 @@
             pltpu.SemaphoreType.DMA((2,)),
         ],
         moved=1 << 21,
-    )(table, region_grid, *in_hbm(input_weight, output_weight))
+    )(table, *in_hbm(input_weight, output_weight))
 
     half_sum = struct((lon_count * packet.weight_size, LANES), bf16)
     results = call(
         functools.partial(window_kernel, packet),
         "window",
-        whole(11),
+        whole(10),
         [
             half_sum,
             half_sum,
@@ -532,16 +546,15 @@
         moved=5 << 20,
     )(
             own,
-        from_lon,
+        from_near,
+        from_near_diag,
         from_lat,
-        from_diag,
         gain,
         weight_in,
         input_weight_t,
         weight_out,
         bias_full,
         place,
-        eye,
     )
     keep, send, scores_low, *saved = results
 
@@ -574,11 +587,11 @@
 
     held = trade(parts, 0)
     piece = struct((QUARTER, features), bf16)
-    back_own, back_lon, back_lat, gain_part = call(
+    back_own, back_near, back_lat, gain_part = call(
         field_kernel,
         "grad_field",
         whole(8),
-        [piece, struct((2 * QUARTER, features), bf16), piece, struct((16, LANES), bf16)],
+        [piece, others, piece, struct((16, LANES), bf16)],
         flops=10**8,
         moved=5 << 20,
     )(weight_in, *saved, gain, place_t, eye)
@@ -586,8 +599,8 @@
     gain_other = swap(gain_part, "lat", 1)
     held, home_lat, gain_other = lax.optimization_barrier((held, home_lat, gain_other))
     gains = [gain_part, gain_other]
-    home_lon = move(back_lon, 1, 0)
-    home_diag = move(home_lon, 0, 1)
+    home_near = move(back_near, -1, 0)
+    home_diag = move(home_near, 0, 1)
     for shift in range(2, lon_count.bit_length() - 1, 2):
         groups //= 4
         parts = call(
@@ -630,8 +643,12 @@
         gain_sum = gain_sum + swap(gain_sum, "lat", 1 << bit)
 
     grad_field = call(
-        unpack_kernel, "unpack_quarters", whole(4), struct((WIN_LAT, WIN_LON, LEV, features), bf16), moved=4 << 20
-    )(back_own, home_lon, home_lat, home_diag)
+        unpack_kernel,
+        "unpack_quarters",
+        whole(4),
+        struct((WIN_LAT, WIN_LON, LEV, features), bf16),
+        moved=4 << 20,
+    )(back_own, home_near, home_lat, home_diag)
     return (
         jnp.transpose(grad_field, (2, 0, 1, 3)),
         grad_input_weight,

time: 45.9 us -> 44.3 us (0.965)
  starting transfers between devices: 21.4 us -> 18.2 us
  waiting for transfers between devices: 11.2 us -> 14 us
  Pallas kernels: 12.3 us -> 11.2 us
    ppermute x6, waiting for transfers between devices: 0.02 us -> 3.65 us  [move(): return lax.ppermute(value, ('lon', 'lat'), pairs)]
    ppermute x6, starting transfers between devices: 9.02 us -> 6 us  [move(): return lax.ppermute(value, ('lon', 'lat'), pairs)]
    pallas_call x4, Pallas kernels: 8.65 us -> 7.61 us  [the longest x1 3.17 us: on_device(): call(functools.partial(window_kernel, packet), 'window', whole(10), [half...]
    ppermute x12, waiting for transfers between devices: 11.2 us -> 10.4 us  [swap(): lax.ppermute(value, axis, [(source, source ^ mask) for source in range(co...]
  transfers between devices with their start and end apart: 18 -> 18, of which waited for: 8 -> 10; matrix products, arithmetic and copies ran while one was open for 0% -> 0% of each run, Pallas kernels for 15% -> 13%
where the time goes in v4:
time: 44.3 us; the launch traced here: 44.1 us
  starting transfers between devices  18.2 us (41%)
  waiting for transfers between devices  14 us (32%)
  Pallas kernels  11.2 us (25%)
  between operations  0.73 us (2%)
    ppermute x12, starting transfers between devices, swap(): lax.ppermute(value, axis, [(source, source ^ mask) for source in range(co...  12.2 us
    ppermute x12, waiting for transfers between devices, swap(): lax.ppermute(value, axis, [(source, source ^ mask) for source in range(co...  10.4 us
    ppermute x6, starting transfers between devices, move(): return lax.ppermute(value, ('lon', 'lat'), pairs)  6 us
    ppermute x6, waiting for transfers between devices, move(): return lax.ppermute(value, ('lon', 'lat'), pairs)  3.65 us
    pallas_call x1, Pallas kernels, on_device(): call(functools.partial(window_kernel, packet), 'window', whole(10), [half...  3.17 us
    pallas_call x1, Pallas kernels, on_device(): call(bias_kernel, 'expand_bias', whole(1) + [hbm] * 2, [struct((HEADS, CE...  2.25 us
    pallas_call x1, Pallas kernels, on_device(): call(functools.partial(fold_kernel, packet), 'fold_table', whole(3), stru...  1.9 us
    pallas_call x1, Pallas kernels, on_device(): call(load_kernel, 'load', [hbm] * 5, [others, same, others, others] + [st...  1.18 us
  transfers between devices with their start and end apart: 18, of which 10 were waited for; matrix products, arithmetic and copies ran while one was open for 0% of the time, Pallas kernels for 13%

profile of v4, /device:TPU:0, one launch (start us, length us, event | category | flops | bytes accessed | tf_op | source)
XLA Modules:
  0.0 44.1 jit_solution(3522511640578515467)
XLA Ops:
  0.6 1.2 %load.1 = (bf16[72,384]{1,0:T(8,128)(2,1)S(1)}, bf16[80,384]{1,0:T(8,128)(2,1)S(1)}, bf16[72,384]{1,0:T(8,128)(2,1)S(1)}, bf16[72,384]{1,0:T(8,128)(2,1)S(1)}, b...) custom-call(bf16[6,12,2,384]{3,2,1,0:T(2,128)(2,1)} %bitcast.7, bf16[6,12,2,384]{3,2,1,0:T(2,128)(2,1)} %bitcast.8, ...), custom_call_target="tpu_custom_call" | custom-call | bytes 1048576 | tf_op jit(solution)/shard_map/load/pallas_call | solution.py:495
  1.8 3.0 %collective-permute-start = (bf16[80,384]{1,0:T(8,128)(2,1)S(1)}, bf16[80,384]{1,0:T(8,128)(2,1)S(1)}, u32[]{:S(2)}, u32[]{:S(2)}) collective-permute-start(bf16[80,384]{1,0:T(8,128)(2,1)S(1)} %get-tuple-element.62), channel_id=1, source_target_pairs={{0,2},{1,3},{2,4},{3,5},{4,6},{5,7},{6,8},{7,9},{8,10},{9,11},{10,... | collective-permute-start | bytes 184328 | tf_op jit(solution)/shard_map/ppermute | solution.py:478
  4.8 0.7 %collective-permute-start.1 = (bf16[72,384]{1,0:T(8,128)(2,1)S(1)}, bf16[72,384]{1,0:T(8,128)(2,1)S(1)}, u32[]{:S(2)}, u32[]{:S(2)}) collective-permute-start(bf16[72,384]{1,0:T(8,128)(2,1)S(1)} %get-tuple-element.63), channel_id=1, source_target_pairs={{0,3},{1,2},{2,5},{3,4},{4,7},{5,6},{6,9},{7,8},{8,11},{9,10},{10,... | collective-permute-start | bytes 165896 | tf_op jit(solution)/shard_map/ppermute | solution.py:478
  5.5 1.0 %collective-permute-start.2 = (bf16[72,384]{1,0:T(8,128)(2,1)S(1)}, bf16[72,384]{1,0:T(8,128)(2,1)S(1)}, u32[]{:S(2)}, u32[]{:S(2)}) collective-permute-start(bf16[72,384]{1,0:T(8,128)(2,1)S(1)} %get-tuple-element.64), channel_id=1, source_target_pairs={{0,1},{1,0},{2,3},{3,2},{4,5},{5,4},{6,7},{7,6},{8,9},{9,8},{10,11... | collective-permute-start | bytes 165896 | tf_op jit(solution)/shard_map/ppermute | solution.py:478
  6.4 2.3 %expand_bias.1 = (bf16[12,144,144]{2,1,0:T(8,128)(2,1)S(1)}, bf16[384,384]{1,0:T(8,128)(2,1)S(1)}, bf16[384,384]{1,0:T(8,128)(2,1)S(1)}, bf16[192,192]{1,0:T(8,1...) custom-call(bf16[12,3312]{1,0:T(8,128)(2,1)S(1)} %get-tuple-element., ...), custom_call_target="tpu_custom_call" | custom-call | bytes 2097152 | tf_op jit(solution)/shard_map/expand_bias/pallas_call | solution.py:507
  8.7 3.6 %collective-permute-done.1.near_diag_ref = bf16[72,384]{1,0:T(8,128)(2,1)S(1)} collective-permute-done((bf16[72,384]{1,0:T(8,128)(2,1)S(1)}, bf16[72,384]{1,0:T(8,128)(2,1)S(1)}, u32[]{:S(2)}, u32[]{:S(2)}) %collective-permute-start.1) | collective-permute-done | bytes 55328 | tf_op jit(solution)/shard_map/ppermute | solution.py:478
  12.3 0.0 collective-permute-done.2.lat_ref
  12.3 0.0 collective-permute-done.near_ref
  12.3 3.2 %window.1 = (bf16[2304,128]{1,0:T(8,128)(2,1)S(1)}, bf16[2304,128]{1,0:T(8,128)(2,1)S(1)}, bf16[12,144,144]{2,1,0:T(8,128)(2,1)S(1)}, bf16[4,384,144]{2,1,0:T(8,...) custom-call(bf16[72,384]{1,0:T(8,128)(2,1)S(1)} %get-tuple-element.61.own_ref, ...), custom_call_target="tpu_custom_call" | custom-call | flops 1000000000 | bytes 5242880 | tf_op jit(solution)/shard_map/window/pallas_call | solution.py:531
  15.5 0.1 collective-permute-start.3
  15.6 1.9 %fold_table.1.table_ref = bf16[320,128]{1,0:T(8,128)(2,1)S(1)} custom-call(bf16[12,144,144]{2,1,0:T(8,128)(2,1)S(1)} %get-tuple-element.72.scores_ref, bf16[384,384]{1,0:T(8,128)(2,1)S(1)} %get-tuple-element.73.lanes_ref, bf16[192,192]{1,0:T(8,128)(2,1)S(1)} %get-tuple-element.74.rows_ref), custom_call_target="tpu_custom_call" | custom-call | bytes 2097152 | tf_op jit(solution)/shard_map/fold_table/pallas_call | solution.py:562
  17.5 0.1 collective-permute-done.3.recv_ref
  17.6 0.1 add_lat.1
  17.7 0.1 collective-permute-start.5
  17.8 0.1 collective-permute-start.6
  17.9 3.4 %collective-permute-start.7 = (bf16[656,128]{1,0:T(8,128)(2,1)S(1)}, bf16[656,128]{1,0:T(8,128)(2,1)S(1)}, u32[]{:S(2)}, u32[]{:S(2)}) collective-permute-start(bf16[656,128]{1,0:T(8,128)(2,1)S(1)} %get-tuple-element.93), channel_id=1, source_target_pairs={{0,2},{2,0},{4,6},{6,4},{8,10},{10,8},{12,14},{14,12},{16,18},{18,... | collective-permute-start | bytes 503816 | tf_op jit(solution)/shard_map/ppermute | solution.py:482
  21.3 1.0 %grad_field.1 = (bf16[36,384]{1,0:T(8,128)(2,1)S(1)}, bf16[72,384]{1,0:T(8,128)(2,1)S(1)}, bf16[36,384]{1,0:T(8,128)(2,1)S(1)}, bf16[16,128]{1,0:T(8,128)(2,1)S(1)}) custom-call(bf16[384,1152]{1,0:T(8,128)(2,1)S(1)} %get-tuple-element.60.win_ref, bf16[4,384,144]{2,1,0:T(8,128)(2,1)S(1)} %get-tuple-element.83.grad_projected_ref, ...), custom_call_target="tpu_custom_call" | custom-call | flops 100000000 | bytes 5242880 | tf_op jit(solution)/shard_map/grad_field/pallas_call | solution.py:590
  22.3 0.1 collective-permute-start.8
  22.4 0.5 %collective-permute-start.9 = (bf16[16,128]{1,0:T(8,128)(2,1)S(1)}, bf16[16,128]{1,0:T(8,128)(2,1)S(1)}, u32[]{:S(2)}, u32[]{:S(2)}) collective-permute-start(bf16[16,128]{1,0:T(8,128)(2,1)S(1)} %get-tuple-element.96.refs_0_), channel_id=1, source_target_pairs={{0,1},{1,0},{2,3},{3,2},{4,5},{5,4},{6,7},{7,6},{8,9},{9,8},{10,11... | collective-permute-start | bytes 12296 | tf_op jit(solution)/shard_map/ppermute | solution.py:482
  22.8 0.8 %collective-permute-done.9.refs_1_ = bf16[16,128]{1,0:T(8,128)(2,1)S(1)} collective-permute-done((bf16[16,128]{1,0:T(8,128)(2,1)S(1)}, bf16[16,128]{1,0:T(8,128)(2,1)S(1)}, u32[]{:S(2)}, u32[]{:S(2)}) %collective-permute-start.9) | collective-permute-done | bytes 4128 | tf_op jit(solution)/shard_map/ppermute | solution.py:482
  23.7 1.3 %collective-permute-start.4 = (bf16[72,384]{1,0:T(8,128)(2,1)S(1)}, bf16[72,384]{1,0:T(8,128)(2,1)S(1)}, u32[]{:S(2)}, u32[]{:S(2)}) collective-permute-start(bf16[72,384]{1,0:T(8,128)(2,1)S(1)} %get-tuple-element.90), channel_id=1, source_target_pairs={{0,30},{1,31},{2,0},{3,1},{4,2},{5,3},{6,4},{7,5},{8,6},{9,7},{10,... | collective-permute-start | bytes 165896 | tf_op jit(solution)/shard_map/ppermute | solution.py:478
  25.0 0.0 collective-permute-done.8.lat_ref
  25.0 0.8 %collective-permute-done.5.refs_2_ = bf16[656,128]{1,0:T(8,128)(2,1)S(1)} collective-permute-done((bf16[656,128]{1,0:T(8,128)(2,1)S(1)}, bf16[656,128]{1,0:T(8,128)(2,1)S(1)}, u32[]{:S(2)}, u32[]{:S(2)}) %collective-permute-start.5) | collective-permute-done | bytes 167968 | tf_op jit(solution)/shard_map/ppermute | solution.py:482
  25.8 2.3 %collective-permute-done.6.refs_3_ = bf16[656,128]{1,0:T(8,128)(2,1)S(1)} collective-permute-done((bf16[656,128]{1,0:T(8,128)(2,1)S(1)}, bf16[656,128]{1,0:T(8,128)(2,1)S(1)}, u32[]{:S(2)}, u32[]{:S(2)}) %collective-permute-start.6) | collective-permute-done | bytes 167968 | tf_op jit(solution)/shard_map/ppermute | solution.py:482
  28.1 0.0 collective-permute-done.7.refs_4_
  28.1 0.1 add_lon.1
  28.2 2.4 %collective-permute-start.11 = (bf16[240,128]{1,0:T(8,128)(2,1)S(1)}, bf16[240,128]{1,0:T(8,128)(2,1)S(1)}, u32[]{:S(2)}, u32[]{:S(2)}) collective-permute-start(bf16[240,128]{1,0:T(8,128)(2,1)S(1)} %get-tuple-element.103), channel_id=1, source_target_pairs={{0,24},{2,26},{4,28},{6,30},{8,16},{10,18},{12,20},{14,22},{16,8},... | collective-permute-start | bytes 184328 | tf_op jit(solution)/shard_map/ppermute | solution.py:482
  30.5 0.0 collective-permute-start.12
  30.5 2.1 %collective-permute-start.13 = (bf16[240,128]{1,0:T(8,128)(2,1)S(1)}, bf16[240,128]{1,0:T(8,128)(2,1)S(1)}, u32[]{:S(2)}, u32[]{:S(2)}) collective-permute-start(bf16[240,128]{1,0:T(8,128)(2,1)S(1)} %get-tuple-element.105), channel_id=1, source_target_pairs={{0,8},{2,10},{4,12},{6,14},{8,0},{10,2},{12,4},{14,6},{16,24},{18,... | collective-permute-start | bytes 184328 | tf_op jit(solution)/shard_map/ppermute | solution.py:482
  32.6 0.0 collective-permute-done.4.near_ref
  32.6 0.0 collective-permute-start.10
  32.6 1.9 %collective-permute-done.11.a_ref = bf16[240,128]{1,0:T(8,128)(2,1)S(1)} collective-permute-done((bf16[240,128]{1,0:T(8,128)(2,1)S(1)}, bf16[240,128]{1,0:T(8,128)(2,1)S(1)}, u32[]{:S(2)}, u32[]{:S(2)}) %collective-permute-start.11) | collective-permute-done | bytes 61472 | tf_op jit(solution)/shard_map/ppermute | solution.py:482
  34.5 1.7 %collective-permute-done.12.b_ref = bf16[240,128]{1,0:T(8,128)(2,1)S(1)} collective-permute-done((bf16[240,128]{1,0:T(8,128)(2,1)S(1)}, bf16[240,128]{1,0:T(8,128)(2,1)S(1)}, u32[]{:S(2)}, u32[]{:S(2)}) %collective-permute-start.12) | collective-permute-done | bytes 61472 | tf_op jit(solution)/shard_map/ppermute | solution.py:482
  36.2 0.0 collective-permute-done.13.c_ref
  36.3 0.1 collective-permute-start.14
  36.4 2.2 %collective-permute-start.17 = (bf16[96,128]{1,0:T(8,128)(2,1)S(1)}, bf16[96,128]{1,0:T(8,128)(2,1)S(1)}, u32[]{:S(2)}, u32[]{:S(2)}) collective-permute-start(bf16[96,128]{1,0:T(8,128)(2,1)S(1)} %get-tuple-element.108.a_ref), channel_id=1, source_target_pairs={{0,6},{2,4},{4,2},{6,0},{8,14},{10,12},{12,10},{14,8},{16,22},{18,... | collective-permute-start | bytes 73736 | tf_op jit(solution)/shard_map/ppermute | solution.py:482
  38.5 1.0 %collective-permute-start.16 = (bf16[96,128]{1,0:T(8,128)(2,1)S(1)}, bf16[96,128]{1,0:T(8,128)(2,1)S(1)}, u32[]{:S(2)}, u32[]{:S(2)}) collective-permute-start(bf16[96,128]{1,0:T(8,128)(2,1)S(1)} %get-tuple-element.108.a_ref), channel_id=1, source_target_pairs={{0,4},{2,6},{4,0},{6,2},{8,12},{10,14},{12,8},{14,10},{16,20},{18,... | collective-permute-start | bytes 73736 | tf_op jit(solution)/shard_map/ppermute | solution.py:482
  39.5 0.4 collective-permute-start.15
  39.9 0.0 collective-permute-done.10.near_diag_ref
  39.9 0.7 %unpack_quarters.1 = bf16[6,12,2,384]{3,2,1,0:T(2,128)(2,1)} custom-call(bf16[36,384]{1,0:T(8,128)(2,1)S(1)} %get-tuple-element.89.own_ref, bf16[72,384]{1,0:T(8,128)(2,1)S(1)} %collective-permute-done.4.near_ref, bf16[36,384]{1,0:T(8,128)(2,1)S(1)} %collective-permute-done.8.lat_ref, bf16[72,384]{1,0:T(8,128)(2,1)S(1)} %collective-permute-done.10.near_diag_ref), custom_call_target="tpu_custom_call" | custom-call | bytes 4194304 | tf_op jit(solution)/shard_map/unpack_quarters/pallas_call | solution.py:645
  40.6 0.6 %collective-permute-done.17.d_ref = bf16[96,128]{1,0:T(8,128)(2,1)S(1)} collective-permute-done((bf16[96,128]{1,0:T(8,128)(2,1)S(1)}, bf16[96,128]{1,0:T(8,128)(2,1)S(1)}, u32[]{:S(2)}, u32[]{:S(2)}) %collective-permute-start.17) | collective-permute-done | bytes 24608 | tf_op jit(solution)/shard_map/ppermute | solution.py:482
  41.1 1.2 %collective-permute-done.16.c_ref = bf16[96,128]{1,0:T(8,128)(2,1)S(1)} collective-permute-done((bf16[96,128]{1,0:T(8,128)(2,1)S(1)}, bf16[96,128]{1,0:T(8,128)(2,1)S(1)}, u32[]{:S(2)}, u32[]{:S(2)}) %collective-permute-start.16) | collective-permute-done | bytes 24608 | tf_op jit(solution)/shard_map/ppermute | solution.py:482
  42.4 1.0 %collective-permute-done.15.b_ref = bf16[96,128]{1,0:T(8,128)(2,1)S(1)} collective-permute-done((bf16[96,128]{1,0:T(8,128)(2,1)S(1)}, bf16[96,128]{1,0:T(8,128)(2,1)S(1)}, u32[]{:S(2)}, u32[]{:S(2)}) %collective-permute-start.15) | collective-permute-done | bytes 24608 | tf_op jit(solution)/shard_map/ppermute | solution.py:482
  43.4 0.0 collective-permute-done.14.other_weights_ref
  43.4 0.8 %finish.1 = (bf16[24,1152]{1,0:T(8,128)(2,1)}, bf16[24,384]{1,0:T(8,128)(2,1)}, f32[12,1,3312]{2,1,0:T(1,128)}, f32[384]{0:T(512)}) custom-call(bf16[144,128]{1,0:T(8,128)(2,1)S(1)} %get-tuple-element.107.weights_ref, bf16[144,128]{1,0:T(8,128)(2,1)S(1)} %collective-permute-done.14.other_weights_ref, bf16[96,128]{1,0:T(8,128)(2,1)S(1)} %get-tuple-element.108.a_ref, ...), custom_call_target="tpu_custom_call" | custom-call | bytes 524288 | tf_op jit(solution)/shard_map/finish/pallas_call | solution.py:629
  (1 shorter events, 0.0 us)
Async XLA Ops:
  1.8 10.5 %collective-permute-start = (bf16[80,384]{1,0:T(8,128)(2,1)S(1)}, bf16[80,384]{1,0:T(8,128)(2,1)S(1)}, u32[]{:S(2)}, u32[]{:S(2)}) collective-permute-start(bf16[80,384]{1,0:T(8,128)(2,1)S(1)} %get-tuple-element.62), channel_id=1, source_target_pairs={{0,2},{1,3},{2,4},{3,5},{4,6},{5,7},{6,8},{7,9},{8,10},{9,11},{10,... | collective-permute-start | bytes 184328 | tf_op jit(solution)/shard_map/ppermute | solution.py:478
  4.8 7.5 %collective-permute-start.1 = (bf16[72,384]{1,0:T(8,128)(2,1)S(1)}, bf16[72,384]{1,0:T(8,128)(2,1)S(1)}, u32[]{:S(2)}, u32[]{:S(2)}) collective-permute-start(bf16[72,384]{1,0:T(8,128)(2,1)S(1)} %get-tuple-element.63), channel_id=1, source_target_pairs={{0,3},{1,2},{2,5},{3,4},{4,7},{5,6},{6,9},{7,8},{8,11},{9,10},{10,... | collective-permute-start | bytes 165896 | tf_op jit(solution)/shard_map/ppermute | solution.py:478
  5.5 6.9 %collective-permute-start.2 = (bf16[72,384]{1,0:T(8,128)(2,1)S(1)}, bf16[72,384]{1,0:T(8,128)(2,1)S(1)}, u32[]{:S(2)}, u32[]{:S(2)}) collective-permute-start(bf16[72,384]{1,0:T(8,128)(2,1)S(1)} %get-tuple-element.64), channel_id=1, source_target_pairs={{0,1},{1,0},{2,3},{3,2},{4,5},{5,4},{6,7},{7,6},{8,9},{9,8},{10,11... | collective-permute-start | bytes 165896 | tf_op jit(solution)/shard_map/ppermute | solution.py:478
  15.5 2.1 %collective-permute-start.3 = (bf16[2304,128]{1,0:T(8,128)(2,1)S(1)}, bf16[2304,128]{1,0:T(8,128)(2,1)S(1)}, u32[]{:S(2)}, u32[]{:S(2)}) collective-permute-start(bf16[2304,128]{1,0:T(8,128)(2,1)S(1)} %get-tuple-element.71), channel_id=1, source_target_pairs={{0,1},{1,0},{2,3},{3,2},{4,5},{5,4},{6,7},{7,6},{8,9},{9,8},{10,11... | collective-permute-start | bytes 1769480 | tf_op jit(solution)/shard_map/ppermute | solution.py:482
  17.7 8.1 %collective-permute-start.5 = (bf16[656,128]{1,0:T(8,128)(2,1)S(1)}, bf16[656,128]{1,0:T(8,128)(2,1)S(1)}, u32[]{:S(2)}, u32[]{:S(2)}) collective-permute-start(bf16[656,128]{1,0:T(8,128)(2,1)S(1)} %get-tuple-element.91), channel_id=1, source_target_pairs={{0,6},{2,4},{4,2},{6,0},{8,14},{10,12},{12,10},{14,8},{16,22},{18,... | collective-permute-start | bytes 503816 | tf_op jit(solution)/shard_map/ppermute | solution.py:482
  17.8 10.3 %collective-permute-start.6 = (bf16[656,128]{1,0:T(8,128)(2,1)S(1)}, bf16[656,128]{1,0:T(8,128)(2,1)S(1)}, u32[]{:S(2)}, u32[]{:S(2)}) collective-permute-start(bf16[656,128]{1,0:T(8,128)(2,1)S(1)} %get-tuple-element.92), channel_id=1, source_target_pairs={{0,4},{2,6},{4,0},{6,2},{8,12},{10,14},{12,8},{14,10},{16,20},{18,... | collective-permute-start | bytes 503816 | tf_op jit(solution)/shard_map/ppermute | solution.py:482
  17.9 10.2 %collective-permute-start.7 = (bf16[656,128]{1,0:T(8,128)(2,1)S(1)}, bf16[656,128]{1,0:T(8,128)(2,1)S(1)}, u32[]{:S(2)}, u32[]{:S(2)}) collective-permute-start(bf16[656,128]{1,0:T(8,128)(2,1)S(1)} %get-tuple-element.93), channel_id=1, source_target_pairs={{0,2},{2,0},{4,6},{6,4},{8,10},{10,8},{12,14},{14,12},{16,18},{18,... | collective-permute-start | bytes 503816 | tf_op jit(solution)/shard_map/ppermute | solution.py:482
  22.3 2.7 %collective-permute-start.8 = (bf16[36,384]{1,0:T(8,128)(2,1)S(1)}, bf16[36,384]{1,0:T(8,128)(2,1)S(1)}, u32[]{:S(2)}, u32[]{:S(2)}) collective-permute-start(bf16[36,384]{1,0:T(8,128)(2,1)S(1)} %get-tuple-element.95), channel_id=1, source_target_pairs={{0,1},{1,0},{2,3},{3,2},{4,5},{5,4},{6,7},{7,6},{8,9},{9,8},{10,11... | collective-permute-start | bytes 82952 | tf_op jit(solution)/shard_map/ppermute | solution.py:478
  22.4 1.3 %collective-permute-start.9 = (bf16[16,128]{1,0:T(8,128)(2,1)S(1)}, bf16[16,128]{1,0:T(8,128)(2,1)S(1)}, u32[]{:S(2)}, u32[]{:S(2)}) collective-permute-start(bf16[16,128]{1,0:T(8,128)(2,1)S(1)} %get-tuple-element.96.refs_0_), channel_id=1, source_target_pairs={{0,1},{1,0},{2,3},{3,2},{4,5},{5,4},{6,7},{7,6},{8,9},{9,8},{10,11... | collective-permute-start | bytes 12296 | tf_op jit(solution)/shard_map/ppermute | solution.py:482
  23.7 9.0 %collective-permute-start.4 = (bf16[72,384]{1,0:T(8,128)(2,1)S(1)}, bf16[72,384]{1,0:T(8,128)(2,1)S(1)}, u32[]{:S(2)}, u32[]{:S(2)}) collective-permute-start(bf16[72,384]{1,0:T(8,128)(2,1)S(1)} %get-tuple-element.90), channel_id=1, source_target_pairs={{0,30},{1,31},{2,0},{3,1},{4,2},{5,3},{6,4},{7,5},{8,6},{9,7},{10,... | collective-permute-start | bytes 165896 | tf_op jit(solution)/shard_map/ppermute | solution.py:478
  28.2 6.3 %collective-permute-start.11 = (bf16[240,128]{1,0:T(8,128)(2,1)S(1)}, bf16[240,128]{1,0:T(8,128)(2,1)S(1)}, u32[]{:S(2)}, u32[]{:S(2)}) collective-permute-start(bf16[240,128]{1,0:T(8,128)(2,1)S(1)} %get-tuple-element.103), channel_id=1, source_target_pairs={{0,24},{2,26},{4,28},{6,30},{8,16},{10,18},{12,20},{14,22},{16,8},... | collective-permute-start | bytes 184328 | tf_op jit(solution)/shard_map/ppermute | solution.py:482
  30.5 5.7 %collective-permute-start.12 = (bf16[240,128]{1,0:T(8,128)(2,1)S(1)}, bf16[240,128]{1,0:T(8,128)(2,1)S(1)}, u32[]{:S(2)}, u32[]{:S(2)}) collective-permute-start(bf16[240,128]{1,0:T(8,128)(2,1)S(1)} %get-tuple-element.104), channel_id=1, source_target_pairs={{0,16},{2,18},{4,20},{6,22},{8,24},{10,26},{12,28},{14,30},{16,0},... | collective-permute-start | bytes 184328 | tf_op jit(solution)/shard_map/ppermute | solution.py:482
  30.5 5.7 %collective-permute-start.13 = (bf16[240,128]{1,0:T(8,128)(2,1)S(1)}, bf16[240,128]{1,0:T(8,128)(2,1)S(1)}, u32[]{:S(2)}, u32[]{:S(2)}) collective-permute-start(bf16[240,128]{1,0:T(8,128)(2,1)S(1)} %get-tuple-element.105), channel_id=1, source_target_pairs={{0,8},{2,10},{4,12},{6,14},{8,0},{10,2},{12,4},{14,6},{16,24},{18,... | collective-permute-start | bytes 184328 | tf_op jit(solution)/shard_map/ppermute | solution.py:482
  32.6 7.3 %collective-permute-start.10 = (bf16[72,384]{1,0:T(8,128)(2,1)S(1)}, bf16[72,384]{1,0:T(8,128)(2,1)S(1)}, u32[]{:S(2)}, u32[]{:S(2)}) collective-permute-start(bf16[72,384]{1,0:T(8,128)(2,1)S(1)} %collective-permute-done.4.near_ref), channel_id=1, source_target_pairs={{0,1},{1,0},{2,3},{3,2},{4,5},{5,4},{6,7},{7,6},{8,9},{9,8},{10,11... | collective-permute-start | bytes 165896 | tf_op jit(solution)/shard_map/ppermute | solution.py:478
  36.3 7.1 %collective-permute-start.14 = (bf16[144,128]{1,0:T(8,128)(2,1)S(1)}, bf16[144,128]{1,0:T(8,128)(2,1)S(1)}, u32[]{:S(2)}, u32[]{:S(2)}) collective-permute-start(bf16[144,128]{1,0:T(8,128)(2,1)S(1)} %get-tuple-element.107.weights_ref), channel_id=1, source_target_pairs={{0,1},{1,0},{2,3},{3,2},{4,5},{5,4},{6,7},{7,6},{8,9},{9,8},{10,11... | collective-permute-start | bytes 110600 | tf_op jit(solution)/shard_map/ppermute | solution.py:482
  36.4 4.8 %collective-permute-start.17 = (bf16[96,128]{1,0:T(8,128)(2,1)S(1)}, bf16[96,128]{1,0:T(8,128)(2,1)S(1)}, u32[]{:S(2)}, u32[]{:S(2)}) collective-permute-start(bf16[96,128]{1,0:T(8,128)(2,1)S(1)} %get-tuple-element.108.a_ref), channel_id=1, source_target_pairs={{0,6},{2,4},{4,2},{6,0},{8,14},{10,12},{12,10},{14,8},{16,22},{18,... | collective-permute-start | bytes 73736 | tf_op jit(solution)/shard_map/ppermute | solution.py:482
  38.5 3.8 %collective-permute-start.16 = (bf16[96,128]{1,0:T(8,128)(2,1)S(1)}, bf16[96,128]{1,0:T(8,128)(2,1)S(1)}, u32[]{:S(2)}, u32[]{:S(2)}) collective-permute-start(bf16[96,128]{1,0:T(8,128)(2,1)S(1)} %get-tuple-element.108.a_ref), channel_id=1, source_target_pairs={{0,4},{2,6},{4,0},{6,2},{8,12},{10,14},{12,8},{14,10},{16,20},{18,... | collective-permute-start | bytes 73736 | tf_op jit(solution)/shard_map/ppermute | solution.py:482
  39.5 3.8 %collective-permute-start.15 = (bf16[96,128]{1,0:T(8,128)(2,1)S(1)}, bf16[96,128]{1,0:T(8,128)(2,1)S(1)}, u32[]{:S(2)}, u32[]{:S(2)}) collective-permute-start(bf16[96,128]{1,0:T(8,128)(2,1)S(1)} %get-tuple-element.108.a_ref), channel_id=1, source_target_pairs={{0,2},{2,0},{4,6},{6,4},{8,10},{10,8},{12,14},{14,12},{16,18},{18,... | collective-permute-start | bytes 73736 | tf_op jit(solution)/shard_map/ppermute | solution.py:482

commit v5 on v4

--- a/solution.py
+++ b/solution.py
@@ -346,7 +346,7 @@
 def fold_kernel(packet, scores_ref, lanes_ref, rows_ref, out_ref, wide, table, flat):
     wide[...] = jnp.zeros(wide.shape, f32)
     table[...] = jnp.zeros(table.shape, f32)
-    flat[...] = jnp.zeros(flat.shape, f32)
+    flat[...] = jnp.zeros(flat.shape, bf16)
     for head in range(HEADS):
         wide[head % 2, :, :CELLS] = scores_ref[head].astype(f32)
         total = wide[head % 2, :PLANE, :]
@@ -354,13 +354,13 @@
             total = pltpu.roll(total, PLANE, 1) + wide[head % 2, PLANE * col : PLANE * (col + 1), :]
         table[16 * head : 16 * head + PLANE, :] = total
     moved = nn_dot(rows_ref[...], table[...].astype(bf16)).astype(bf16)
-    moved = nt_dot(moved, lanes_ref[...])
+    moved = nt_dot(moved, lanes_ref[...]).astype(bf16)
     reach = SPAN // PLANE
     for first, plane_i, plane_j in segments():
-        flat[:HEADS, first : first + reach] = moved[
-            16 * plane_j : 16 * plane_j + HEADS, reach * plane_i : reach * (plane_i + 1)
-        ]
-    tiles = [flat[:HEADS, tile * LANES : (tile + 1) * LANES] for tile in range(packet.table_tiles)]
+        flat[:, first : first + reach] = moved[16 * plane_j : 16 * (plane_j + 1), reach * plane_i : reach * (plane_i + 1)]
+    tiles = [
+        flat[:, tile * LANES : (tile + 1) * LANES].astype(f32)[:HEADS] for tile in range(packet.table_tiles)
+    ]
     tiles.append(jnp.zeros((packet.table_size - packet.table_rows, LANES), f32))
     out_ref[...] = jnp.concatenate(tiles, axis=0).astype(bf16)
 
@@ -406,22 +406,7 @@
     table_ref[...] = summed(refs, slice(packet.weight_size, packet.weight_size + packet.quarter + 16))
 
 
-def finish_kernel(
-    packet,
-    table_scale,
-    factor,
-    weights_ref,
-    other_weights_ref,
-    a_ref,
-    b_ref,
-    c_ref,
-    d_ref,
-    grad_in_ref,
-    grad_out_ref,
-    grad_table_ref,
-    grad_gain_ref,
-    quarters,
-):
+def weights_out_kernel(packet, factor, weights_ref, other_weights_ref, grad_in_ref, grad_out_ref):
     odd = lax.rem(lax.axis_index("lat"), 2) == 1
     own, other = weights_ref[...].astype(f32) * factor, other_weights_ref[...].astype(f32) * factor
     halves = (jnp.where(odd, other, own), jnp.where(odd, own, other))
@@ -430,6 +415,8 @@
     grad_in_ref[...] = jnp.concatenate(tiles[:9], axis=1).astype(bf16)
     grad_out_ref[...] = jnp.concatenate(tiles[9:], axis=1).astype(bf16)
 
+
+def table_out_kernel(packet, table_scale, factor, a_ref, b_ref, c_ref, d_ref, grad_table_ref, grad_gain_ref, quarters):
     low = lax.rem(lax.axis_index("lon"), 4)
     parts = (a_ref, b_ref, c_ref, d_ref)
     for step, ref in enumerate(parts):
@@ -567,7 +554,7 @@
         [
             pltpu.VMEM((2, CELLS, WIDE), f32),
             pltpu.VMEM((HEADS * 16, WIDE), f32),
-            pltpu.VMEM((16, packet.table_tiles * LANES), f32),
+            pltpu.VMEM((16, packet.table_tiles * LANES), bf16),
         ],
         moved=1 << 21,
     )(scores_low, lane_moves, row_moves)
@@ -626,19 +613,22 @@
 
     cells_in_all = latent_field.shape[0] * latent_field.shape[1] * latent_field.shape[2]
     factor = 1.0 / math.sqrt(cells_in_all * lon_count * lat_count)
-    grad_input_weight, grad_output_weight, grad_table, gain_sum = call(
-        functools.partial(finish_kernel, packet, math.sqrt(head_dim), factor),
-        "finish",
-        whole(6),
-        [
-            struct((packet.weight_rows, 3 * features), bf16),
-            struct((packet.weight_rows, features), bf16),
-            struct((HEADS, 1, PLANE * SPAN), f32),
-            struct((features,), f32),
-        ],
+    grad_input_weight, grad_output_weight = call(
+        functools.partial(weights_out_kernel, packet, factor),
+        "weights_out",
+        whole(2),
+        [struct((packet.weight_rows, 3 * features), bf16), struct((packet.weight_rows, features), bf16)],
+        moved=1 << 18,
+    )(weight_sum, weight_other)
+    table_parts, grad_input_weight = lax.optimization_barrier((table_parts, grad_input_weight))
+    grad_table, gain_sum = call(
+        functools.partial(table_out_kernel, packet, math.sqrt(head_dim), factor),
+        "table_out",
+        whole(4),
+        [struct((HEADS, 1, PLANE * SPAN), f32), struct((features,), f32)],
         [pltpu.VMEM((4, packet.quarter, LANES), f32)],
         moved=1 << 19,
-    )(weight_sum, weight_other, *table_parts)
+    )(*table_parts)
     for bit in range(1, lat_count.bit_length() - 1):
         gain_sum = gain_sum + swap(gain_sum, "lat", 1 << bit)
 

time: 44.3 us -> 44.1 us (level)
  waiting for transfers between devices: 14 us -> 13.3 us
  Pallas kernels: 11.2 us -> 11.8 us
    ppermute x12, waiting for transfers between devices: 10.4 us -> 9.62 us  [swap(): lax.ppermute(value, axis, [(source, source ^ mask) for source in range(co...]
    pallas_call x1 -> x2, Pallas kernels: 0.79 us -> 1.42 us  [the longest x1 0.78 us: on_device(): call(functools.partial(table_out_kernel, packet, math.sqrt(head_dim), fac...]
  transfers between devices with their start and end apart: 18 -> 18, of which waited for: 10 -> 9; matrix products, arithmetic and copies ran while one was open for 0% -> 0% of each run, Pallas kernels for 13% -> 15%
where the time goes in v5:
time: 44.1 us; the launch traced here: 44 us
  starting transfers between devices  18.2 us (41%)
  waiting for transfers between devices  13.3 us (30%)
  Pallas kernels  11.8 us (27%)
  between operations  0.73 us (2%)
    ppermute x12, starting transfers between devices, swap(): lax.ppermute(value, axis, [(source, source ^ mask) for source in range(co...  12.2 us
    ppermute x12, waiting for transfers between devices, swap(): lax.ppermute(value, axis, [(source, source ^ mask) for source in range(co...  9.62 us
    ppermute x6, starting transfers between devices, move(): return lax.ppermute(value, ('lon', 'lat'), pairs)  6 us
    ppermute x6, waiting for transfers between devices, move(): return lax.ppermute(value, ('lon', 'lat'), pairs)  3.65 us
    pallas_call x1, Pallas kernels, on_device(): call(functools.partial(window_kernel, packet), 'window', whole(10), [half...  3.17 us
    pallas_call x1, Pallas kernels, on_device(): call(bias_kernel, 'expand_bias', whole(1) + [hbm] * 2, [struct((HEADS, CE...  2.25 us
    pallas_call x1, Pallas kernels, on_device(): call(functools.partial(fold_kernel, packet), 'fold_table', whole(3), stru...  1.84 us
    pallas_call x1, Pallas kernels, on_device(): call(load_kernel, 'load', [hbm] * 5, [others, same, others, others] + [st...  1.18 us
  transfers between devices with their start and end apart: 18, of which 9 were waited for; matrix products, arithmetic and copies ran while one was open for 0% of the time, Pallas kernels for 15%

profile of v5, /device:TPU:0, one launch (start us, length us, event | category | flops | bytes accessed | tf_op | source)
XLA Modules:
  0.0 44.0 jit_solution(17078648317952469979)
XLA Ops:
  0.6 1.2 %load.1 = (bf16[72,384]{1,0:T(8,128)(2,1)S(1)}, bf16[80,384]{1,0:T(8,128)(2,1)S(1)}, bf16[72,384]{1,0:T(8,128)(2,1)S(1)}, bf16[72,384]{1,0:T(8,128)(2,1)S(1)}, b...) custom-call(bf16[6,12,2,384]{3,2,1,0:T(2,128)(2,1)} %bitcast.7, bf16[6,12,2,384]{3,2,1,0:T(2,128)(2,1)} %bitcast.8, ...), custom_call_target="tpu_custom_call" | custom-call | bytes 1048576 | tf_op jit(solution)/shard_map/load/pallas_call | solution.py:482
  1.8 3.0 %collective-permute-start = (bf16[80,384]{1,0:T(8,128)(2,1)S(1)}, bf16[80,384]{1,0:T(8,128)(2,1)S(1)}, u32[]{:S(2)}, u32[]{:S(2)}) collective-permute-start(bf16[80,384]{1,0:T(8,128)(2,1)S(1)} %get-tuple-element.67), channel_id=1, source_target_pairs={{0,2},{1,3},{2,4},{3,5},{4,6},{5,7},{6,8},{7,9},{8,10},{9,11},{10,... | collective-permute-start | bytes 184328 | tf_op jit(solution)/shard_map/ppermute | solution.py:465
  4.8 0.7 %collective-permute-start.1 = (bf16[72,384]{1,0:T(8,128)(2,1)S(1)}, bf16[72,384]{1,0:T(8,128)(2,1)S(1)}, u32[]{:S(2)}, u32[]{:S(2)}) collective-permute-start(bf16[72,384]{1,0:T(8,128)(2,1)S(1)} %get-tuple-element.68), channel_id=1, source_target_pairs={{0,3},{1,2},{2,5},{3,4},{4,7},{5,6},{6,9},{7,8},{8,11},{9,10},{10,... | collective-permute-start | bytes 165896 | tf_op jit(solution)/shard_map/ppermute | solution.py:465
  5.5 1.0 %collective-permute-start.2 = (bf16[72,384]{1,0:T(8,128)(2,1)S(1)}, bf16[72,384]{1,0:T(8,128)(2,1)S(1)}, u32[]{:S(2)}, u32[]{:S(2)}) collective-permute-start(bf16[72,384]{1,0:T(8,128)(2,1)S(1)} %get-tuple-element.69), channel_id=1, source_target_pairs={{0,1},{1,0},{2,3},{3,2},{4,5},{5,4},{6,7},{7,6},{8,9},{9,8},{10,11... | collective-permute-start | bytes 165896 | tf_op jit(solution)/shard_map/ppermute | solution.py:465
  6.4 2.3 %expand_bias.1 = (bf16[12,144,144]{2,1,0:T(8,128)(2,1)S(1)}, bf16[384,384]{1,0:T(8,128)(2,1)S(1)}, bf16[384,384]{1,0:T(8,128)(2,1)S(1)}, bf16[192,192]{1,0:T(8,1...) custom-call(bf16[12,3312]{1,0:T(8,128)(2,1)S(1)} %get-tuple-element., ...), custom_call_target="tpu_custom_call" | custom-call | bytes 2097152 | tf_op jit(solution)/shard_map/expand_bias/pallas_call | solution.py:494
  8.7 3.6 %collective-permute-done.1.near_diag_ref = bf16[72,384]{1,0:T(8,128)(2,1)S(1)} collective-permute-done((bf16[72,384]{1,0:T(8,128)(2,1)S(1)}, bf16[72,384]{1,0:T(8,128)(2,1)S(1)}, u32[]{:S(2)}, u32[]{:S(2)}) %collective-permute-start.1) | collective-permute-done | bytes 55328 | tf_op jit(solution)/shard_map/ppermute | solution.py:465
  12.3 0.0 collective-permute-done.2.lat_ref
  12.3 0.0 collective-permute-done.near_ref
  12.3 3.2 %window.1 = (bf16[2304,128]{1,0:T(8,128)(2,1)S(1)}, bf16[2304,128]{1,0:T(8,128)(2,1)S(1)}, bf16[12,144,144]{2,1,0:T(8,128)(2,1)S(1)}, bf16[4,384,144]{2,1,0:T(8,...) custom-call(bf16[72,384]{1,0:T(8,128)(2,1)S(1)} %get-tuple-element.66.own_ref, ...), custom_call_target="tpu_custom_call" | custom-call | flops 1000000000 | bytes 5242880 | tf_op jit(solution)/shard_map/window/pallas_call | solution.py:518
  15.5 0.1 collective-permute-start.3
  15.6 1.8 %fold_table.1.table_ref = bf16[320,128]{1,0:T(8,128)(2,1)S(1)} custom-call(bf16[12,144,144]{2,1,0:T(8,128)(2,1)S(1)} %get-tuple-element.77.scores_ref, bf16[384,384]{1,0:T(8,128)(2,1)S(1)} %get-tuple-element.78.lanes_ref, bf16[192,192]{1,0:T(8,128)(2,1)S(1)} %get-tuple-element.79.rows_ref), custom_call_target="tpu_custom_call" | custom-call | bytes 2097152 | tf_op jit(solution)/shard_map/fold_table/pallas_call | solution.py:549
  17.4 0.1 collective-permute-done.3.recv_ref
  17.6 0.1 add_lat.1
  17.7 0.1 collective-permute-start.5
  17.8 0.1 collective-permute-start.6
  17.9 3.4 %collective-permute-start.7 = (bf16[656,128]{1,0:T(8,128)(2,1)S(1)}, bf16[656,128]{1,0:T(8,128)(2,1)S(1)}, u32[]{:S(2)}, u32[]{:S(2)}) collective-permute-start(bf16[656,128]{1,0:T(8,128)(2,1)S(1)} %get-tuple-element.98), channel_id=1, source_target_pairs={{0,2},{2,0},{4,6},{6,4},{8,10},{10,8},{12,14},{14,12},{16,18},{18,... | collective-permute-start | bytes 503816 | tf_op jit(solution)/shard_map/ppermute | solution.py:469
  21.3 1.0 %grad_field.1 = (bf16[36,384]{1,0:T(8,128)(2,1)S(1)}, bf16[72,384]{1,0:T(8,128)(2,1)S(1)}, bf16[36,384]{1,0:T(8,128)(2,1)S(1)}, bf16[16,128]{1,0:T(8,128)(2,1)S(1)}) custom-call(bf16[384,1152]{1,0:T(8,128)(2,1)S(1)} %get-tuple-element.65.win_ref, bf16[4,384,144]{2,1,0:T(8,128)(2,1)S(1)} %get-tuple-element.88.grad_projected_ref, ...), custom_call_target="tpu_custom_call" | custom-call | flops 100000000 | bytes 5242880 | tf_op jit(solution)/shard_map/grad_field/pallas_call | solution.py:577
  22.3 0.1 collective-permute-start.8
  22.4 0.5 %collective-permute-start.9 = (bf16[16,128]{1,0:T(8,128)(2,1)S(1)}, bf16[16,128]{1,0:T(8,128)(2,1)S(1)}, u32[]{:S(2)}, u32[]{:S(2)}) collective-permute-start(bf16[16,128]{1,0:T(8,128)(2,1)S(1)} %get-tuple-element.101.refs_0_), channel_id=1, source_target_pairs={{0,1},{1,0},{2,3},{3,2},{4,5},{5,4},{6,7},{7,6},{8,9},{9,8},{10,11... | collective-permute-start | bytes 12296 | tf_op jit(solution)/shard_map/ppermute | solution.py:469
  22.9 0.8 %collective-permute-done.9.refs_1_ = bf16[16,128]{1,0:T(8,128)(2,1)S(1)} collective-permute-done((bf16[16,128]{1,0:T(8,128)(2,1)S(1)}, bf16[16,128]{1,0:T(8,128)(2,1)S(1)}, u32[]{:S(2)}, u32[]{:S(2)}) %collective-permute-start.9) | collective-permute-done | bytes 4128 | tf_op jit(solution)/shard_map/ppermute | solution.py:469
  23.7 1.3 %collective-permute-start.4 = (bf16[72,384]{1,0:T(8,128)(2,1)S(1)}, bf16[72,384]{1,0:T(8,128)(2,1)S(1)}, u32[]{:S(2)}, u32[]{:S(2)}) collective-permute-start(bf16[72,384]{1,0:T(8,128)(2,1)S(1)} %get-tuple-element.95), channel_id=1, source_target_pairs={{0,30},{1,31},{2,0},{3,1},{4,2},{5,3},{6,4},{7,5},{8,6},{9,7},{10,... | collective-permute-start | bytes 165896 | tf_op jit(solution)/shard_map/ppermute | solution.py:465
  25.0 0.0 collective-permute-done.8.lat_ref
  25.0 0.8 %collective-permute-done.5.refs_2_ = bf16[656,128]{1,0:T(8,128)(2,1)S(1)} collective-permute-done((bf16[656,128]{1,0:T(8,128)(2,1)S(1)}, bf16[656,128]{1,0:T(8,128)(2,1)S(1)}, u32[]{:S(2)}, u32[]{:S(2)}) %collective-permute-start.5) | collective-permute-done | bytes 167968 | tf_op jit(solution)/shard_map/ppermute | solution.py:469
  25.8 2.2 %collective-permute-done.6.refs_3_ = bf16[656,128]{1,0:T(8,128)(2,1)S(1)} collective-permute-done((bf16[656,128]{1,0:T(8,128)(2,1)S(1)}, bf16[656,128]{1,0:T(8,128)(2,1)S(1)}, u32[]{:S(2)}, u32[]{:S(2)}) %collective-permute-start.6) | collective-permute-done | bytes 167968 | tf_op jit(solution)/shard_map/ppermute | solution.py:469
  28.0 0.0 collective-permute-done.7.refs_4_
  28.0 0.1 add_lon.1
  28.1 2.4 %collective-permute-start.11 = (bf16[240,128]{1,0:T(8,128)(2,1)S(1)}, bf16[240,128]{1,0:T(8,128)(2,1)S(1)}, u32[]{:S(2)}, u32[]{:S(2)}) collective-permute-start(bf16[240,128]{1,0:T(8,128)(2,1)S(1)} %get-tuple-element.108), channel_id=1, source_target_pairs={{0,24},{2,26},{4,28},{6,30},{8,16},{10,18},{12,20},{14,22},{16,8},... | collective-permute-start | bytes 184328 | tf_op jit(solution)/shard_map/ppermute | solution.py:469
  30.6 0.0 collective-permute-start.12
  30.6 2.0 %collective-permute-start.13 = (bf16[240,128]{1,0:T(8,128)(2,1)S(1)}, bf16[240,128]{1,0:T(8,128)(2,1)S(1)}, u32[]{:S(2)}, u32[]{:S(2)}) collective-permute-start(bf16[240,128]{1,0:T(8,128)(2,1)S(1)} %get-tuple-element.110), channel_id=1, source_target_pairs={{0,8},{2,10},{4,12},{6,14},{8,0},{10,2},{12,4},{14,6},{16,24},{18,... | collective-permute-start | bytes 184328 | tf_op jit(solution)/shard_map/ppermute | solution.py:469
  32.6 0.0 collective-permute-done.4.near_ref
  32.6 0.0 collective-permute-start.10
  32.6 2.0 %collective-permute-done.11.a_ref = bf16[240,128]{1,0:T(8,128)(2,1)S(1)} collective-permute-done((bf16[240,128]{1,0:T(8,128)(2,1)S(1)}, bf16[240,128]{1,0:T(8,128)(2,1)S(1)}, u32[]{:S(2)}, u32[]{:S(2)}) %collective-permute-start.11) | collective-permute-done | bytes 61472 | tf_op jit(solution)/shard_map/ppermute | solution.py:469
  34.6 1.6 %collective-permute-done.12.b_ref = bf16[240,128]{1,0:T(8,128)(2,1)S(1)} collective-permute-done((bf16[240,128]{1,0:T(8,128)(2,1)S(1)}, bf16[240,128]{1,0:T(8,128)(2,1)S(1)}, u32[]{:S(2)}, u32[]{:S(2)}) %collective-permute-start.12) | collective-permute-done | bytes 61472 | tf_op jit(solution)/shard_map/ppermute | solution.py:469
  36.1 0.0 collective-permute-done.13.c_ref
  36.2 0.1 collective-permute-start.17
  36.3 2.2 %collective-permute-start.16 = (bf16[96,128]{1,0:T(8,128)(2,1)S(1)}, bf16[96,128]{1,0:T(8,128)(2,1)S(1)}, u32[]{:S(2)}, u32[]{:S(2)}) collective-permute-start(bf16[96,128]{1,0:T(8,128)(2,1)S(1)} %get-tuple-element.117.a_ref), channel_id=1, source_target_pairs={{0,6},{2,4},{4,2},{6,0},{8,14},{10,12},{12,10},{14,8},{16,22},{18,... | collective-permute-start | bytes 73736 | tf_op jit(solution)/shard_map/ppermute | solution.py:469
  38.5 0.9 %collective-permute-start.15 = (bf16[96,128]{1,0:T(8,128)(2,1)S(1)}, bf16[96,128]{1,0:T(8,128)(2,1)S(1)}, u32[]{:S(2)}, u32[]{:S(2)}) collective-permute-start(bf16[96,128]{1,0:T(8,128)(2,1)S(1)} %get-tuple-element.117.a_ref), channel_id=1, source_target_pairs={{0,4},{2,6},{4,0},{6,2},{8,12},{10,14},{12,8},{14,10},{16,20},{18,... | collective-permute-start | bytes 73736 | tf_op jit(solution)/shard_map/ppermute | solution.py:469
  39.4 0.4 collective-permute-start.14
  39.8 0.0 collective-permute-done.10.near_diag_ref
  39.8 0.7 %unpack_quarters.1 = bf16[6,12,2,384]{3,2,1,0:T(2,128)(2,1)} custom-call(bf16[36,384]{1,0:T(8,128)(2,1)S(1)} %get-tuple-element.94.own_ref, bf16[72,384]{1,0:T(8,128)(2,1)S(1)} %collective-permute-done.4.near_ref, bf16[36,384]{1,0:T(8,128)(2,1)S(1)} %collective-permute-done.8.lat_ref, bf16[72,384]{1,0:T(8,128)(2,1)S(1)} %collective-permute-done.10.near_diag_ref), custom_call_target="tpu_custom_call" | custom-call | bytes 4194304 | tf_op jit(solution)/shard_map/unpack_quarters/pallas_call | solution.py:635
  40.5 0.0 collective-permute-done.17.other_weights_ref
  40.5 0.6 %weights_out.1 = (bf16[24,1152]{1,0:T(8,128)(2,1)}, bf16[24,384]{1,0:T(8,128)(2,1)}) custom-call(bf16[144,128]{1,0:T(8,128)(2,1)S(1)} %get-tuple-element.113.weights_ref, bf16[144,128]{1,0:T(8,128)(2,1)S(1)} %collective-permute-done.17.other_weights_ref), custom_call_target="tpu_custom_call" | custom-call | bytes 262144 | tf_op jit(solution)/shard_map/weights_out/pallas_call | solution.py:616
  41.1 0.0 collective-permute-done.16.d_ref
  41.1 1.2 %collective-permute-done.15.c_ref = bf16[96,128]{1,0:T(8,128)(2,1)S(1)} collective-permute-done((bf16[96,128]{1,0:T(8,128)(2,1)S(1)}, bf16[96,128]{1,0:T(8,128)(2,1)S(1)}, u32[]{:S(2)}, u32[]{:S(2)}) %collective-permute-start.15) | collective-permute-done | bytes 24608 | tf_op jit(solution)/shard_map/ppermute | solution.py:469
  42.3 0.9 %collective-permute-done.14.b_ref = bf16[96,128]{1,0:T(8,128)(2,1)S(1)} collective-permute-done((bf16[96,128]{1,0:T(8,128)(2,1)S(1)}, bf16[96,128]{1,0:T(8,128)(2,1)S(1)}, u32[]{:S(2)}, u32[]{:S(2)}) %collective-permute-start.14) | collective-permute-done | bytes 24608 | tf_op jit(solution)/shard_map/ppermute | solution.py:469
  43.2 0.8 %table_out.1 = (f32[12,1,3312]{2,1,0:T(1,128)}, f32[384]{0:T(512)}) custom-call(bf16[96,128]{1,0:T(8,128)(2,1)S(1)} %get-tuple-element.117.a_ref, bf16[96,128]{1,0:T(8,128)(2,1)S(1)} %collective-permute-done.14.b_ref, bf16[96,128]{1,0:T(8,128)(2,1)S(1)} %collective-permute-done.15.c_ref, bf16[96,128]{1,0:T(8,128)(2,1)S(1)} %collective-permute-done.16.d_ref), custom_call_target="tpu_custom_call" | custom-call | bytes 524288 | tf_op jit(solution)/shard_map/table_out/pallas_call | solution.py:624
  (1 shorter events, 0.0 us)
Async XLA Ops:
  1.8 10.5 %collective-permute-start = (bf16[80,384]{1,0:T(8,128)(2,1)S(1)}, bf16[80,384]{1,0:T(8,128)(2,1)S(1)}, u32[]{:S(2)}, u32[]{:S(2)}) collective-permute-start(bf16[80,384]{1,0:T(8,128)(2,1)S(1)} %get-tuple-element.67), channel_id=1, source_target_pairs={{0,2},{1,3},{2,4},{3,5},{4,6},{5,7},{6,8},{7,9},{8,10},{9,11},{10,... | collective-permute-start | bytes 184328 | tf_op jit(solution)/shard_map/ppermute | solution.py:465
  4.8 7.5 %collective-permute-start.1 = (bf16[72,384]{1,0:T(8,128)(2,1)S(1)}, bf16[72,384]{1,0:T(8,128)(2,1)S(1)}, u32[]{:S(2)}, u32[]{:S(2)}) collective-permute-start(bf16[72,384]{1,0:T(8,128)(2,1)S(1)} %get-tuple-element.68), channel_id=1, source_target_pairs={{0,3},{1,2},{2,5},{3,4},{4,7},{5,6},{6,9},{7,8},{8,11},{9,10},{10,... | collective-permute-start | bytes 165896 | tf_op jit(solution)/shard_map/ppermute | solution.py:465
  5.5 6.9 %collective-permute-start.2 = (bf16[72,384]{1,0:T(8,128)(2,1)S(1)}, bf16[72,384]{1,0:T(8,128)(2,1)S(1)}, u32[]{:S(2)}, u32[]{:S(2)}) collective-permute-start(bf16[72,384]{1,0:T(8,128)(2,1)S(1)} %get-tuple-element.69), channel_id=1, source_target_pairs={{0,1},{1,0},{2,3},{3,2},{4,5},{5,4},{6,7},{7,6},{8,9},{9,8},{10,11... | collective-permute-start | bytes 165896 | tf_op jit(solution)/shard_map/ppermute | solution.py:465
  15.5 2.1 %collective-permute-start.3 = (bf16[2304,128]{1,0:T(8,128)(2,1)S(1)}, bf16[2304,128]{1,0:T(8,128)(2,1)S(1)}, u32[]{:S(2)}, u32[]{:S(2)}) collective-permute-start(bf16[2304,128]{1,0:T(8,128)(2,1)S(1)} %get-tuple-element.76), channel_id=1, source_target_pairs={{0,1},{1,0},{2,3},{3,2},{4,5},{5,4},{6,7},{7,6},{8,9},{9,8},{10,11... | collective-permute-start | bytes 1769480 | tf_op jit(solution)/shard_map/ppermute | solution.py:469
  17.7 8.1 %collective-permute-start.5 = (bf16[656,128]{1,0:T(8,128)(2,1)S(1)}, bf16[656,128]{1,0:T(8,128)(2,1)S(1)}, u32[]{:S(2)}, u32[]{:S(2)}) collective-permute-start(bf16[656,128]{1,0:T(8,128)(2,1)S(1)} %get-tuple-element.96), channel_id=1, source_target_pairs={{0,6},{2,4},{4,2},{6,0},{8,14},{10,12},{12,10},{14,8},{16,22},{18,... | collective-permute-start | bytes 503816 | tf_op jit(solution)/shard_map/ppermute | solution.py:469
  17.8 10.2 %collective-permute-start.6 = (bf16[656,128]{1,0:T(8,128)(2,1)S(1)}, bf16[656,128]{1,0:T(8,128)(2,1)S(1)}, u32[]{:S(2)}, u32[]{:S(2)}) collective-permute-start(bf16[656,128]{1,0:T(8,128)(2,1)S(1)} %get-tuple-element.97), channel_id=1, source_target_pairs={{0,4},{2,6},{4,0},{6,2},{8,12},{10,14},{12,8},{14,10},{16,20},{18,... | collective-permute-start | bytes 503816 | tf_op jit(solution)/shard_map/ppermute | solution.py:469
  17.9 10.2 %collective-permute-start.7 = (bf16[656,128]{1,0:T(8,128)(2,1)S(1)}, bf16[656,128]{1,0:T(8,128)(2,1)S(1)}, u32[]{:S(2)}, u32[]{:S(2)}) collective-permute-start(bf16[656,128]{1,0:T(8,128)(2,1)S(1)} %get-tuple-element.98), channel_id=1, source_target_pairs={{0,2},{2,0},{4,6},{6,4},{8,10},{10,8},{12,14},{14,12},{16,18},{18,... | collective-permute-start | bytes 503816 | tf_op jit(solution)/shard_map/ppermute | solution.py:469
  22.3 2.7 %collective-permute-start.8 = (bf16[36,384]{1,0:T(8,128)(2,1)S(1)}, bf16[36,384]{1,0:T(8,128)(2,1)S(1)}, u32[]{:S(2)}, u32[]{:S(2)}) collective-permute-start(bf16[36,384]{1,0:T(8,128)(2,1)S(1)} %get-tuple-element.100), channel_id=1, source_target_pairs={{0,1},{1,0},{2,3},{3,2},{4,5},{5,4},{6,7},{7,6},{8,9},{9,8},{10,11... | collective-permute-start | bytes 82952 | tf_op jit(solution)/shard_map/ppermute | solution.py:465
  22.4 1.3 %collective-permute-start.9 = (bf16[16,128]{1,0:T(8,128)(2,1)S(1)}, bf16[16,128]{1,0:T(8,128)(2,1)S(1)}, u32[]{:S(2)}, u32[]{:S(2)}) collective-permute-start(bf16[16,128]{1,0:T(8,128)(2,1)S(1)} %get-tuple-element.101.refs_0_), channel_id=1, source_target_pairs={{0,1},{1,0},{2,3},{3,2},{4,5},{5,4},{6,7},{7,6},{8,9},{9,8},{10,11... | collective-permute-start | bytes 12296 | tf_op jit(solution)/shard_map/ppermute | solution.py:469
  23.7 8.9 %collective-permute-start.4 = (bf16[72,384]{1,0:T(8,128)(2,1)S(1)}, bf16[72,384]{1,0:T(8,128)(2,1)S(1)}, u32[]{:S(2)}, u32[]{:S(2)}) collective-permute-start(bf16[72,384]{1,0:T(8,128)(2,1)S(1)} %get-tuple-element.95), channel_id=1, source_target_pairs={{0,30},{1,31},{2,0},{3,1},{4,2},{5,3},{6,4},{7,5},{8,6},{9,7},{10,... | collective-permute-start | bytes 165896 | tf_op jit(solution)/shard_map/ppermute | solution.py:465
  28.1 6.4 %collective-permute-start.11 = (bf16[240,128]{1,0:T(8,128)(2,1)S(1)}, bf16[240,128]{1,0:T(8,128)(2,1)S(1)}, u32[]{:S(2)}, u32[]{:S(2)}) collective-permute-start(bf16[240,128]{1,0:T(8,128)(2,1)S(1)} %get-tuple-element.108), channel_id=1, source_target_pairs={{0,24},{2,26},{4,28},{6,30},{8,16},{10,18},{12,20},{14,22},{16,8},... | collective-permute-start | bytes 184328 | tf_op jit(solution)/shard_map/ppermute | solution.py:469
  30.6 5.6 %collective-permute-start.12 = (bf16[240,128]{1,0:T(8,128)(2,1)S(1)}, bf16[240,128]{1,0:T(8,128)(2,1)S(1)}, u32[]{:S(2)}, u32[]{:S(2)}) collective-permute-start(bf16[240,128]{1,0:T(8,128)(2,1)S(1)} %get-tuple-element.109), channel_id=1, source_target_pairs={{0,16},{2,18},{4,20},{6,22},{8,24},{10,26},{12,28},{14,30},{16,0},... | collective-permute-start | bytes 184328 | tf_op jit(solution)/shard_map/ppermute | solution.py:469
  30.6 5.6 %collective-permute-start.13 = (bf16[240,128]{1,0:T(8,128)(2,1)S(1)}, bf16[240,128]{1,0:T(8,128)(2,1)S(1)}, u32[]{:S(2)}, u32[]{:S(2)}) collective-permute-start(bf16[240,128]{1,0:T(8,128)(2,1)S(1)} %get-tuple-element.110), channel_id=1, source_target_pairs={{0,8},{2,10},{4,12},{6,14},{8,0},{10,2},{12,4},{14,6},{16,24},{18,... | collective-permute-start | bytes 184328 | tf_op jit(solution)/shard_map/ppermute | solution.py:469
  32.6 7.2 %collective-permute-start.10 = (bf16[72,384]{1,0:T(8,128)(2,1)S(1)}, bf16[72,384]{1,0:T(8,128)(2,1)S(1)}, u32[]{:S(2)}, u32[]{:S(2)}) collective-permute-start(bf16[72,384]{1,0:T(8,128)(2,1)S(1)} %collective-permute-done.4.near_ref), channel_id=1, source_target_pairs={{0,1},{1,0},{2,3},{3,2},{4,5},{5,4},{6,7},{7,6},{8,9},{9,8},{10,11... | collective-permute-start | bytes 165896 | tf_op jit(solution)/shard_map/ppermute | solution.py:465
  36.2 4.3 %collective-permute-start.17 = (bf16[144,128]{1,0:T(8,128)(2,1)S(1)}, bf16[144,128]{1,0:T(8,128)(2,1)S(1)}, u32[]{:S(2)}, u32[]{:S(2)}) collective-permute-start(bf16[144,128]{1,0:T(8,128)(2,1)S(1)} %get-tuple-element.113.weights_ref), channel_id=1, source_target_pairs={{0,1},{1,0},{2,3},{3,2},{4,5},{5,4},{6,7},{7,6},{8,9},{9,8},{10,11... | collective-permute-start | bytes 110600 | tf_op jit(solution)/shard_map/ppermute | solution.py:469
  36.3 4.9 %collective-permute-start.16 = (bf16[96,128]{1,0:T(8,128)(2,1)S(1)}, bf16[96,128]{1,0:T(8,128)(2,1)S(1)}, u32[]{:S(2)}, u32[]{:S(2)}) collective-permute-start(bf16[96,128]{1,0:T(8,128)(2,1)S(1)} %get-tuple-element.117.a_ref), channel_id=1, source_target_pairs={{0,6},{2,4},{4,2},{6,0},{8,14},{10,12},{12,10},{14,8},{16,22},{18,... | collective-permute-start | bytes 73736 | tf_op jit(solution)/shard_map/ppermute | solution.py:469
  38.5 3.8 %collective-permute-start.15 = (bf16[96,128]{1,0:T(8,128)(2,1)S(1)}, bf16[96,128]{1,0:T(8,128)(2,1)S(1)}, u32[]{:S(2)}, u32[]{:S(2)}) collective-permute-start(bf16[96,128]{1,0:T(8,128)(2,1)S(1)} %get-tuple-element.117.a_ref), channel_id=1, source_target_pairs={{0,4},{2,6},{4,0},{6,2},{8,12},{10,14},{12,8},{14,10},{16,20},{18,... | collective-permute-start | bytes 73736 | tf_op jit(solution)/shard_map/ppermute | solution.py:469
  39.4 3.8 %collective-permute-start.14 = (bf16[96,128]{1,0:T(8,128)(2,1)S(1)}, bf16[96,128]{1,0:T(8,128)(2,1)S(1)}, u32[]{:S(2)}, u32[]{:S(2)}) collective-permute-start(bf16[96,128]{1,0:T(8,128)(2,1)S(1)} %get-tuple-element.117.a_ref), channel_id=1, source_target_pairs={{0,2},{2,0},{4,6},{6,4},{8,10},{10,8},{12,14},{14,12},{16,18},{18,... | collective-permute-start | bytes 73736 | tf_op jit(solution)/shard_map/ppermute | solution.py:469

commit v6 on v5

--- a/solution.py
+++ b/solution.py
@@ -400,15 +400,17 @@
         out_ref[groups * size + quarter :] = gain
 
 
-def last_sum_kernel(packet, a_ref, b_ref, c_ref, d_ref, weight_ref, table_ref):
-    refs = (a_ref, b_ref, c_ref, d_ref)
-    weight_ref[...] = summed(refs, slice(0, packet.weight_size))
+def last_sum_kernel(packet, a_ref, b_ref, c_ref, d_ref, upper_ref, lower_ref, table_ref):
+    refs, cut = (a_ref, b_ref, c_ref, d_ref), upper_ref.shape[0]
+    upper_ref[...] = summed(refs, slice(0, cut))
+    lower_ref[...] = summed(refs, slice(cut, packet.weight_size))
     table_ref[...] = summed(refs, slice(packet.weight_size, packet.weight_size + packet.quarter + 16))
 
 
-def weights_out_kernel(packet, factor, weights_ref, other_weights_ref, grad_in_ref, grad_out_ref):
+def weights_out_kernel(packet, factor, upper_ref, lower_ref, other_upper_ref, other_lower_ref, grad_in_ref, grad_out_ref):
     odd = lax.rem(lax.axis_index("lat"), 2) == 1
-    own, other = weights_ref[...].astype(f32) * factor, other_weights_ref[...].astype(f32) * factor
+    own = jnp.concatenate([upper_ref[...], lower_ref[...]], axis=0).astype(f32) * factor
+    other = jnp.concatenate([other_upper_ref[...], other_lower_ref[...]], axis=0).astype(f32) * factor
     halves = (jnp.where(odd, other, own), jnp.where(odd, own, other))
     size = packet.weight_rows
     tiles = [half[tile * size : (tile + 1) * size] for half in halves for tile in range(6)]
@@ -599,27 +601,28 @@
         )(*gains, *held)
         gains = []
         held = trade(parts, shift)
-    weight_sum, table_sum = call(
+    cut = rounded_up(packet.weight_size // 2, 16)
+    *weight_sums, table_sum = call(
         functools.partial(last_sum_kernel, packet),
         "add_last",
         whole(4),
-        [struct((packet.weight_size, LANES), bf16), struct((packet.quarter + 16, LANES), bf16)],
+        [struct((rows, LANES), bf16) for rows in (cut, packet.weight_size - cut, packet.quarter + 16)],
         moved=1 << 18,
     )(*held)
     table_parts = trade([table_sum] * 4, 0)[::-1]
     for bit in range(1, lat_count.bit_length() - 1):
-        weight_sum = weight_sum + swap(weight_sum, "lat", 1 << bit)
-    weight_other = swap(weight_sum, "lat", 1)
+        weight_sums = [part + swap(part, "lat", 1 << bit) for part in weight_sums]
+    weight_others = [swap(part, "lat", 1) for part in weight_sums]
 
     cells_in_all = latent_field.shape[0] * latent_field.shape[1] * latent_field.shape[2]
     factor = 1.0 / math.sqrt(cells_in_all * lon_count * lat_count)
     grad_input_weight, grad_output_weight = call(
         functools.partial(weights_out_kernel, packet, factor),
         "weights_out",
-        whole(2),
+        whole(4),
         [struct((packet.weight_rows, 3 * features), bf16), struct((packet.weight_rows, features), bf16)],
         moved=1 << 18,
-    )(weight_sum, weight_other)
+    )(*weight_sums, *weight_others)
     table_parts, grad_input_weight = lax.optimization_barrier((table_parts, grad_input_weight))
     grad_table, gain_sum = call(
         functools.partial(table_out_kernel, packet, math.sqrt(head_dim), factor),

time: 44.1 us -> 44.1 us (level)
    ppermute x12 -> x13, waiting for transfers between devices: 9.62 us -> 8.43 us  [swap(): lax.ppermute(value, axis, [(source, source ^ mask) for source in range(co...]
    ppermute x6, waiting for transfers between devices: 3.65 us -> 4.69 us  [move(): return lax.ppermute(value, ('lon', 'lat'), pairs)]
    ppermute x12 -> x13, starting transfers between devices: 12.2 us -> 12.1 us  [swap(): lax.ppermute(value, axis, [(source, source ^ mask) for source in range(co...]
  transfers between devices with their start and end apart: 18 -> 19, of which waited for: 9 -> 10; matrix products, arithmetic and copies ran while one was open for 0% -> 0% of each run, Pallas kernels for 15% -> 15%
where the time goes in v6:
time: 44.1 us; the launch traced here: 43.9 us
  starting transfers between devices  18.3 us (41%)
  waiting for transfers between devices  13.1 us (30%)
  Pallas kernels  11.8 us (27%)
  between operations  0.72 us (2%)
    ppermute x13, starting transfers between devices, swap(): lax.ppermute(value, axis, [(source, source ^ mask) for source in range(co...  12.1 us
    ppermute x13, waiting for transfers between devices, swap(): lax.ppermute(value, axis, [(source, source ^ mask) for source in range(co...  8.43 us
    ppermute x6, starting transfers between devices, move(): return lax.ppermute(value, ('lon', 'lat'), pairs)  6.15 us
    ppermute x6, waiting for transfers between devices, move(): return lax.ppermute(value, ('lon', 'lat'), pairs)  4.69 us
    pallas_call x1, Pallas kernels, on_device(): call(functools.partial(window_kernel, packet), 'window', whole(10), [half...  3.17 us
    pallas_call x1, Pallas kernels, on_device(): call(bias_kernel, 'expand_bias', whole(1) + [hbm] * 2, [struct((HEADS, CE...  2.25 us
    pallas_call x1, Pallas kernels, on_device(): call(functools.partial(fold_kernel, packet), 'fold_table', whole(3), stru...  1.84 us
    pallas_call x1, Pallas kernels, on_device(): call(load_kernel, 'load', [hbm] * 5, [others, same, others, others] + [st...  1.18 us
  transfers between devices with their start and end apart: 19, of which 10 were waited for; matrix products, arithmetic and copies ran while one was open for 0% of the time, Pallas kernels for 15%

profile of v6, /device:TPU:0, one launch (start us, length us, event | category | flops | bytes accessed | tf_op | source)
XLA Modules:
  0.0 43.9 jit_solution(4912759655070670897)
XLA Ops:
  0.6 1.2 %load.1 = (bf16[72,384]{1,0:T(8,128)(2,1)S(1)}, bf16[80,384]{1,0:T(8,128)(2,1)S(1)}, bf16[72,384]{1,0:T(8,128)(2,1)S(1)}, bf16[72,384]{1,0:T(8,128)(2,1)S(1)}, b...) custom-call(bf16[6,12,2,384]{3,2,1,0:T(2,128)(2,1)} %bitcast.7, bf16[6,12,2,384]{3,2,1,0:T(2,128)(2,1)} %bitcast.8, ...), custom_call_target="tpu_custom_call" | custom-call | bytes 1048576 | tf_op jit(solution)/shard_map/load/pallas_call | solution.py:484
  1.8 3.0 %collective-permute-start = (bf16[80,384]{1,0:T(8,128)(2,1)S(1)}, bf16[80,384]{1,0:T(8,128)(2,1)S(1)}, u32[]{:S(2)}, u32[]{:S(2)}) collective-permute-start(bf16[80,384]{1,0:T(8,128)(2,1)S(1)} %get-tuple-element.68), channel_id=1, source_target_pairs={{0,2},{1,3},{2,4},{3,5},{4,6},{5,7},{6,8},{7,9},{8,10},{9,11},{10,... | collective-permute-start | bytes 184328 | tf_op jit(solution)/shard_map/ppermute | solution.py:467
  4.8 0.7 %collective-permute-start.1 = (bf16[72,384]{1,0:T(8,128)(2,1)S(1)}, bf16[72,384]{1,0:T(8,128)(2,1)S(1)}, u32[]{:S(2)}, u32[]{:S(2)}) collective-permute-start(bf16[72,384]{1,0:T(8,128)(2,1)S(1)} %get-tuple-element.69), channel_id=1, source_target_pairs={{0,3},{1,2},{2,5},{3,4},{4,7},{5,6},{6,9},{7,8},{8,11},{9,10},{10,... | collective-permute-start | bytes 165896 | tf_op jit(solution)/shard_map/ppermute | solution.py:467
  5.5 1.0 %collective-permute-start.2 = (bf16[72,384]{1,0:T(8,128)(2,1)S(1)}, bf16[72,384]{1,0:T(8,128)(2,1)S(1)}, u32[]{:S(2)}, u32[]{:S(2)}) collective-permute-start(bf16[72,384]{1,0:T(8,128)(2,1)S(1)} %get-tuple-element.70), channel_id=1, source_target_pairs={{0,1},{1,0},{2,3},{3,2},{4,5},{5,4},{6,7},{7,6},{8,9},{9,8},{10,11... | collective-permute-start | bytes 165896 | tf_op jit(solution)/shard_map/ppermute | solution.py:467
  6.4 2.3 %expand_bias.1 = (bf16[12,144,144]{2,1,0:T(8,128)(2,1)S(1)}, bf16[384,384]{1,0:T(8,128)(2,1)S(1)}, bf16[384,384]{1,0:T(8,128)(2,1)S(1)}, bf16[192,192]{1,0:T(8,1...) custom-call(bf16[12,3312]{1,0:T(8,128)(2,1)S(1)} %get-tuple-element., ...), custom_call_target="tpu_custom_call" | custom-call | bytes 2097152 | tf_op jit(solution)/shard_map/expand_bias/pallas_call | solution.py:496
  8.7 3.6 %collective-permute-done.1.near_diag_ref = bf16[72,384]{1,0:T(8,128)(2,1)S(1)} collective-permute-done((bf16[72,384]{1,0:T(8,128)(2,1)S(1)}, bf16[72,384]{1,0:T(8,128)(2,1)S(1)}, u32[]{:S(2)}, u32[]{:S(2)}) %collective-permute-start.1) | collective-permute-done | bytes 55328 | tf_op jit(solution)/shard_map/ppermute | solution.py:467
  12.3 0.0 collective-permute-done.2.lat_ref
  12.3 0.0 collective-permute-done.near_ref
  12.3 3.2 %window.1 = (bf16[2304,128]{1,0:T(8,128)(2,1)S(1)}, bf16[2304,128]{1,0:T(8,128)(2,1)S(1)}, bf16[12,144,144]{2,1,0:T(8,128)(2,1)S(1)}, bf16[4,384,144]{2,1,0:T(8,...) custom-call(bf16[72,384]{1,0:T(8,128)(2,1)S(1)} %get-tuple-element.67.own_ref, ...), custom_call_target="tpu_custom_call" | custom-call | flops 1000000000 | bytes 5242880 | tf_op jit(solution)/shard_map/window/pallas_call | solution.py:520
  15.5 0.1 collective-permute-start.3
  15.6 1.8 %fold_table.1.table_ref = bf16[320,128]{1,0:T(8,128)(2,1)S(1)} custom-call(bf16[12,144,144]{2,1,0:T(8,128)(2,1)S(1)} %get-tuple-element.78.scores_ref, bf16[384,384]{1,0:T(8,128)(2,1)S(1)} %get-tuple-element.79.lanes_ref, bf16[192,192]{1,0:T(8,128)(2,1)S(1)} %get-tuple-element.80.rows_ref), custom_call_target="tpu_custom_call" | custom-call | bytes 2097152 | tf_op jit(solution)/shard_map/fold_table/pallas_call | solution.py:551
  17.4 0.1 collective-permute-done.3.recv_ref
  17.6 0.1 add_lat.1
  17.7 0.1 collective-permute-start.5
  17.8 0.1 collective-permute-start.6
  17.9 3.4 %collective-permute-start.7 = (bf16[656,128]{1,0:T(8,128)(2,1)S(1)}, bf16[656,128]{1,0:T(8,128)(2,1)S(1)}, u32[]{:S(2)}, u32[]{:S(2)}) collective-permute-start(bf16[656,128]{1,0:T(8,128)(2,1)S(1)} %get-tuple-element.99), channel_id=1, source_target_pairs={{0,2},{2,0},{4,6},{6,4},{8,10},{10,8},{12,14},{14,12},{16,18},{18,... | collective-permute-start | bytes 503816 | tf_op jit(solution)/shard_map/ppermute | solution.py:471
  21.3 1.0 %grad_field.1 = (bf16[36,384]{1,0:T(8,128)(2,1)S(1)}, bf16[72,384]{1,0:T(8,128)(2,1)S(1)}, bf16[36,384]{1,0:T(8,128)(2,1)S(1)}, bf16[16,128]{1,0:T(8,128)(2,1)S(1)}) custom-call(bf16[384,1152]{1,0:T(8,128)(2,1)S(1)} %get-tuple-element.66.win_ref, bf16[4,384,144]{2,1,0:T(8,128)(2,1)S(1)} %get-tuple-element.89.grad_projected_ref, ...), custom_call_target="tpu_custom_call" | custom-call | flops 100000000 | bytes 5242880 | tf_op jit(solution)/shard_map/grad_field/pallas_call | solution.py:579
  22.3 1.4 %collective-permute-start.4 = (bf16[72,384]{1,0:T(8,128)(2,1)S(1)}, bf16[72,384]{1,0:T(8,128)(2,1)S(1)}, u32[]{:S(2)}, u32[]{:S(2)}) collective-permute-start(bf16[72,384]{1,0:T(8,128)(2,1)S(1)} %get-tuple-element.96), channel_id=1, source_target_pairs={{0,30},{1,31},{2,0},{3,1},{4,2},{5,3},{6,4},{7,5},{8,6},{9,7},{10,... | collective-permute-start | bytes 165896 | tf_op jit(solution)/shard_map/ppermute | solution.py:467
  23.7 0.0 collective-permute-start.9
  23.7 1.2 %collective-permute-done.9.refs_1_ = bf16[16,128]{1,0:T(8,128)(2,1)S(1)} collective-permute-done((bf16[16,128]{1,0:T(8,128)(2,1)S(1)}, bf16[16,128]{1,0:T(8,128)(2,1)S(1)}, u32[]{:S(2)}, u32[]{:S(2)}) %collective-permute-start.9) | collective-permute-done | bytes 4128 | tf_op jit(solution)/shard_map/ppermute | solution.py:471
  24.8 0.2 collective-permute-start.8
  25.0 1.0 %collective-permute-done.8.lat_ref = bf16[36,384]{1,0:T(8,128)(2,1)S(1)} collective-permute-done((bf16[36,384]{1,0:T(8,128)(2,1)S(1)}, bf16[36,384]{1,0:T(8,128)(2,1)S(1)}, u32[]{:S(2)}, u32[]{:S(2)}) %collective-permute-start.8) | collective-permute-done | bytes 27680 | tf_op jit(solution)/shard_map/ppermute | solution.py:467
  26.0 0.0 collective-permute-done.5.refs_2_
  26.0 2.0 %collective-permute-done.6.refs_3_ = bf16[656,128]{1,0:T(8,128)(2,1)S(1)} collective-permute-done((bf16[656,128]{1,0:T(8,128)(2,1)S(1)}, bf16[656,128]{1,0:T(8,128)(2,1)S(1)}, u32[]{:S(2)}, u32[]{:S(2)}) %collective-permute-start.6) | collective-permute-done | bytes 167968 | tf_op jit(solution)/shard_map/ppermute | solution.py:471
  28.0 0.0 collective-permute-done.7.refs_4_
  28.0 0.1 add_lon.1
  28.1 2.4 %collective-permute-start.11 = (bf16[240,128]{1,0:T(8,128)(2,1)S(1)}, bf16[240,128]{1,0:T(8,128)(2,1)S(1)}, u32[]{:S(2)}, u32[]{:S(2)}) collective-permute-start(bf16[240,128]{1,0:T(8,128)(2,1)S(1)} %get-tuple-element.109), channel_id=1, source_target_pairs={{0,24},{2,26},{4,28},{6,30},{8,16},{10,18},{12,20},{14,22},{16,8},... | collective-permute-start | bytes 184328 | tf_op jit(solution)/shard_map/ppermute | solution.py:471
  30.6 0.0 collective-permute-start.12
  30.6 2.0 %collective-permute-start.13 = (bf16[240,128]{1,0:T(8,128)(2,1)S(1)}, bf16[240,128]{1,0:T(8,128)(2,1)S(1)}, u32[]{:S(2)}, u32[]{:S(2)}) collective-permute-start(bf16[240,128]{1,0:T(8,128)(2,1)S(1)} %get-tuple-element.111), channel_id=1, source_target_pairs={{0,8},{2,10},{4,12},{6,14},{8,0},{10,2},{12,4},{14,6},{16,24},{18,... | collective-permute-start | bytes 184328 | tf_op jit(solution)/shard_map/ppermute | solution.py:471
  32.6 0.0 collective-permute-done.4.near_ref
  32.6 0.0 collective-permute-start.10
  32.6 2.0 %collective-permute-done.11.a_ref = bf16[240,128]{1,0:T(8,128)(2,1)S(1)} collective-permute-done((bf16[240,128]{1,0:T(8,128)(2,1)S(1)}, bf16[240,128]{1,0:T(8,128)(2,1)S(1)}, u32[]{:S(2)}, u32[]{:S(2)}) %collective-permute-start.11) | collective-permute-done | bytes 61472 | tf_op jit(solution)/shard_map/ppermute | solution.py:471
  34.6 1.6 %collective-permute-done.12.b_ref = bf16[240,128]{1,0:T(8,128)(2,1)S(1)} collective-permute-done((bf16[240,128]{1,0:T(8,128)(2,1)S(1)}, bf16[240,128]{1,0:T(8,128)(2,1)S(1)}, u32[]{:S(2)}, u32[]{:S(2)}) %collective-permute-start.12) | collective-permute-done | bytes 61472 | tf_op jit(solution)/shard_map/ppermute | solution.py:471
  36.1 0.0 collective-permute-done.13.c_ref
  36.2 2.8 %collective-permute-start.16 = (bf16[96,128]{1,0:T(8,128)(2,1)S(1)}, bf16[96,128]{1,0:T(8,128)(2,1)S(1)}, u32[]{:S(2)}, u32[]{:S(2)}) collective-permute-start(bf16[96,128]{1,0:T(8,128)(2,1)S(1)} %get-tuple-element.119.a_ref), channel_id=1, source_target_pairs={{0,6},{2,4},{4,2},{6,0},{8,14},{10,12},{12,10},{14,8},{16,22},{18,... | collective-permute-start | bytes 73736 | tf_op jit(solution)/shard_map/ppermute | solution.py:471
  38.9 0.4 collective-permute-start.15
  39.3 0.4 collective-permute-start.14
  39.7 0.0 collective-permute-start.17
  39.7 0.0 collective-permute-done.10.near_diag_ref
  39.7 0.5 %collective-permute-start.18 = (bf16[64,128]{1,0:T(8,128)(2,1)S(1)}, bf16[64,128]{1,0:T(8,128)(2,1)S(1)}, u32[]{:S(2)}, u32[]{:S(2)}) collective-permute-start(bf16[64,128]{1,0:T(8,128)(2,1)S(1)} %get-tuple-element.115.lower_ref), channel_id=1, source_target_pairs={{0,1},{1,0},{2,3},{3,2},{4,5},{5,4},{6,7},{7,6},{8,9},{9,8},{10,11... | collective-permute-start | bytes 49160 | tf_op jit(solution)/shard_map/ppermute | solution.py:471
  40.2 0.7 %unpack_quarters.1 = bf16[6,12,2,384]{3,2,1,0:T(2,128)(2,1)} custom-call(bf16[36,384]{1,0:T(8,128)(2,1)S(1)} %get-tuple-element.95.own_ref, bf16[72,384]{1,0:T(8,128)(2,1)S(1)} %collective-permute-done.4.near_ref, bf16[36,384]{1,0:T(8,128)(2,1)S(1)} %collective-permute-done.8.lat_ref, bf16[72,384]{1,0:T(8,128)(2,1)S(1)} %collective-permute-done.10.near_diag_ref), custom_call_target="tpu_custom_call" | custom-call | bytes 4194304 | tf_op jit(solution)/shard_map/unpack_quarters/pallas_call | solution.py:638
  40.9 0.2 collective-permute-done.18.other_lower_ref
  41.1 0.0 collective-permute-done.17.other_upper_ref
  41.1 0.6 %weights_out.1 = (bf16[24,1152]{1,0:T(8,128)(2,1)}, bf16[24,384]{1,0:T(8,128)(2,1)}) custom-call(bf16[80,128]{1,0:T(8,128)(2,1)S(1)} %get-tuple-element.114.upper_ref, bf16[64,128]{1,0:T(8,128)(2,1)S(1)} %get-tuple-element.115.lower_ref, bf16[80,128]{1,0:T(8,128)(2,1)S(1)} %collective-permute-done.17.other_upper_ref, ...), custom_call_target="tpu_custom_call" | custom-call | bytes 262144 | tf_op jit(solution)/shard_map/weights_out/pallas_call | solution.py:619
  41.7 0.0 collective-permute-done.16.d_ref
  41.7 1.0 %collective-permute-done.15.c_ref = bf16[96,128]{1,0:T(8,128)(2,1)S(1)} collective-permute-done((bf16[96,128]{1,0:T(8,128)(2,1)S(1)}, bf16[96,128]{1,0:T(8,128)(2,1)S(1)}, u32[]{:S(2)}, u32[]{:S(2)}) %collective-permute-start.15) | collective-permute-done | bytes 24608 | tf_op jit(solution)/shard_map/ppermute | solution.py:471
  42.8 0.4 collective-permute-done.14.b_ref
  43.1 0.8 %table_out.1 = (f32[12,1,3312]{2,1,0:T(1,128)}, f32[384]{0:T(512)}) custom-call(bf16[96,128]{1,0:T(8,128)(2,1)S(1)} %get-tuple-element.119.a_ref, bf16[96,128]{1,0:T(8,128)(2,1)S(1)} %collective-permute-done.14.b_ref, bf16[96,128]{1,0:T(8,128)(2,1)S(1)} %collective-permute-done.15.c_ref, bf16[96,128]{1,0:T(8,128)(2,1)S(1)} %collective-permute-done.16.d_ref), custom_call_target="tpu_custom_call" | custom-call | bytes 524288 | tf_op jit(solution)/shard_map/table_out/pallas_call | solution.py:627
  (1 shorter events, 0.0 us)
Async XLA Ops:
  1.8 10.5 %collective-permute-start = (bf16[80,384]{1,0:T(8,128)(2,1)S(1)}, bf16[80,384]{1,0:T(8,128)(2,1)S(1)}, u32[]{:S(2)}, u32[]{:S(2)}) collective-permute-start(bf16[80,384]{1,0:T(8,128)(2,1)S(1)} %get-tuple-element.68), channel_id=1, source_target_pairs={{0,2},{1,3},{2,4},{3,5},{4,6},{5,7},{6,8},{7,9},{8,10},{9,11},{10,... | collective-permute-start | bytes 184328 | tf_op jit(solution)/shard_map/ppermute | solution.py:467
  4.8 7.5 %collective-permute-start.1 = (bf16[72,384]{1,0:T(8,128)(2,1)S(1)}, bf16[72,384]{1,0:T(8,128)(2,1)S(1)}, u32[]{:S(2)}, u32[]{:S(2)}) collective-permute-start(bf16[72,384]{1,0:T(8,128)(2,1)S(1)} %get-tuple-element.69), channel_id=1, source_target_pairs={{0,3},{1,2},{2,5},{3,4},{4,7},{5,6},{6,9},{7,8},{8,11},{9,10},{10,... | collective-permute-start | bytes 165896 | tf_op jit(solution)/shard_map/ppermute | solution.py:467
  5.5 6.9 %collective-permute-start.2 = (bf16[72,384]{1,0:T(8,128)(2,1)S(1)}, bf16[72,384]{1,0:T(8,128)(2,1)S(1)}, u32[]{:S(2)}, u32[]{:S(2)}) collective-permute-start(bf16[72,384]{1,0:T(8,128)(2,1)S(1)} %get-tuple-element.70), channel_id=1, source_target_pairs={{0,1},{1,0},{2,3},{3,2},{4,5},{5,4},{6,7},{7,6},{8,9},{9,8},{10,11... | collective-permute-start | bytes 165896 | tf_op jit(solution)/shard_map/ppermute | solution.py:467
  15.5 2.1 %collective-permute-start.3 = (bf16[2304,128]{1,0:T(8,128)(2,1)S(1)}, bf16[2304,128]{1,0:T(8,128)(2,1)S(1)}, u32[]{:S(2)}, u32[]{:S(2)}) collective-permute-start(bf16[2304,128]{1,0:T(8,128)(2,1)S(1)} %get-tuple-element.77), channel_id=1, source_target_pairs={{0,1},{1,0},{2,3},{3,2},{4,5},{5,4},{6,7},{7,6},{8,9},{9,8},{10,11... | collective-permute-start | bytes 1769480 | tf_op jit(solution)/shard_map/ppermute | solution.py:471
  17.7 8.3 %collective-permute-start.5 = (bf16[656,128]{1,0:T(8,128)(2,1)S(1)}, bf16[656,128]{1,0:T(8,128)(2,1)S(1)}, u32[]{:S(2)}, u32[]{:S(2)}) collective-permute-start(bf16[656,128]{1,0:T(8,128)(2,1)S(1)} %get-tuple-element.97), channel_id=1, source_target_pairs={{0,6},{2,4},{4,2},{6,0},{8,14},{10,12},{12,10},{14,8},{16,22},{18,... | collective-permute-start | bytes 503816 | tf_op jit(solution)/shard_map/ppermute | solution.py:471
  17.8 10.2 %collective-permute-start.6 = (bf16[656,128]{1,0:T(8,128)(2,1)S(1)}, bf16[656,128]{1,0:T(8,128)(2,1)S(1)}, u32[]{:S(2)}, u32[]{:S(2)}) collective-permute-start(bf16[656,128]{1,0:T(8,128)(2,1)S(1)} %get-tuple-element.98), channel_id=1, source_target_pairs={{0,4},{2,6},{4,0},{6,2},{8,12},{10,14},{12,8},{14,10},{16,20},{18,... | collective-permute-start | bytes 503816 | tf_op jit(solution)/shard_map/ppermute | solution.py:471
  17.9 10.2 %collective-permute-start.7 = (bf16[656,128]{1,0:T(8,128)(2,1)S(1)}, bf16[656,128]{1,0:T(8,128)(2,1)S(1)}, u32[]{:S(2)}, u32[]{:S(2)}) collective-permute-start(bf16[656,128]{1,0:T(8,128)(2,1)S(1)} %get-tuple-element.99), channel_id=1, source_target_pairs={{0,2},{2,0},{4,6},{6,4},{8,10},{10,8},{12,14},{14,12},{16,18},{18,... | collective-permute-start | bytes 503816 | tf_op jit(solution)/shard_map/ppermute | solution.py:471
  22.3 10.3 %collective-permute-start.4 = (bf16[72,384]{1,0:T(8,128)(2,1)S(1)}, bf16[72,384]{1,0:T(8,128)(2,1)S(1)}, u32[]{:S(2)}, u32[]{:S(2)}) collective-permute-start(bf16[72,384]{1,0:T(8,128)(2,1)S(1)} %get-tuple-element.96), channel_id=1, source_target_pairs={{0,30},{1,31},{2,0},{3,1},{4,2},{5,3},{6,4},{7,5},{8,6},{9,7},{10,... | collective-permute-start | bytes 165896 | tf_op jit(solution)/shard_map/ppermute | solution.py:467
  23.7 1.2 %collective-permute-start.9 = (bf16[16,128]{1,0:T(8,128)(2,1)S(1)}, bf16[16,128]{1,0:T(8,128)(2,1)S(1)}, u32[]{:S(2)}, u32[]{:S(2)}) collective-permute-start(bf16[16,128]{1,0:T(8,128)(2,1)S(1)} %get-tuple-element.102.refs_0_), channel_id=1, source_target_pairs={{0,1},{1,0},{2,3},{3,2},{4,5},{5,4},{6,7},{7,6},{8,9},{9,8},{10,11... | collective-permute-start | bytes 12296 | tf_op jit(solution)/shard_map/ppermute | solution.py:471
  24.8 1.2 %collective-permute-start.8 = (bf16[36,384]{1,0:T(8,128)(2,1)S(1)}, bf16[36,384]{1,0:T(8,128)(2,1)S(1)}, u32[]{:S(2)}, u32[]{:S(2)}) collective-permute-start(bf16[36,384]{1,0:T(8,128)(2,1)S(1)} %get-tuple-element.101), channel_id=1, source_target_pairs={{0,1},{1,0},{2,3},{3,2},{4,5},{5,4},{6,7},{7,6},{8,9},{9,8},{10,11... | collective-permute-start | bytes 82952 | tf_op jit(solution)/shard_map/ppermute | solution.py:467
  28.1 6.4 %collective-permute-start.11 = (bf16[240,128]{1,0:T(8,128)(2,1)S(1)}, bf16[240,128]{1,0:T(8,128)(2,1)S(1)}, u32[]{:S(2)}, u32[]{:S(2)}) collective-permute-start(bf16[240,128]{1,0:T(8,128)(2,1)S(1)} %get-tuple-element.109), channel_id=1, source_target_pairs={{0,24},{2,26},{4,28},{6,30},{8,16},{10,18},{12,20},{14,22},{16,8},... | collective-permute-start | bytes 184328 | tf_op jit(solution)/shard_map/ppermute | solution.py:471
  30.6 5.6 %collective-permute-start.12 = (bf16[240,128]{1,0:T(8,128)(2,1)S(1)}, bf16[240,128]{1,0:T(8,128)(2,1)S(1)}, u32[]{:S(2)}, u32[]{:S(2)}) collective-permute-start(bf16[240,128]{1,0:T(8,128)(2,1)S(1)} %get-tuple-element.110), channel_id=1, source_target_pairs={{0,16},{2,18},{4,20},{6,22},{8,24},{10,26},{12,28},{14,30},{16,0},... | collective-permute-start | bytes 184328 | tf_op jit(solution)/shard_map/ppermute | solution.py:471
  30.6 5.6 %collective-permute-start.13 = (bf16[240,128]{1,0:T(8,128)(2,1)S(1)}, bf16[240,128]{1,0:T(8,128)(2,1)S(1)}, u32[]{:S(2)}, u32[]{:S(2)}) collective-permute-start(bf16[240,128]{1,0:T(8,128)(2,1)S(1)} %get-tuple-element.111), channel_id=1, source_target_pairs={{0,8},{2,10},{4,12},{6,14},{8,0},{10,2},{12,4},{14,6},{16,24},{18,... | collective-permute-start | bytes 184328 | tf_op jit(solution)/shard_map/ppermute | solution.py:471
  32.6 7.2 %collective-permute-start.10 = (bf16[72,384]{1,0:T(8,128)(2,1)S(1)}, bf16[72,384]{1,0:T(8,128)(2,1)S(1)}, u32[]{:S(2)}, u32[]{:S(2)}) collective-permute-start(bf16[72,384]{1,0:T(8,128)(2,1)S(1)} %collective-permute-done.4.near_ref), channel_id=1, source_target_pairs={{0,1},{1,0},{2,3},{3,2},{4,5},{5,4},{6,7},{7,6},{8,9},{9,8},{10,11... | collective-permute-start | bytes 165896 | tf_op jit(solution)/shard_map/ppermute | solution.py:467
  36.2 5.6 %collective-permute-start.16 = (bf16[96,128]{1,0:T(8,128)(2,1)S(1)}, bf16[96,128]{1,0:T(8,128)(2,1)S(1)}, u32[]{:S(2)}, u32[]{:S(2)}) collective-permute-start(bf16[96,128]{1,0:T(8,128)(2,1)S(1)} %get-tuple-element.119.a_ref), channel_id=1, source_target_pairs={{0,6},{2,4},{4,2},{6,0},{8,14},{10,12},{12,10},{14,8},{16,22},{18,... | collective-permute-start | bytes 73736 | tf_op jit(solution)/shard_map/ppermute | solution.py:471
  38.9 3.8 %collective-permute-start.15 = (bf16[96,128]{1,0:T(8,128)(2,1)S(1)}, bf16[96,128]{1,0:T(8,128)(2,1)S(1)}, u32[]{:S(2)}, u32[]{:S(2)}) collective-permute-start(bf16[96,128]{1,0:T(8,128)(2,1)S(1)} %get-tuple-element.119.a_ref), channel_id=1, source_target_pairs={{0,4},{2,6},{4,0},{6,2},{8,12},{10,14},{12,8},{14,10},{16,20},{18,... | collective-permute-start | bytes 73736 | tf_op jit(solution)/shard_map/ppermute | solution.py:471
  39.3 3.8 %collective-permute-start.14 = (bf16[96,128]{1,0:T(8,128)(2,1)S(1)}, bf16[96,128]{1,0:T(8,128)(2,1)S(1)}, u32[]{:S(2)}, u32[]{:S(2)}) collective-permute-start(bf16[96,128]{1,0:T(8,128)(2,1)S(1)} %get-tuple-element.119.a_ref), channel_id=1, source_target_pairs={{0,2},{2,0},{4,6},{6,4},{8,10},{10,8},{12,14},{14,12},{16,18},{18,... | collective-permute-start | bytes 73736 | tf_op jit(solution)/shard_map/ppermute | solution.py:471
  39.7 1.4 %collective-permute-start.17 = (bf16[80,128]{1,0:T(8,128)(2,1)S(1)}, bf16[80,128]{1,0:T(8,128)(2,1)S(1)}, u32[]{:S(2)}, u32[]{:S(2)}) collective-permute-start(bf16[80,128]{1,0:T(8,128)(2,1)S(1)} %get-tuple-element.114.upper_ref), channel_id=1, source_target_pairs={{0,1},{1,0},{2,3},{3,2},{4,5},{5,4},{6,7},{7,6},{8,9},{9,8},{10,11... | collective-permute-start | bytes 61448 | tf_op jit(solution)/shard_map/ppermute | solution.py:471
  39.7 1.3 %collective-permute-start.18 = (bf16[64,128]{1,0:T(8,128)(2,1)S(1)}, bf16[64,128]{1,0:T(8,128)(2,1)S(1)}, u32[]{:S(2)}, u32[]{:S(2)}) collective-permute-start(bf16[64,128]{1,0:T(8,128)(2,1)S(1)} %get-tuple-element.115.lower_ref), channel_id=1, source_target_pairs={{0,1},{1,0},{2,3},{3,2},{4,5},{5,4},{6,7},{7,6},{8,9},{9,8},{10,11... | collective-permute-start | bytes 49160 | tf_op jit(solution)/shard_map/ppermute | solution.py:471

commit v7 on v6

--- a/solution.py
+++ b/solution.py
@@ -152,9 +152,7 @@
     square = (features, features)
     eye = one_hot(counted(square, 0) == counted(square, 1))
     eye_ref[...] = eye
-    source, lane = cell_source(counted((CELLS, 1), 0), 2 * QUARTER), counted((CELLS, 2 * CELLS), 1)
-    place_ref[:CELLS] = one_hot(source == lane)
-    place_ref[CELLS:] = one_hot(source + QUARTER == lane)
+    place_ref[...] = one_hot(cell_source(counted((CELLS, 1), 0), QUARTER) == counted((CELLS, CELLS), 1))
     place_t_ref[...] = one_hot(cell_source(counted((1, CELLS), 1), QUARTER) == counted((CELLS, CELLS), 0))
     lane = counted((1, WIDE), 1)
     target = jnp.where(lane < SPAN, lax.rem(lane, PLANE) * (SPAN // PLANE) + lax.div(lane, PLANE), -1)
@@ -212,17 +210,17 @@
     group_heads = LANES // head_dim
     score_scale = head_dim ** (-0.5)
     near = near_ref[...].astype(f32)
-    west, east = [near[: 2 * QUARTER], near_diag_ref[...].astype(f32)], [own_ref[...].astype(f32), lat_ref[...].astype(f32)]
-    stacked = jnp.concatenate([west[0], east[0], west[1], east[1]], axis=0).astype(bf16)
+    quarters = (near, own_ref[...].astype(f32), near_diag_ref[...].astype(f32), lat_ref[...].astype(f32))
+    sides = [jnp.concatenate([quarter[at : at + QUARTER] for quarter in quarters], axis=0) for at in (0, QUARTER)]
     cell, lane = counted((CELLS, CELLS), 0), counted((CELLS, CELLS), 1)
     source = lax.rem(cell, PLANE) * WIN_LON + lax.div(cell, PLANE)
     ids = near[2 * QUARTER : 2 * QUARTER + 1, :CELLS]
     region_col = jnp.sum(jnp.where(source == lane, ids, 0.0), axis=1, keepdims=True)
     region_row = jnp.sum(jnp.where(cell == lane, region_col, 0.0), axis=0, keepdims=True)
     same = region_col == region_row
-    placed = nn_dot(place_ref[...], stacked)
-    field = placed[:CELLS]
-    cot = placed[CELLS:].astype(bf16)
+    placed = nn_dot(place_ref[...], jnp.concatenate(sides, axis=1).astype(bf16))
+    field, cot_f32 = placed[:, :features], placed[:, features:]
+    cot = cot_f32.astype(bf16)
     cot_ref[...] = cot
     gain = gain_ref[...].reshape(1, features)
 
@@ -239,7 +237,7 @@
     grad_att_t = nt_dot(wout_ref[...], cot).astype(bf16)
     key_value_t = jnp.transpose(wide_keys_values).astype(bf16)
     left[0] = jnp.transpose(normed.astype(f32)).astype(bf16)
-    right[3] = jnp.transpose(placed[CELLS:]).astype(bf16)
+    right[3] = jnp.transpose(cot_f32).astype(bf16)
 
     def spread(head_rows, slot):
         parts = []
@@ -503,7 +501,7 @@
             struct((WIDE, WIDE), bf16),
             struct((HEADS * 16, HEADS * 16), bf16),
             struct((features, features), bf16),
-            struct((2 * CELLS, 2 * CELLS), bf16),
+            struct((CELLS, CELLS), bf16),
             struct((CELLS, CELLS), bf16),
             struct(input_weight.shape, bf16),
             struct(output_weight.shape, bf16),

time: 44.1 us -> 44 us (level)
  no operation moved by 1% of the time
where the time goes in v7:
time: 44 us; the launch traced here: 43.8 us
  starting transfers between devices  18.3 us (42%)
  waiting for transfers between devices  13.1 us (30%)
  Pallas kernels  11.7 us (27%)
  between operations  0.72 us (2%)
    ppermute x13, starting transfers between devices, swap(): lax.ppermute(value, axis, [(source, source ^ mask) for source in range(co...  12.1 us
    ppermute x13, waiting for transfers between devices, swap(): lax.ppermute(value, axis, [(source, source ^ mask) for source in range(co...  8.42 us
    ppermute x6, starting transfers between devices, move(): return lax.ppermute(value, ('lon', 'lat'), pairs)  6.15 us
    ppermute x6, waiting for transfers between devices, move(): return lax.ppermute(value, ('lon', 'lat'), pairs)  4.73 us
    pallas_call x1, Pallas kernels, on_device(): call(functools.partial(window_kernel, packet), 'window', whole(10), [half...  3.09 us
    pallas_call x1, Pallas kernels, on_device(): call(bias_kernel, 'expand_bias', whole(1) + [hbm] * 2, [struct((HEADS, CE...  2.21 us
    pallas_call x1, Pallas kernels, on_device(): call(functools.partial(fold_kernel, packet), 'fold_table', whole(3), stru...  1.83 us
    pallas_call x1, Pallas kernels, on_device(): call(load_kernel, 'load', [hbm] * 5, [others, same, others, others] + [st...  1.18 us
  transfers between devices with their start and end apart: 19, of which 10 were waited for; matrix products, arithmetic and copies ran while one was open for 0% of the time, Pallas kernels for 15%

profile of v7, /device:TPU:0, one launch (start us, length us, event | category | flops | bytes accessed | tf_op | source)
XLA Modules:
  0.0 43.8 jit_solution(4709674604944039548)
XLA Ops:
  0.6 1.2 %load.1 = (bf16[72,384]{1,0:T(8,128)(2,1)S(1)}, bf16[80,384]{1,0:T(8,128)(2,1)S(1)}, bf16[72,384]{1,0:T(8,128)(2,1)S(1)}, bf16[72,384]{1,0:T(8,128)(2,1)S(1)}, b...) custom-call(bf16[6,12,2,384]{3,2,1,0:T(2,128)(2,1)} %bitcast.7, bf16[6,12,2,384]{3,2,1,0:T(2,128)(2,1)} %bitcast.8, ...), custom_call_target="tpu_custom_call" | custom-call | bytes 1048576 | tf_op jit(solution)/shard_map/load/pallas_call | solution.py:482
  1.8 3.0 %collective-permute-start = (bf16[80,384]{1,0:T(8,128)(2,1)S(1)}, bf16[80,384]{1,0:T(8,128)(2,1)S(1)}, u32[]{:S(2)}, u32[]{:S(2)}) collective-permute-start(bf16[80,384]{1,0:T(8,128)(2,1)S(1)} %get-tuple-element.68), channel_id=1, source_target_pairs={{0,2},{1,3},{2,4},{3,5},{4,6},{5,7},{6,8},{7,9},{8,10},{9,11},{10,... | collective-permute-start | bytes 184328 | tf_op jit(solution)/shard_map/ppermute | solution.py:465
  4.8 0.7 %collective-permute-start.1 = (bf16[72,384]{1,0:T(8,128)(2,1)S(1)}, bf16[72,384]{1,0:T(8,128)(2,1)S(1)}, u32[]{:S(2)}, u32[]{:S(2)}) collective-permute-start(bf16[72,384]{1,0:T(8,128)(2,1)S(1)} %get-tuple-element.69), channel_id=1, source_target_pairs={{0,3},{1,2},{2,5},{3,4},{4,7},{5,6},{6,9},{7,8},{8,11},{9,10},{10,... | collective-permute-start | bytes 165896 | tf_op jit(solution)/shard_map/ppermute | solution.py:465
  5.5 1.0 %collective-permute-start.2 = (bf16[72,384]{1,0:T(8,128)(2,1)S(1)}, bf16[72,384]{1,0:T(8,128)(2,1)S(1)}, u32[]{:S(2)}, u32[]{:S(2)}) collective-permute-start(bf16[72,384]{1,0:T(8,128)(2,1)S(1)} %get-tuple-element.70), channel_id=1, source_target_pairs={{0,1},{1,0},{2,3},{3,2},{4,5},{5,4},{6,7},{7,6},{8,9},{9,8},{10,11... | collective-permute-start | bytes 165896 | tf_op jit(solution)/shard_map/ppermute | solution.py:465
  6.4 2.2 %expand_bias.1 = (bf16[12,144,144]{2,1,0:T(8,128)(2,1)S(1)}, bf16[384,384]{1,0:T(8,128)(2,1)S(1)}, bf16[384,384]{1,0:T(8,128)(2,1)S(1)}, bf16[192,192]{1,0:T(8,1...) custom-call(bf16[12,3312]{1,0:T(8,128)(2,1)S(1)} %get-tuple-element., ...), custom_call_target="tpu_custom_call" | custom-call | bytes 2097152 | tf_op jit(solution)/shard_map/expand_bias/pallas_call | solution.py:494
  8.6 3.7 %collective-permute-done.1.near_diag_ref = bf16[72,384]{1,0:T(8,128)(2,1)S(1)} collective-permute-done((bf16[72,384]{1,0:T(8,128)(2,1)S(1)}, bf16[72,384]{1,0:T(8,128)(2,1)S(1)}, u32[]{:S(2)}, u32[]{:S(2)}) %collective-permute-start.1) | collective-permute-done | bytes 55328 | tf_op jit(solution)/shard_map/ppermute | solution.py:465
  12.3 0.0 collective-permute-done.2.lat_ref
  12.3 0.0 collective-permute-done.near_ref
  12.3 3.1 %window.1 = (bf16[2304,128]{1,0:T(8,128)(2,1)S(1)}, bf16[2304,128]{1,0:T(8,128)(2,1)S(1)}, bf16[12,144,144]{2,1,0:T(8,128)(2,1)S(1)}, bf16[4,384,144]{2,1,0:T(8,...) custom-call(bf16[72,384]{1,0:T(8,128)(2,1)S(1)} %get-tuple-element.67.own_ref, ...), custom_call_target="tpu_custom_call" | custom-call | flops 1000000000 | bytes 5242880 | tf_op jit(solution)/shard_map/window/pallas_call | solution.py:518
  15.4 0.1 collective-permute-start.3
  15.5 1.8 %fold_table.1.table_ref = bf16[320,128]{1,0:T(8,128)(2,1)S(1)} custom-call(bf16[12,144,144]{2,1,0:T(8,128)(2,1)S(1)} %get-tuple-element.78.scores_ref, bf16[384,384]{1,0:T(8,128)(2,1)S(1)} %get-tuple-element.79.lanes_ref, bf16[192,192]{1,0:T(8,128)(2,1)S(1)} %get-tuple-element.80.rows_ref), custom_call_target="tpu_custom_call" | custom-call | bytes 2097152 | tf_op jit(solution)/shard_map/fold_table/pallas_call | solution.py:549
  17.3 0.2 collective-permute-done.3.recv_ref
  17.5 0.1 add_lat.1
  17.6 0.1 collective-permute-start.5
  17.7 0.1 collective-permute-start.6
  17.8 3.4 %collective-permute-start.7 = (bf16[656,128]{1,0:T(8,128)(2,1)S(1)}, bf16[656,128]{1,0:T(8,128)(2,1)S(1)}, u32[]{:S(2)}, u32[]{:S(2)}) collective-permute-start(bf16[656,128]{1,0:T(8,128)(2,1)S(1)} %get-tuple-element.99), channel_id=1, source_target_pairs={{0,2},{2,0},{4,6},{6,4},{8,10},{10,8},{12,14},{14,12},{16,18},{18,... | collective-permute-start | bytes 503816 | tf_op jit(solution)/shard_map/ppermute | solution.py:469
  21.2 1.0 %grad_field.1 = (bf16[36,384]{1,0:T(8,128)(2,1)S(1)}, bf16[72,384]{1,0:T(8,128)(2,1)S(1)}, bf16[36,384]{1,0:T(8,128)(2,1)S(1)}, bf16[16,128]{1,0:T(8,128)(2,1)S(1)}) custom-call(bf16[384,1152]{1,0:T(8,128)(2,1)S(1)} %get-tuple-element.66.win_ref, bf16[4,384,144]{2,1,0:T(8,128)(2,1)S(1)} %get-tuple-element.89.grad_projected_ref, ...), custom_call_target="tpu_custom_call" | custom-call | flops 100000000 | bytes 5242880 | tf_op jit(solution)/shard_map/grad_field/pallas_call | solution.py:577
  22.2 1.4 %collective-permute-start.4 = (bf16[72,384]{1,0:T(8,128)(2,1)S(1)}, bf16[72,384]{1,0:T(8,128)(2,1)S(1)}, u32[]{:S(2)}, u32[]{:S(2)}) collective-permute-start(bf16[72,384]{1,0:T(8,128)(2,1)S(1)} %get-tuple-element.96), channel_id=1, source_target_pairs={{0,30},{1,31},{2,0},{3,1},{4,2},{5,3},{6,4},{7,5},{8,6},{9,7},{10,... | collective-permute-start | bytes 165896 | tf_op jit(solution)/shard_map/ppermute | solution.py:465
  23.6 0.0 collective-permute-start.9
  23.6 1.2 %collective-permute-done.9.refs_1_ = bf16[16,128]{1,0:T(8,128)(2,1)S(1)} collective-permute-done((bf16[16,128]{1,0:T(8,128)(2,1)S(1)}, bf16[16,128]{1,0:T(8,128)(2,1)S(1)}, u32[]{:S(2)}, u32[]{:S(2)}) %collective-permute-start.9) | collective-permute-done | bytes 4128 | tf_op jit(solution)/shard_map/ppermute | solution.py:469
  24.7 0.2 collective-permute-start.8
  24.9 1.0 %collective-permute-done.8.lat_ref = bf16[36,384]{1,0:T(8,128)(2,1)S(1)} collective-permute-done((bf16[36,384]{1,0:T(8,128)(2,1)S(1)}, bf16[36,384]{1,0:T(8,128)(2,1)S(1)}, u32[]{:S(2)}, u32[]{:S(2)}) %collective-permute-start.8) | collective-permute-done | bytes 27680 | tf_op jit(solution)/shard_map/ppermute | solution.py:465
  26.0 0.0 collective-permute-done.5.refs_2_
  26.0 2.0 %collective-permute-done.6.refs_3_ = bf16[656,128]{1,0:T(8,128)(2,1)S(1)} collective-permute-done((bf16[656,128]{1,0:T(8,128)(2,1)S(1)}, bf16[656,128]{1,0:T(8,128)(2,1)S(1)}, u32[]{:S(2)}, u32[]{:S(2)}) %collective-permute-start.6) | collective-permute-done | bytes 167968 | tf_op jit(solution)/shard_map/ppermute | solution.py:469
  27.9 0.0 collective-permute-done.7.refs_4_
  27.9 0.1 add_lon.1
  28.0 2.5 %collective-permute-start.11 = (bf16[240,128]{1,0:T(8,128)(2,1)S(1)}, bf16[240,128]{1,0:T(8,128)(2,1)S(1)}, u32[]{:S(2)}, u32[]{:S(2)}) collective-permute-start(bf16[240,128]{1,0:T(8,128)(2,1)S(1)} %get-tuple-element.109), channel_id=1, source_target_pairs={{0,24},{2,26},{4,28},{6,30},{8,16},{10,18},{12,20},{14,22},{16,8},... | collective-permute-start | bytes 184328 | tf_op jit(solution)/shard_map/ppermute | solution.py:469
  30.5 0.0 collective-permute-start.12
  30.5 2.0 %collective-permute-start.13 = (bf16[240,128]{1,0:T(8,128)(2,1)S(1)}, bf16[240,128]{1,0:T(8,128)(2,1)S(1)}, u32[]{:S(2)}, u32[]{:S(2)}) collective-permute-start(bf16[240,128]{1,0:T(8,128)(2,1)S(1)} %get-tuple-element.111), channel_id=1, source_target_pairs={{0,8},{2,10},{4,12},{6,14},{8,0},{10,2},{12,4},{14,6},{16,24},{18,... | collective-permute-start | bytes 184328 | tf_op jit(solution)/shard_map/ppermute | solution.py:469
  32.5 0.0 collective-permute-done.4.near_ref
  32.5 0.0 collective-permute-start.10
  32.5 2.0 %collective-permute-done.11.a_ref = bf16[240,128]{1,0:T(8,128)(2,1)S(1)} collective-permute-done((bf16[240,128]{1,0:T(8,128)(2,1)S(1)}, bf16[240,128]{1,0:T(8,128)(2,1)S(1)}, u32[]{:S(2)}, u32[]{:S(2)}) %collective-permute-start.11) | collective-permute-done | bytes 61472 | tf_op jit(solution)/shard_map/ppermute | solution.py:469
  34.5 1.6 %collective-permute-done.12.b_ref = bf16[240,128]{1,0:T(8,128)(2,1)S(1)} collective-permute-done((bf16[240,128]{1,0:T(8,128)(2,1)S(1)}, bf16[240,128]{1,0:T(8,128)(2,1)S(1)}, u32[]{:S(2)}, u32[]{:S(2)}) %collective-permute-start.12) | collective-permute-done | bytes 61472 | tf_op jit(solution)/shard_map/ppermute | solution.py:469
  36.1 0.0 collective-permute-done.13.c_ref
  36.1 2.8 %collective-permute-start.16 = (bf16[96,128]{1,0:T(8,128)(2,1)S(1)}, bf16[96,128]{1,0:T(8,128)(2,1)S(1)}, u32[]{:S(2)}, u32[]{:S(2)}) collective-permute-start(bf16[96,128]{1,0:T(8,128)(2,1)S(1)} %get-tuple-element.119.a_ref), channel_id=1, source_target_pairs={{0,6},{2,4},{4,2},{6,0},{8,14},{10,12},{12,10},{14,8},{16,22},{18,... | collective-permute-start | bytes 73736 | tf_op jit(solution)/shard_map/ppermute | solution.py:469
  38.8 0.4 collective-permute-start.15
  39.2 0.4 collective-permute-start.14
  39.6 0.0 collective-permute-start.17
  39.7 0.0 collective-permute-done.10.near_diag_ref
  39.7 0.5 %collective-permute-start.18 = (bf16[64,128]{1,0:T(8,128)(2,1)S(1)}, bf16[64,128]{1,0:T(8,128)(2,1)S(1)}, u32[]{:S(2)}, u32[]{:S(2)}) collective-permute-start(bf16[64,128]{1,0:T(8,128)(2,1)S(1)} %get-tuple-element.115.lower_ref), channel_id=1, source_target_pairs={{0,1},{1,0},{2,3},{3,2},{4,5},{5,4},{6,7},{7,6},{8,9},{9,8},{10,11... | collective-permute-start | bytes 49160 | tf_op jit(solution)/shard_map/ppermute | solution.py:469
  40.2 0.7 %unpack_quarters.1 = bf16[6,12,2,384]{3,2,1,0:T(2,128)(2,1)} custom-call(bf16[36,384]{1,0:T(8,128)(2,1)S(1)} %get-tuple-element.95.own_ref, bf16[72,384]{1,0:T(8,128)(2,1)S(1)} %collective-permute-done.4.near_ref, bf16[36,384]{1,0:T(8,128)(2,1)S(1)} %collective-permute-done.8.lat_ref, bf16[72,384]{1,0:T(8,128)(2,1)S(1)} %collective-permute-done.10.near_diag_ref), custom_call_target="tpu_custom_call" | custom-call | bytes 4194304 | tf_op jit(solution)/shard_map/unpack_quarters/pallas_call | solution.py:636
  40.8 0.2 collective-permute-done.18.other_lower_ref
  41.0 0.0 collective-permute-done.17.other_upper_ref
  41.0 0.6 %weights_out.1 = (bf16[24,1152]{1,0:T(8,128)(2,1)}, bf16[24,384]{1,0:T(8,128)(2,1)}) custom-call(bf16[80,128]{1,0:T(8,128)(2,1)S(1)} %get-tuple-element.114.upper_ref, bf16[64,128]{1,0:T(8,128)(2,1)S(1)} %get-tuple-element.115.lower_ref, bf16[80,128]{1,0:T(8,128)(2,1)S(1)} %collective-permute-done.17.other_upper_ref, ...), custom_call_target="tpu_custom_call" | custom-call | bytes 262144 | tf_op jit(solution)/shard_map/weights_out/pallas_call | solution.py:617
  41.6 0.0 collective-permute-done.16.d_ref
  41.7 1.0 %collective-permute-done.15.c_ref = bf16[96,128]{1,0:T(8,128)(2,1)S(1)} collective-permute-done((bf16[96,128]{1,0:T(8,128)(2,1)S(1)}, bf16[96,128]{1,0:T(8,128)(2,1)S(1)}, u32[]{:S(2)}, u32[]{:S(2)}) %collective-permute-start.15) | collective-permute-done | bytes 24608 | tf_op jit(solution)/shard_map/ppermute | solution.py:469
  42.7 0.4 collective-permute-done.14.b_ref
  43.0 0.8 %table_out.1 = (f32[12,1,3312]{2,1,0:T(1,128)}, f32[384]{0:T(512)}) custom-call(bf16[96,128]{1,0:T(8,128)(2,1)S(1)} %get-tuple-element.119.a_ref, bf16[96,128]{1,0:T(8,128)(2,1)S(1)} %collective-permute-done.14.b_ref, bf16[96,128]{1,0:T(8,128)(2,1)S(1)} %collective-permute-done.15.c_ref, bf16[96,128]{1,0:T(8,128)(2,1)S(1)} %collective-permute-done.16.d_ref), custom_call_target="tpu_custom_call" | custom-call | bytes 524288 | tf_op jit(solution)/shard_map/table_out/pallas_call | solution.py:625
  (1 shorter events, 0.0 us)
Async XLA Ops:
  1.8 10.5 %collective-permute-start = (bf16[80,384]{1,0:T(8,128)(2,1)S(1)}, bf16[80,384]{1,0:T(8,128)(2,1)S(1)}, u32[]{:S(2)}, u32[]{:S(2)}) collective-permute-start(bf16[80,384]{1,0:T(8,128)(2,1)S(1)} %get-tuple-element.68), channel_id=1, source_target_pairs={{0,2},{1,3},{2,4},{3,5},{4,6},{5,7},{6,8},{7,9},{8,10},{9,11},{10,... | collective-permute-start | bytes 184328 | tf_op jit(solution)/shard_map/ppermute | solution.py:465
  4.8 7.5 %collective-permute-start.1 = (bf16[72,384]{1,0:T(8,128)(2,1)S(1)}, bf16[72,384]{1,0:T(8,128)(2,1)S(1)}, u32[]{:S(2)}, u32[]{:S(2)}) collective-permute-start(bf16[72,384]{1,0:T(8,128)(2,1)S(1)} %get-tuple-element.69), channel_id=1, source_target_pairs={{0,3},{1,2},{2,5},{3,4},{4,7},{5,6},{6,9},{7,8},{8,11},{9,10},{10,... | collective-permute-start | bytes 165896 | tf_op jit(solution)/shard_map/ppermute | solution.py:465
  5.5 6.9 %collective-permute-start.2 = (bf16[72,384]{1,0:T(8,128)(2,1)S(1)}, bf16[72,384]{1,0:T(8,128)(2,1)S(1)}, u32[]{:S(2)}, u32[]{:S(2)}) collective-permute-start(bf16[72,384]{1,0:T(8,128)(2,1)S(1)} %get-tuple-element.70), channel_id=1, source_target_pairs={{0,1},{1,0},{2,3},{3,2},{4,5},{5,4},{6,7},{7,6},{8,9},{9,8},{10,11... | collective-permute-start | bytes 165896 | tf_op jit(solution)/shard_map/ppermute | solution.py:465
  15.4 2.1 %collective-permute-start.3 = (bf16[2304,128]{1,0:T(8,128)(2,1)S(1)}, bf16[2304,128]{1,0:T(8,128)(2,1)S(1)}, u32[]{:S(2)}, u32[]{:S(2)}) collective-permute-start(bf16[2304,128]{1,0:T(8,128)(2,1)S(1)} %get-tuple-element.77), channel_id=1, source_target_pairs={{0,1},{1,0},{2,3},{3,2},{4,5},{5,4},{6,7},{7,6},{8,9},{9,8},{10,11... | collective-permute-start | bytes 1769480 | tf_op jit(solution)/shard_map/ppermute | solution.py:469
  17.6 8.3 %collective-permute-start.5 = (bf16[656,128]{1,0:T(8,128)(2,1)S(1)}, bf16[656,128]{1,0:T(8,128)(2,1)S(1)}, u32[]{:S(2)}, u32[]{:S(2)}) collective-permute-start(bf16[656,128]{1,0:T(8,128)(2,1)S(1)} %get-tuple-element.97), channel_id=1, source_target_pairs={{0,6},{2,4},{4,2},{6,0},{8,14},{10,12},{12,10},{14,8},{16,22},{18,... | collective-permute-start | bytes 503816 | tf_op jit(solution)/shard_map/ppermute | solution.py:469
  17.7 10.2 %collective-permute-start.6 = (bf16[656,128]{1,0:T(8,128)(2,1)S(1)}, bf16[656,128]{1,0:T(8,128)(2,1)S(1)}, u32[]{:S(2)}, u32[]{:S(2)}) collective-permute-start(bf16[656,128]{1,0:T(8,128)(2,1)S(1)} %get-tuple-element.98), channel_id=1, source_target_pairs={{0,4},{2,6},{4,0},{6,2},{8,12},{10,14},{12,8},{14,10},{16,20},{18,... | collective-permute-start | bytes 503816 | tf_op jit(solution)/shard_map/ppermute | solution.py:469
  17.8 10.2 %collective-permute-start.7 = (bf16[656,128]{1,0:T(8,128)(2,1)S(1)}, bf16[656,128]{1,0:T(8,128)(2,1)S(1)}, u32[]{:S(2)}, u32[]{:S(2)}) collective-permute-start(bf16[656,128]{1,0:T(8,128)(2,1)S(1)} %get-tuple-element.99), channel_id=1, source_target_pairs={{0,2},{2,0},{4,6},{6,4},{8,10},{10,8},{12,14},{14,12},{16,18},{18,... | collective-permute-start | bytes 503816 | tf_op jit(solution)/shard_map/ppermute | solution.py:469
  22.2 10.3 %collective-permute-start.4 = (bf16[72,384]{1,0:T(8,128)(2,1)S(1)}, bf16[72,384]{1,0:T(8,128)(2,1)S(1)}, u32[]{:S(2)}, u32[]{:S(2)}) collective-permute-start(bf16[72,384]{1,0:T(8,128)(2,1)S(1)} %get-tuple-element.96), channel_id=1, source_target_pairs={{0,30},{1,31},{2,0},{3,1},{4,2},{5,3},{6,4},{7,5},{8,6},{9,7},{10,... | collective-permute-start | bytes 165896 | tf_op jit(solution)/shard_map/ppermute | solution.py:465
  23.6 1.2 %collective-permute-start.9 = (bf16[16,128]{1,0:T(8,128)(2,1)S(1)}, bf16[16,128]{1,0:T(8,128)(2,1)S(1)}, u32[]{:S(2)}, u32[]{:S(2)}) collective-permute-start(bf16[16,128]{1,0:T(8,128)(2,1)S(1)} %get-tuple-element.102.refs_0_), channel_id=1, source_target_pairs={{0,1},{1,0},{2,3},{3,2},{4,5},{5,4},{6,7},{7,6},{8,9},{9,8},{10,11... | collective-permute-start | bytes 12296 | tf_op jit(solution)/shard_map/ppermute | solution.py:469
  24.7 1.2 %collective-permute-start.8 = (bf16[36,384]{1,0:T(8,128)(2,1)S(1)}, bf16[36,384]{1,0:T(8,128)(2,1)S(1)}, u32[]{:S(2)}, u32[]{:S(2)}) collective-permute-start(bf16[36,384]{1,0:T(8,128)(2,1)S(1)} %get-tuple-element.101), channel_id=1, source_target_pairs={{0,1},{1,0},{2,3},{3,2},{4,5},{5,4},{6,7},{7,6},{8,9},{9,8},{10,11... | collective-permute-start | bytes 82952 | tf_op jit(solution)/shard_map/ppermute | solution.py:465
  28.0 6.4 %collective-permute-start.11 = (bf16[240,128]{1,0:T(8,128)(2,1)S(1)}, bf16[240,128]{1,0:T(8,128)(2,1)S(1)}, u32[]{:S(2)}, u32[]{:S(2)}) collective-permute-start(bf16[240,128]{1,0:T(8,128)(2,1)S(1)} %get-tuple-element.109), channel_id=1, source_target_pairs={{0,24},{2,26},{4,28},{6,30},{8,16},{10,18},{12,20},{14,22},{16,8},... | collective-permute-start | bytes 184328 | tf_op jit(solution)/shard_map/ppermute | solution.py:469
  30.5 5.6 %collective-permute-start.12 = (bf16[240,128]{1,0:T(8,128)(2,1)S(1)}, bf16[240,128]{1,0:T(8,128)(2,1)S(1)}, u32[]{:S(2)}, u32[]{:S(2)}) collective-permute-start(bf16[240,128]{1,0:T(8,128)(2,1)S(1)} %get-tuple-element.110), channel_id=1, source_target_pairs={{0,16},{2,18},{4,20},{6,22},{8,24},{10,26},{12,28},{14,30},{16,0},... | collective-permute-start | bytes 184328 | tf_op jit(solution)/shard_map/ppermute | solution.py:469
  30.5 5.6 %collective-permute-start.13 = (bf16[240,128]{1,0:T(8,128)(2,1)S(1)}, bf16[240,128]{1,0:T(8,128)(2,1)S(1)}, u32[]{:S(2)}, u32[]{:S(2)}) collective-permute-start(bf16[240,128]{1,0:T(8,128)(2,1)S(1)} %get-tuple-element.111), channel_id=1, source_target_pairs={{0,8},{2,10},{4,12},{6,14},{8,0},{10,2},{12,4},{14,6},{16,24},{18,... | collective-permute-start | bytes 184328 | tf_op jit(solution)/shard_map/ppermute | solution.py:469
  32.5 7.2 %collective-permute-start.10 = (bf16[72,384]{1,0:T(8,128)(2,1)S(1)}, bf16[72,384]{1,0:T(8,128)(2,1)S(1)}, u32[]{:S(2)}, u32[]{:S(2)}) collective-permute-start(bf16[72,384]{1,0:T(8,128)(2,1)S(1)} %collective-permute-done.4.near_ref), channel_id=1, source_target_pairs={{0,1},{1,0},{2,3},{3,2},{4,5},{5,4},{6,7},{7,6},{8,9},{9,8},{10,11... | collective-permute-start | bytes 165896 | tf_op jit(solution)/shard_map/ppermute | solution.py:465
  36.1 5.6 %collective-permute-start.16 = (bf16[96,128]{1,0:T(8,128)(2,1)S(1)}, bf16[96,128]{1,0:T(8,128)(2,1)S(1)}, u32[]{:S(2)}, u32[]{:S(2)}) collective-permute-start(bf16[96,128]{1,0:T(8,128)(2,1)S(1)} %get-tuple-element.119.a_ref), channel_id=1, source_target_pairs={{0,6},{2,4},{4,2},{6,0},{8,14},{10,12},{12,10},{14,8},{16,22},{18,... | collective-permute-start | bytes 73736 | tf_op jit(solution)/shard_map/ppermute | solution.py:469
  38.8 3.8 %collective-permute-start.15 = (bf16[96,128]{1,0:T(8,128)(2,1)S(1)}, bf16[96,128]{1,0:T(8,128)(2,1)S(1)}, u32[]{:S(2)}, u32[]{:S(2)}) collective-permute-start(bf16[96,128]{1,0:T(8,128)(2,1)S(1)} %get-tuple-element.119.a_ref), channel_id=1, source_target_pairs={{0,4},{2,6},{4,0},{6,2},{8,12},{10,14},{12,8},{14,10},{16,20},{18,... | collective-permute-start | bytes 73736 | tf_op jit(solution)/shard_map/ppermute | solution.py:469
  39.2 3.8 %collective-permute-start.14 = (bf16[96,128]{1,0:T(8,128)(2,1)S(1)}, bf16[96,128]{1,0:T(8,128)(2,1)S(1)}, u32[]{:S(2)}, u32[]{:S(2)}) collective-permute-start(bf16[96,128]{1,0:T(8,128)(2,1)S(1)} %get-tuple-element.119.a_ref), channel_id=1, source_target_pairs={{0,2},{2,0},{4,6},{6,4},{8,10},{10,8},{12,14},{14,12},{16,18},{18,... | collective-permute-start | bytes 73736 | tf_op jit(solution)/shard_map/ppermute | solution.py:469
  39.6 1.4 %collective-permute-start.17 = (bf16[80,128]{1,0:T(8,128)(2,1)S(1)}, bf16[80,128]{1,0:T(8,128)(2,1)S(1)}, u32[]{:S(2)}, u32[]{:S(2)}) collective-permute-start(bf16[80,128]{1,0:T(8,128)(2,1)S(1)} %get-tuple-element.114.upper_ref), channel_id=1, source_target_pairs={{0,1},{1,0},{2,3},{3,2},{4,5},{5,4},{6,7},{7,6},{8,9},{9,8},{10,11... | collective-permute-start | bytes 61448 | tf_op jit(solution)/shard_map/ppermute | solution.py:469
  39.7 1.3 %collective-permute-start.18 = (bf16[64,128]{1,0:T(8,128)(2,1)S(1)}, bf16[64,128]{1,0:T(8,128)(2,1)S(1)}, u32[]{:S(2)}, u32[]{:S(2)}) collective-permute-start(bf16[64,128]{1,0:T(8,128)(2,1)S(1)} %get-tuple-element.115.lower_ref), channel_id=1, source_target_pairs={{0,1},{1,0},{2,3},{3,2},{4,5},{5,4},{6,7},{7,6},{8,9},{9,8},{10,11... | collective-permute-start | bytes 49160 | tf_op jit(solution)/shard_map/ppermute | solution.py:469

commit v8 on v7

--- a/solution.py
+++ b/solution.py
@@ -284,10 +284,10 @@
     for turn in range(HEADS + 2):
         if turn < HEADS:
             raw[turn] = scores_of(turn)
+        if 1 <= turn <= HEADS:
+            soft[turn - 1] = softmax_of(turn - 1, *raw.pop(turn - 1))
         if turn >= 2:
             products_of(turn - 2, *soft.pop(turn - 2))
-        if 1 <= turn <= HEADS:
-            soft[turn - 1] = softmax_of(turn - 1, *raw.pop(turn - 1))
 
     odd = lax.rem(lax.axis_index("lat"), 2)
 

time: 44 us -> 44 us (level)
  no operation moved by 1% of the time
where the time goes in v8:
time: 44 us; the launch traced here: 43.8 us
  starting transfers between devices  18.3 us (42%)
  waiting for transfers between devices  13.1 us (30%)
  Pallas kernels  11.7 us (27%)
  between operations  0.72 us (2%)
    ppermute x13, starting transfers between devices, swap(): lax.ppermute(value, axis, [(source, source ^ mask) for source in range(co...  12.1 us
    ppermute x13, waiting for transfers between devices, swap(): lax.ppermute(value, axis, [(source, source ^ mask) for source in range(co...  8.42 us
    ppermute x6, starting transfers between devices, move(): return lax.ppermute(value, ('lon', 'lat'), pairs)  6.15 us
    ppermute x6, waiting for transfers between devices, move(): return lax.ppermute(value, ('lon', 'lat'), pairs)  4.73 us
    pallas_call x1, Pallas kernels, on_device(): call(functools.partial(window_kernel, packet), 'window', whole(10), [half...  3.09 us
    pallas_call x1, Pallas kernels, on_device(): call(bias_kernel, 'expand_bias', whole(1) + [hbm] * 2, [struct((HEADS, CE...  2.21 us
    pallas_call x1, Pallas kernels, on_device(): call(functools.partial(fold_kernel, packet), 'fold_table', whole(3), stru...  1.83 us
    pallas_call x1, Pallas kernels, on_device(): call(load_kernel, 'load', [hbm] * 5, [others, same, others, others] + [st...  1.18 us
  transfers between devices with their start and end apart: 19, of which 10 were waited for; matrix products, arithmetic and copies ran while one was open for 0% of the time, Pallas kernels for 15%

profile of v8, /device:TPU:0, one launch (start us, length us, event | category | flops | bytes accessed | tf_op | source)
XLA Modules:
  0.0 43.8 jit_solution(4709674604944039548)
XLA Ops:
  0.6 1.2 %load.1 = (bf16[72,384]{1,0:T(8,128)(2,1)S(1)}, bf16[80,384]{1,0:T(8,128)(2,1)S(1)}, bf16[72,384]{1,0:T(8,128)(2,1)S(1)}, bf16[72,384]{1,0:T(8,128)(2,1)S(1)}, b...) custom-call(bf16[6,12,2,384]{3,2,1,0:T(2,128)(2,1)} %bitcast.7, bf16[6,12,2,384]{3,2,1,0:T(2,128)(2,1)} %bitcast.8, ...), custom_call_target="tpu_custom_call" | custom-call | bytes 1048576 | tf_op jit(solution)/shard_map/load/pallas_call | solution.py:482
  1.8 3.0 %collective-permute-start = (bf16[80,384]{1,0:T(8,128)(2,1)S(1)}, bf16[80,384]{1,0:T(8,128)(2,1)S(1)}, u32[]{:S(2)}, u32[]{:S(2)}) collective-permute-start(bf16[80,384]{1,0:T(8,128)(2,1)S(1)} %get-tuple-element.68), channel_id=1, source_target_pairs={{0,2},{1,3},{2,4},{3,5},{4,6},{5,7},{6,8},{7,9},{8,10},{9,11},{10,... | collective-permute-start | bytes 184328 | tf_op jit(solution)/shard_map/ppermute | solution.py:465
  4.8 0.7 %collective-permute-start.1 = (bf16[72,384]{1,0:T(8,128)(2,1)S(1)}, bf16[72,384]{1,0:T(8,128)(2,1)S(1)}, u32[]{:S(2)}, u32[]{:S(2)}) collective-permute-start(bf16[72,384]{1,0:T(8,128)(2,1)S(1)} %get-tuple-element.69), channel_id=1, source_target_pairs={{0,3},{1,2},{2,5},{3,4},{4,7},{5,6},{6,9},{7,8},{8,11},{9,10},{10,... | collective-permute-start | bytes 165896 | tf_op jit(solution)/shard_map/ppermute | solution.py:465
  5.5 1.0 %collective-permute-start.2 = (bf16[72,384]{1,0:T(8,128)(2,1)S(1)}, bf16[72,384]{1,0:T(8,128)(2,1)S(1)}, u32[]{:S(2)}, u32[]{:S(2)}) collective-permute-start(bf16[72,384]{1,0:T(8,128)(2,1)S(1)} %get-tuple-element.70), channel_id=1, source_target_pairs={{0,1},{1,0},{2,3},{3,2},{4,5},{5,4},{6,7},{7,6},{8,9},{9,8},{10,11... | collective-permute-start | bytes 165896 | tf_op jit(solution)/shard_map/ppermute | solution.py:465
  6.4 2.2 %expand_bias.1 = (bf16[12,144,144]{2,1,0:T(8,128)(2,1)S(1)}, bf16[384,384]{1,0:T(8,128)(2,1)S(1)}, bf16[384,384]{1,0:T(8,128)(2,1)S(1)}, bf16[192,192]{1,0:T(8,1...) custom-call(bf16[12,3312]{1,0:T(8,128)(2,1)S(1)} %get-tuple-element., ...), custom_call_target="tpu_custom_call" | custom-call | bytes 2097152 | tf_op jit(solution)/shard_map/expand_bias/pallas_call | solution.py:494
  8.6 3.7 %collective-permute-done.1.near_diag_ref = bf16[72,384]{1,0:T(8,128)(2,1)S(1)} collective-permute-done((bf16[72,384]{1,0:T(8,128)(2,1)S(1)}, bf16[72,384]{1,0:T(8,128)(2,1)S(1)}, u32[]{:S(2)}, u32[]{:S(2)}) %collective-permute-start.1) | collective-permute-done | bytes 55328 | tf_op jit(solution)/shard_map/ppermute | solution.py:465
  12.3 0.0 collective-permute-done.2.lat_ref
  12.3 0.0 collective-permute-done.near_ref
  12.3 3.1 %window.1 = (bf16[2304,128]{1,0:T(8,128)(2,1)S(1)}, bf16[2304,128]{1,0:T(8,128)(2,1)S(1)}, bf16[12,144,144]{2,1,0:T(8,128)(2,1)S(1)}, bf16[4,384,144]{2,1,0:T(8,...) custom-call(bf16[72,384]{1,0:T(8,128)(2,1)S(1)} %get-tuple-element.67.own_ref, ...), custom_call_target="tpu_custom_call" | custom-call | flops 1000000000 | bytes 5242880 | tf_op jit(solution)/shard_map/window/pallas_call | solution.py:518
  15.4 0.1 collective-permute-start.3
  15.5 1.8 %fold_table.1.table_ref = bf16[320,128]{1,0:T(8,128)(2,1)S(1)} custom-call(bf16[12,144,144]{2,1,0:T(8,128)(2,1)S(1)} %get-tuple-element.78.scores_ref, bf16[384,384]{1,0:T(8,128)(2,1)S(1)} %get-tuple-element.79.lanes_ref, bf16[192,192]{1,0:T(8,128)(2,1)S(1)} %get-tuple-element.80.rows_ref), custom_call_target="tpu_custom_call" | custom-call | bytes 2097152 | tf_op jit(solution)/shard_map/fold_table/pallas_call | solution.py:549
  17.3 0.2 collective-permute-done.3.recv_ref
  17.5 0.1 add_lat.1
  17.6 0.1 collective-permute-start.5
  17.7 0.1 collective-permute-start.6
  17.8 3.4 %collective-permute-start.7 = (bf16[656,128]{1,0:T(8,128)(2,1)S(1)}, bf16[656,128]{1,0:T(8,128)(2,1)S(1)}, u32[]{:S(2)}, u32[]{:S(2)}) collective-permute-start(bf16[656,128]{1,0:T(8,128)(2,1)S(1)} %get-tuple-element.99), channel_id=1, source_target_pairs={{0,2},{2,0},{4,6},{6,4},{8,10},{10,8},{12,14},{14,12},{16,18},{18,... | collective-permute-start | bytes 503816 | tf_op jit(solution)/shard_map/ppermute | solution.py:469
  21.2 1.0 %grad_field.1 = (bf16[36,384]{1,0:T(8,128)(2,1)S(1)}, bf16[72,384]{1,0:T(8,128)(2,1)S(1)}, bf16[36,384]{1,0:T(8,128)(2,1)S(1)}, bf16[16,128]{1,0:T(8,128)(2,1)S(1)}) custom-call(bf16[384,1152]{1,0:T(8,128)(2,1)S(1)} %get-tuple-element.66.win_ref, bf16[4,384,144]{2,1,0:T(8,128)(2,1)S(1)} %get-tuple-element.89.grad_projected_ref, ...), custom_call_target="tpu_custom_call" | custom-call | flops 100000000 | bytes 5242880 | tf_op jit(solution)/shard_map/grad_field/pallas_call | solution.py:577
  22.2 1.4 %collective-permute-start.4 = (bf16[72,384]{1,0:T(8,128)(2,1)S(1)}, bf16[72,384]{1,0:T(8,128)(2,1)S(1)}, u32[]{:S(2)}, u32[]{:S(2)}) collective-permute-start(bf16[72,384]{1,0:T(8,128)(2,1)S(1)} %get-tuple-element.96), channel_id=1, source_target_pairs={{0,30},{1,31},{2,0},{3,1},{4,2},{5,3},{6,4},{7,5},{8,6},{9,7},{10,... | collective-permute-start | bytes 165896 | tf_op jit(solution)/shard_map/ppermute | solution.py:465
  23.6 0.0 collective-permute-start.9
  23.6 1.2 %collective-permute-done.9.refs_1_ = bf16[16,128]{1,0:T(8,128)(2,1)S(1)} collective-permute-done((bf16[16,128]{1,0:T(8,128)(2,1)S(1)}, bf16[16,128]{1,0:T(8,128)(2,1)S(1)}, u32[]{:S(2)}, u32[]{:S(2)}) %collective-permute-start.9) | collective-permute-done | bytes 4128 | tf_op jit(solution)/shard_map/ppermute | solution.py:469
  24.7 0.2 collective-permute-start.8
  24.9 1.0 %collective-permute-done.8.lat_ref = bf16[36,384]{1,0:T(8,128)(2,1)S(1)} collective-permute-done((bf16[36,384]{1,0:T(8,128)(2,1)S(1)}, bf16[36,384]{1,0:T(8,128)(2,1)S(1)}, u32[]{:S(2)}, u32[]{:S(2)}) %collective-permute-start.8) | collective-permute-done | bytes 27680 | tf_op jit(solution)/shard_map/ppermute | solution.py:465
  26.0 0.0 collective-permute-done.5.refs_2_
  26.0 2.0 %collective-permute-done.6.refs_3_ = bf16[656,128]{1,0:T(8,128)(2,1)S(1)} collective-permute-done((bf16[656,128]{1,0:T(8,128)(2,1)S(1)}, bf16[656,128]{1,0:T(8,128)(2,1)S(1)}, u32[]{:S(2)}, u32[]{:S(2)}) %collective-permute-start.6) | collective-permute-done | bytes 167968 | tf_op jit(solution)/shard_map/ppermute | solution.py:469
  27.9 0.0 collective-permute-done.7.refs_4_
  27.9 0.1 add_lon.1
  28.0 2.5 %collective-permute-start.11 = (bf16[240,128]{1,0:T(8,128)(2,1)S(1)}, bf16[240,128]{1,0:T(8,128)(2,1)S(1)}, u32[]{:S(2)}, u32[]{:S(2)}) collective-permute-start(bf16[240,128]{1,0:T(8,128)(2,1)S(1)} %get-tuple-element.109), channel_id=1, source_target_pairs={{0,24},{2,26},{4,28},{6,30},{8,16},{10,18},{12,20},{14,22},{16,8},... | collective-permute-start | bytes 184328 | tf_op jit(solution)/shard_map/ppermute | solution.py:469
  30.5 0.0 collective-permute-start.12
  30.5 2.0 %collective-permute-start.13 = (bf16[240,128]{1,0:T(8,128)(2,1)S(1)}, bf16[240,128]{1,0:T(8,128)(2,1)S(1)}, u32[]{:S(2)}, u32[]{:S(2)}) collective-permute-start(bf16[240,128]{1,0:T(8,128)(2,1)S(1)} %get-tuple-element.111), channel_id=1, source_target_pairs={{0,8},{2,10},{4,12},{6,14},{8,0},{10,2},{12,4},{14,6},{16,24},{18,... | collective-permute-start | bytes 184328 | tf_op jit(solution)/shard_map/ppermute | solution.py:469
  32.5 0.0 collective-permute-done.4.near_ref
  32.5 0.0 collective-permute-start.10
  32.5 2.0 %collective-permute-done.11.a_ref = bf16[240,128]{1,0:T(8,128)(2,1)S(1)} collective-permute-done((bf16[240,128]{1,0:T(8,128)(2,1)S(1)}, bf16[240,128]{1,0:T(8,128)(2,1)S(1)}, u32[]{:S(2)}, u32[]{:S(2)}) %collective-permute-start.11) | collective-permute-done | bytes 61472 | tf_op jit(solution)/shard_map/ppermute | solution.py:469
  34.5 1.6 %collective-permute-done.12.b_ref = bf16[240,128]{1,0:T(8,128)(2,1)S(1)} collective-permute-done((bf16[240,128]{1,0:T(8,128)(2,1)S(1)}, bf16[240,128]{1,0:T(8,128)(2,1)S(1)}, u32[]{:S(2)}, u32[]{:S(2)}) %collective-permute-start.12) | collective-permute-done | bytes 61472 | tf_op jit(solution)/shard_map/ppermute | solution.py:469
  36.1 0.0 collective-permute-done.13.c_ref
  36.1 2.8 %collective-permute-start.16 = (bf16[96,128]{1,0:T(8,128)(2,1)S(1)}, bf16[96,128]{1,0:T(8,128)(2,1)S(1)}, u32[]{:S(2)}, u32[]{:S(2)}) collective-permute-start(bf16[96,128]{1,0:T(8,128)(2,1)S(1)} %get-tuple-element.119.a_ref), channel_id=1, source_target_pairs={{0,6},{2,4},{4,2},{6,0},{8,14},{10,12},{12,10},{14,8},{16,22},{18,... | collective-permute-start | bytes 73736 | tf_op jit(solution)/shard_map/ppermute | solution.py:469
  38.8 0.4 collective-permute-start.15
  39.2 0.4 collective-permute-start.14
  39.6 0.0 collective-permute-start.17
  39.7 0.0 collective-permute-done.10.near_diag_ref
  39.7 0.5 %collective-permute-start.18 = (bf16[64,128]{1,0:T(8,128)(2,1)S(1)}, bf16[64,128]{1,0:T(8,128)(2,1)S(1)}, u32[]{:S(2)}, u32[]{:S(2)}) collective-permute-start(bf16[64,128]{1,0:T(8,128)(2,1)S(1)} %get-tuple-element.115.lower_ref), channel_id=1, source_target_pairs={{0,1},{1,0},{2,3},{3,2},{4,5},{5,4},{6,7},{7,6},{8,9},{9,8},{10,11... | collective-permute-start | bytes 49160 | tf_op jit(solution)/shard_map/ppermute | solution.py:469
  40.2 0.7 %unpack_quarters.1 = bf16[6,12,2,384]{3,2,1,0:T(2,128)(2,1)} custom-call(bf16[36,384]{1,0:T(8,128)(2,1)S(1)} %get-tuple-element.95.own_ref, bf16[72,384]{1,0:T(8,128)(2,1)S(1)} %collective-permute-done.4.near_ref, bf16[36,384]{1,0:T(8,128)(2,1)S(1)} %collective-permute-done.8.lat_ref, bf16[72,384]{1,0:T(8,128)(2,1)S(1)} %collective-permute-done.10.near_diag_ref), custom_call_target="tpu_custom_call" | custom-call | bytes 4194304 | tf_op jit(solution)/shard_map/unpack_quarters/pallas_call | solution.py:636
  40.8 0.2 collective-permute-done.18.other_lower_ref
  41.0 0.0 collective-permute-done.17.other_upper_ref
  41.0 0.6 %weights_out.1 = (bf16[24,1152]{1,0:T(8,128)(2,1)}, bf16[24,384]{1,0:T(8,128)(2,1)}) custom-call(bf16[80,128]{1,0:T(8,128)(2,1)S(1)} %get-tuple-element.114.upper_ref, bf16[64,128]{1,0:T(8,128)(2,1)S(1)} %get-tuple-element.115.lower_ref, bf16[80,128]{1,0:T(8,128)(2,1)S(1)} %collective-permute-done.17.other_upper_ref, ...), custom_call_target="tpu_custom_call" | custom-call | bytes 262144 | tf_op jit(solution)/shard_map/weights_out/pallas_call | solution.py:617
  41.6 0.0 collective-permute-done.16.d_ref
  41.7 1.0 %collective-permute-done.15.c_ref = bf16[96,128]{1,0:T(8,128)(2,1)S(1)} collective-permute-done((bf16[96,128]{1,0:T(8,128)(2,1)S(1)}, bf16[96,128]{1,0:T(8,128)(2,1)S(1)}, u32[]{:S(2)}, u32[]{:S(2)}) %collective-permute-start.15) | collective-permute-done | bytes 24608 | tf_op jit(solution)/shard_map/ppermute | solution.py:469
  42.7 0.4 collective-permute-done.14.b_ref
  43.0 0.8 %table_out.1 = (f32[12,1,3312]{2,1,0:T(1,128)}, f32[384]{0:T(512)}) custom-call(bf16[96,128]{1,0:T(8,128)(2,1)S(1)} %get-tuple-element.119.a_ref, bf16[96,128]{1,0:T(8,128)(2,1)S(1)} %collective-permute-done.14.b_ref, bf16[96,128]{1,0:T(8,128)(2,1)S(1)} %collective-permute-done.15.c_ref, bf16[96,128]{1,0:T(8,128)(2,1)S(1)} %collective-permute-done.16.d_ref), custom_call_target="tpu_custom_call" | custom-call | bytes 524288 | tf_op jit(solution)/shard_map/table_out/pallas_call | solution.py:625
  (1 shorter events, 0.0 us)
Async XLA Ops:
  1.8 10.5 %collective-permute-start = (bf16[80,384]{1,0:T(8,128)(2,1)S(1)}, bf16[80,384]{1,0:T(8,128)(2,1)S(1)}, u32[]{:S(2)}, u32[]{:S(2)}) collective-permute-start(bf16[80,384]{1,0:T(8,128)(2,1)S(1)} %get-tuple-element.68), channel_id=1, source_target_pairs={{0,2},{1,3},{2,4},{3,5},{4,6},{5,7},{6,8},{7,9},{8,10},{9,11},{10,... | collective-permute-start | bytes 184328 | tf_op jit(solution)/shard_map/ppermute | solution.py:465
  4.8 7.5 %collective-permute-start.1 = (bf16[72,384]{1,0:T(8,128)(2,1)S(1)}, bf16[72,384]{1,0:T(8,128)(2,1)S(1)}, u32[]{:S(2)}, u32[]{:S(2)}) collective-permute-start(bf16[72,384]{1,0:T(8,128)(2,1)S(1)} %get-tuple-element.69), channel_id=1, source_target_pairs={{0,3},{1,2},{2,5},{3,4},{4,7},{5,6},{6,9},{7,8},{8,11},{9,10},{10,... | collective-permute-start | bytes 165896 | tf_op jit(solution)/shard_map/ppermute | solution.py:465
  5.5 6.9 %collective-permute-start.2 = (bf16[72,384]{1,0:T(8,128)(2,1)S(1)}, bf16[72,384]{1,0:T(8,128)(2,1)S(1)}, u32[]{:S(2)}, u32[]{:S(2)}) collective-permute-start(bf16[72,384]{1,0:T(8,128)(2,1)S(1)} %get-tuple-element.70), channel_id=1, source_target_pairs={{0,1},{1,0},{2,3},{3,2},{4,5},{5,4},{6,7},{7,6},{8,9},{9,8},{10,11... | collective-permute-start | bytes 165896 | tf_op jit(solution)/shard_map/ppermute | solution.py:465
  15.4 2.1 %collective-permute-start.3 = (bf16[2304,128]{1,0:T(8,128)(2,1)S(1)}, bf16[2304,128]{1,0:T(8,128)(2,1)S(1)}, u32[]{:S(2)}, u32[]{:S(2)}) collective-permute-start(bf16[2304,128]{1,0:T(8,128)(2,1)S(1)} %get-tuple-element.77), channel_id=1, source_target_pairs={{0,1},{1,0},{2,3},{3,2},{4,5},{5,4},{6,7},{7,6},{8,9},{9,8},{10,11... | collective-permute-start | bytes 1769480 | tf_op jit(solution)/shard_map/ppermute | solution.py:469
  17.6 8.3 %collective-permute-start.5 = (bf16[656,128]{1,0:T(8,128)(2,1)S(1)}, bf16[656,128]{1,0:T(8,128)(2,1)S(1)}, u32[]{:S(2)}, u32[]{:S(2)}) collective-permute-start(bf16[656,128]{1,0:T(8,128)(2,1)S(1)} %get-tuple-element.97), channel_id=1, source_target_pairs={{0,6},{2,4},{4,2},{6,0},{8,14},{10,12},{12,10},{14,8},{16,22},{18,... | collective-permute-start | bytes 503816 | tf_op jit(solution)/shard_map/ppermute | solution.py:469
  17.7 10.2 %collective-permute-start.6 = (bf16[656,128]{1,0:T(8,128)(2,1)S(1)}, bf16[656,128]{1,0:T(8,128)(2,1)S(1)}, u32[]{:S(2)}, u32[]{:S(2)}) collective-permute-start(bf16[656,128]{1,0:T(8,128)(2,1)S(1)} %get-tuple-element.98), channel_id=1, source_target_pairs={{0,4},{2,6},{4,0},{6,2},{8,12},{10,14},{12,8},{14,10},{16,20},{18,... | collective-permute-start | bytes 503816 | tf_op jit(solution)/shard_map/ppermute | solution.py:469
  17.8 10.2 %collective-permute-start.7 = (bf16[656,128]{1,0:T(8,128)(2,1)S(1)}, bf16[656,128]{1,0:T(8,128)(2,1)S(1)}, u32[]{:S(2)}, u32[]{:S(2)}) collective-permute-start(bf16[656,128]{1,0:T(8,128)(2,1)S(1)} %get-tuple-element.99), channel_id=1, source_target_pairs={{0,2},{2,0},{4,6},{6,4},{8,10},{10,8},{12,14},{14,12},{16,18},{18,... | collective-permute-start | bytes 503816 | tf_op jit(solution)/shard_map/ppermute | solution.py:469
  22.2 10.3 %collective-permute-start.4 = (bf16[72,384]{1,0:T(8,128)(2,1)S(1)}, bf16[72,384]{1,0:T(8,128)(2,1)S(1)}, u32[]{:S(2)}, u32[]{:S(2)}) collective-permute-start(bf16[72,384]{1,0:T(8,128)(2,1)S(1)} %get-tuple-element.96), channel_id=1, source_target_pairs={{0,30},{1,31},{2,0},{3,1},{4,2},{5,3},{6,4},{7,5},{8,6},{9,7},{10,... | collective-permute-start | bytes 165896 | tf_op jit(solution)/shard_map/ppermute | solution.py:465
  23.6 1.2 %collective-permute-start.9 = (bf16[16,128]{1,0:T(8,128)(2,1)S(1)}, bf16[16,128]{1,0:T(8,128)(2,1)S(1)}, u32[]{:S(2)}, u32[]{:S(2)}) collective-permute-start(bf16[16,128]{1,0:T(8,128)(2,1)S(1)} %get-tuple-element.102.refs_0_), channel_id=1, source_target_pairs={{0,1},{1,0},{2,3},{3,2},{4,5},{5,4},{6,7},{7,6},{8,9},{9,8},{10,11... | collective-permute-start | bytes 12296 | tf_op jit(solution)/shard_map/ppermute | solution.py:469
  24.7 1.2 %collective-permute-start.8 = (bf16[36,384]{1,0:T(8,128)(2,1)S(1)}, bf16[36,384]{1,0:T(8,128)(2,1)S(1)}, u32[]{:S(2)}, u32[]{:S(2)}) collective-permute-start(bf16[36,384]{1,0:T(8,128)(2,1)S(1)} %get-tuple-element.101), channel_id=1, source_target_pairs={{0,1},{1,0},{2,3},{3,2},{4,5},{5,4},{6,7},{7,6},{8,9},{9,8},{10,11... | collective-permute-start | bytes 82952 | tf_op jit(solution)/shard_map/ppermute | solution.py:465
  28.0 6.4 %collective-permute-start.11 = (bf16[240,128]{1,0:T(8,128)(2,1)S(1)}, bf16[240,128]{1,0:T(8,128)(2,1)S(1)}, u32[]{:S(2)}, u32[]{:S(2)}) collective-permute-start(bf16[240,128]{1,0:T(8,128)(2,1)S(1)} %get-tuple-element.109), channel_id=1, source_target_pairs={{0,24},{2,26},{4,28},{6,30},{8,16},{10,18},{12,20},{14,22},{16,8},... | collective-permute-start | bytes 184328 | tf_op jit(solution)/shard_map/ppermute | solution.py:469
  30.5 5.6 %collective-permute-start.12 = (bf16[240,128]{1,0:T(8,128)(2,1)S(1)}, bf16[240,128]{1,0:T(8,128)(2,1)S(1)}, u32[]{:S(2)}, u32[]{:S(2)}) collective-permute-start(bf16[240,128]{1,0:T(8,128)(2,1)S(1)} %get-tuple-element.110), channel_id=1, source_target_pairs={{0,16},{2,18},{4,20},{6,22},{8,24},{10,26},{12,28},{14,30},{16,0},... | collective-permute-start | bytes 184328 | tf_op jit(solution)/shard_map/ppermute | solution.py:469
  30.5 5.6 %collective-permute-start.13 = (bf16[240,128]{1,0:T(8,128)(2,1)S(1)}, bf16[240,128]{1,0:T(8,128)(2,1)S(1)}, u32[]{:S(2)}, u32[]{:S(2)}) collective-permute-start(bf16[240,128]{1,0:T(8,128)(2,1)S(1)} %get-tuple-element.111), channel_id=1, source_target_pairs={{0,8},{2,10},{4,12},{6,14},{8,0},{10,2},{12,4},{14,6},{16,24},{18,... | collective-permute-start | bytes 184328 | tf_op jit(solution)/shard_map/ppermute | solution.py:469
  32.5 7.2 %collective-permute-start.10 = (bf16[72,384]{1,0:T(8,128)(2,1)S(1)}, bf16[72,384]{1,0:T(8,128)(2,1)S(1)}, u32[]{:S(2)}, u32[]{:S(2)}) collective-permute-start(bf16[72,384]{1,0:T(8,128)(2,1)S(1)} %collective-permute-done.4.near_ref), channel_id=1, source_target_pairs={{0,1},{1,0},{2,3},{3,2},{4,5},{5,4},{6,7},{7,6},{8,9},{9,8},{10,11... | collective-permute-start | bytes 165896 | tf_op jit(solution)/shard_map/ppermute | solution.py:465
  36.1 5.6 %collective-permute-start.16 = (bf16[96,128]{1,0:T(8,128)(2,1)S(1)}, bf16[96,128]{1,0:T(8,128)(2,1)S(1)}, u32[]{:S(2)}, u32[]{:S(2)}) collective-permute-start(bf16[96,128]{1,0:T(8,128)(2,1)S(1)} %get-tuple-element.119.a_ref), channel_id=1, source_target_pairs={{0,6},{2,4},{4,2},{6,0},{8,14},{10,12},{12,10},{14,8},{16,22},{18,... | collective-permute-start | bytes 73736 | tf_op jit(solution)/shard_map/ppermute | solution.py:469
  38.8 3.8 %collective-permute-start.15 = (bf16[96,128]{1,0:T(8,128)(2,1)S(1)}, bf16[96,128]{1,0:T(8,128)(2,1)S(1)}, u32[]{:S(2)}, u32[]{:S(2)}) collective-permute-start(bf16[96,128]{1,0:T(8,128)(2,1)S(1)} %get-tuple-element.119.a_ref), channel_id=1, source_target_pairs={{0,4},{2,6},{4,0},{6,2},{8,12},{10,14},{12,8},{14,10},{16,20},{18,... | collective-permute-start | bytes 73736 | tf_op jit(solution)/shard_map/ppermute | solution.py:469
  39.2 3.8 %collective-permute-start.14 = (bf16[96,128]{1,0:T(8,128)(2,1)S(1)}, bf16[96,128]{1,0:T(8,128)(2,1)S(1)}, u32[]{:S(2)}, u32[]{:S(2)}) collective-permute-start(bf16[96,128]{1,0:T(8,128)(2,1)S(1)} %get-tuple-element.119.a_ref), channel_id=1, source_target_pairs={{0,2},{2,0},{4,6},{6,4},{8,10},{10,8},{12,14},{14,12},{16,18},{18,... | collective-permute-start | bytes 73736 | tf_op jit(solution)/shard_map/ppermute | solution.py:469
  39.6 1.4 %collective-permute-start.17 = (bf16[80,128]{1,0:T(8,128)(2,1)S(1)}, bf16[80,128]{1,0:T(8,128)(2,1)S(1)}, u32[]{:S(2)}, u32[]{:S(2)}) collective-permute-start(bf16[80,128]{1,0:T(8,128)(2,1)S(1)} %get-tuple-element.114.upper_ref), channel_id=1, source_target_pairs={{0,1},{1,0},{2,3},{3,2},{4,5},{5,4},{6,7},{7,6},{8,9},{9,8},{10,11... | collective-permute-start | bytes 61448 | tf_op jit(solution)/shard_map/ppermute | solution.py:469
  39.7 1.3 %collective-permute-start.18 = (bf16[64,128]{1,0:T(8,128)(2,1)S(1)}, bf16[64,128]{1,0:T(8,128)(2,1)S(1)}, u32[]{:S(2)}, u32[]{:S(2)}) collective-permute-start(bf16[64,128]{1,0:T(8,128)(2,1)S(1)} %get-tuple-element.115.lower_ref), channel_id=1, source_target_pairs={{0,1},{1,0},{2,3},{3,2},{4,5},{5,4},{6,7},{7,6},{8,9},{9,8},{10,11... | collective-permute-start | bytes 49160 | tf_op jit(solution)/shard_map/ppermute | solution.py:469
